TPU v7x, 32 devices: a whole 2x2x4 slice. The times are simulated.
32 devices in a mesh: batch: 4 (over x, core), seq: 8 (over z, y).
Axes of the slice: x: 2, y: 2, z: 4, core: 2. Of those that a mesh axis runs over, the one named last changes fastest.
Arguments:
- tokens: bfloat16 [8, 1, 1152, 512], P('batch', None, 'seq'), may hold values from -5 to 5
- cotangent: bfloat16 [8, 1, 1152, 512], P('batch', None, 'seq'), may hold values from -5 to 5
- doc_lengths: int32 [8, 1, 4], P('batch'), may hold values from 1 to 336, 384 in all within a row
- owners: int32 [6], replicated, may hold values from 0 to 3, as said below
- master: float32 [4, 8, 512, 512], P('batch', None, 'seq'), as said below
- first_moment: float32 [4, 8, 512, 512], P('batch', None, 'seq'), may hold values from -32 to 32
- second_moment: float32 [4, 8, 512, 512], P('batch', None, 'seq'), may hold values from 92.16 to 1228.8
- ln_gain: float32 [2, 512], replicated, may hold values from 0.5 to 1.5
- ln_bias: float32 [2, 512], replicated, may hold values from -1.2 to 1.2
- norm_m: float32 [4, 512], replicated, may hold values from -32 to 32
- norm_v: float32 [4, 512], replicated, may hold values from 92.16 to 1228.8
- slopes: float32 [8], replicated, may hold values from 0.0013020834 to 0.1
- slope_m: float32 [8], replicated, may hold values from -32768 to 32768
- slope_v: float32 [8], replicated, may hold values from 3072000 to 307200000
Outputs:
- mixed: float32 [8, 1, 1152, 512], P('batch', None, 'seq')
- input_grad: float32 [8, 1, 1152, 512], P('batch', None, 'seq')
- new_master: float32 [4, 8, 512, 512], P('batch', None, 'seq')
- new_first: float32 [4, 8, 512, 512], P('batch', None, 'seq')
- new_second: float32 [4, 8, 512, 512], P('batch', None, 'seq')
- new_low: bfloat16 [4, 8, 512, 512], P('batch', None, 'seq')
- new_norm: float32 [4, 512], replicated
- new_norm_m: float32 [4, 512], replicated
- new_norm_v: float32 [4, 512], replicated
- new_slopes: float32 [8], replicated
- new_slope_m: float32 [8], replicated
- new_slope_v: float32 [8], replicated
Inputs may be any that keep to these rules, and one draw needn't show every extreme that they name: The owner of the two feed-forward matrices owns no other matrix and holds exactly 8 blocks; the pooling and query-key-value matrices have different owners; no owner holds more than 8 blocks. `master`: slots beyond an owner's blocks hold values that are only copied.
All inputs are finite; a program needn't handle non-finite values.
Results may differ from a plain program's by a relative error of at most 0.014.
Values may be sent and summed in bfloat16 or wider, within the bound.
A program may use at most 192 MiB of HBM per device.

v0:
```python
import jax
import jax.numpy as jnp
from jax import lax
from jax.sharding import PartitionSpec as P

FF = 2048
STEP = 10


beta_one = 0.9
beta_two = 0.95
adam_eps = 1e-08
decay_rate = 0.1
rate_matrix = 0.02
rate_norm = 0.2
rate_slope = 0.01
ln_eps = 1e-05
masked_score = -1000000000.0
row_kinds = (True, False, True, False, True, False)


def broadcast(value, axis, source):
    kept = jnp.where(lax.axis_index(axis) == source, value, 0).astype(value.dtype)
    return lax.psum(kept, axis)


def for_sending(value):

    def short(part):
        return part.astype(jnp.bfloat16) if part.dtype == jnp.float32 else part

    return jax.tree.map(short, value)


def passed_along(value, axis, by):
    peers = lax.axis_size(axis)
    pairs = [(i, i + by) for i in range(peers) if 0 <= i + by < peers]
    return lax.ppermute(value, axis, pairs)


def layer_norm(values, gain, shift):
    center = jnp.mean(values, -1, keepdims=True)
    centred = values - center
    spread = jnp.mean(centred * centred, -1, keepdims=True)
    return centred * lax.rsqrt(spread + ln_eps) * gain + shift


def gelu_tanh(values):
    return jax.nn.gelu(values, approximate=True)


def block_counts(features, hidden):
    return [3, 3, 1, hidden // features, hidden // features, 3]


def block_starts(owners, sizes):
    starts_list = []
    for matrix_id in range(len(sizes)):
        shared = jnp.zeros((), jnp.int32)
        for earlier_id in range(matrix_id):
            shared = shared + jnp.where(
                owners[earlier_id] == owners[matrix_id], sizes[earlier_id], 0
            ).astype(jnp.int32)
        starts_list.append(shared)
    return starts_list


def slot_table(owners, device, sizes, slot_count):
    starts_list = block_starts(owners, sizes)
    slot_ids = jnp.arange(slot_count, dtype=jnp.int32)
    numbers = jnp.arange(sum(sizes), dtype=jnp.int32)
    slot_map = jnp.zeros((slot_count, sum(sizes)), jnp.float32)
    block_base = 0
    for matrix_id in range(len(sizes)):
        inside = (
            (owners[matrix_id] == device)
            & (slot_ids >= starts_list[matrix_id])
            & (slot_ids < starts_list[matrix_id] + sizes[matrix_id])
        )
        target = block_base + slot_ids - starts_list[matrix_id]
        slot_map = slot_map + (inside[:, None] & (target[:, None] == numbers[None, :])).astype(
            jnp.float32
        )
        block_base += sizes[matrix_id]
    return slot_map


def to_matrix(blocks, by_rows):
    if by_rows:
        return blocks.reshape(-1, blocks.shape[2])
    return blocks.transpose(1, 0, 2).reshape(blocks.shape[1], -1)


def to_blocks(matrix, by_rows, features):
    if by_rows:
        return matrix.reshape(-1, features, features)
    return matrix.reshape(features, -1, features).transpose(1, 0, 2)


def all_blocks(matrices, features):
    return jnp.concatenate(
        [to_blocks(matrices[matrix_id], row_kinds[matrix_id], features) for matrix_id in range(6)],
        0,
    )


def adam_update(weight, gradient, first_moment, second, fix_first, fix_second, rate, decay):
    first_new = beta_one * first_moment + (1.0 - beta_one) * gradient
    second_new = beta_two * second + (1.0 - beta_two) * gradient * gradient
    direction = first_new / fix_first / (jnp.sqrt(second_new / fix_second) + adam_eps)
    return (weight - rate * (direction + decay * weight), first_new, second_new)


def scores_for(query_block, key_rows, start_row, segment, head_slope):
    block_rows = query_block.shape[0]
    row_total = key_rows.shape[0]
    row_ids = start_row + jnp.arange(block_rows, dtype=jnp.int32)
    col_ids = jnp.arange(row_total, dtype=jnp.int32)
    distance = (row_ids[:, None] - col_ids[None, :]).astype(jnp.float32)
    seg_rows = lax.dynamic_slice_in_dim(segment, start_row, block_rows)
    allowed = (seg_rows[:, None] == segment[None, :]) & (col_ids[None, :] <= row_ids[:, None])
    raw_score = (
        jnp.dot(query_block, key_rows.T, preferred_element_type=jnp.float32) * 0.125
        - head_slope * distance
    )
    return (jnp.where(allowed, raw_score, masked_score), distance)


def attend(queries, key_rows, values, segment, head_slope, block_rows):
    row_total, head_width = queries.shape

    def per_block(start_row):
        query_block = lax.dynamic_slice_in_dim(queries, start_row, block_rows)
        scores, distance = scores_for(query_block, key_rows, start_row, segment, head_slope)
        largest = jnp.max(scores, -1, keepdims=True)
        log_total = largest + jnp.log(jnp.sum(jnp.exp(scores - largest), -1, keepdims=True))
        probability = jnp.exp(scores - log_total).astype(jnp.bfloat16)
        return (jnp.dot(probability, values, preferred_element_type=jnp.float32), log_total[:, 0])

    row_starts = jnp.arange(row_total // block_rows, dtype=jnp.int32) * block_rows
    attended, log_totals = lax.map(per_block, row_starts)
    return (attended.reshape(row_total, head_width), log_totals.reshape(row_total))


def attend_back(queries, key_rows, values, segment, head_slope, log_totals, grad_out, block_rows):
    row_total, head_width = queries.shape

    def per_block(carried, start_row):
        grad_keys, grad_values, grad_slope = carried
        query_block = lax.dynamic_slice_in_dim(queries, start_row, block_rows)
        grad_block = lax.dynamic_slice_in_dim(grad_out, start_row, block_rows)
        total_block = lax.dynamic_slice_in_dim(log_totals, start_row, block_rows)
        scores, distance = scores_for(query_block, key_rows, start_row, segment, head_slope)
        probability = jnp.exp(scores - total_block[:, None])
        grad_prob = jnp.dot(grad_block, values.T, preferred_element_type=jnp.float32)
        grad_score = (
            probability * (grad_prob - jnp.sum(probability * grad_prob, -1, keepdims=True))
        ).astype(jnp.bfloat16)
        grad_query = jnp.dot(grad_score, key_rows, preferred_element_type=jnp.float32) * 0.125
        grad_keys = (
            grad_keys
            + jnp.dot(grad_score.T, query_block, preferred_element_type=jnp.float32) * 0.125
        )
        grad_values = grad_values + jnp.dot(
            probability.astype(jnp.bfloat16).T, grad_block, preferred_element_type=jnp.float32
        )
        grad_slope = grad_slope - jnp.sum(grad_score.astype(jnp.float32) * distance)
        return ((grad_keys, grad_values, grad_slope), grad_query)

    row_starts = jnp.arange(row_total // block_rows, dtype=jnp.int32) * block_rows
    initial = (
        jnp.zeros((row_total, head_width), jnp.float32),
        jnp.zeros((row_total, head_width), jnp.float32),
        jnp.zeros((), jnp.float32),
    )
    (grad_keys, grad_values, grad_slope), grad_queries = lax.scan(per_block, initial, row_starts)
    return (grad_queries.reshape(row_total, head_width), grad_keys, grad_values, grad_slope)


def body(
    tokens,
    cotangent,
    doc_lengths,
    owners,
    master,
    first_moment,
    second_moment,
    ln_gain,
    ln_bias,
    norm_m,
    norm_v,
    slopes,
    slope_m,
    slope_v,
):
    micro_count, lane_count, tok_rows, features = tokens.shape
    unit_rows = tok_rows // 3
    seq_devices = lax.axis_size("seq")
    head_count = slopes.shape[0]
    head_width = features // head_count
    lane_units = unit_rows * seq_devices
    block_rows = min(512, lane_units)
    unit_total = lane_count * unit_rows
    slot_count = master.shape[1]
    sizes = block_counts(features, FF)
    starts_list = block_starts(owners, sizes)
    batch_rank = lax.axis_index("batch")
    seq_rank = lax.axis_index("seq")
    lane_rank = seq_rank // head_count
    head_rank = seq_rank % head_count
    low_slots = master[0].astype(jnp.bfloat16)
    fetched = []
    for matrix_id in range(6):
        owned_rows = lax.dynamic_slice_in_dim(
            low_slots, starts_list[matrix_id], sizes[matrix_id], 0
        )
        fetched.append(broadcast(owned_rows, "batch", owners[matrix_id]))
    gathered = lax.all_gather(for_sending(tuple(fetched)), "seq", axis=1, tiled=True)
    pool_weight, qkv_weight, out_weight, in_weight, back_weight, up_weight = [
        to_matrix(gathered[matrix_id], row_kinds[matrix_id]) for matrix_id in range(6)
    ]
    doc_ends = jnp.cumsum(doc_lengths, -1)
    doc_starts = jnp.concatenate(
        [jnp.zeros((micro_count, lane_count, 1), jnp.int32), doc_ends[..., :-1]], -1
    )
    unit_ids = seq_rank * unit_rows + jnp.arange(unit_rows, dtype=jnp.int32)
    keep_mask = 1.0 - jnp.any(
        unit_ids[None, None, :, None] == doc_starts[:, :, None, :], -1
    ).astype(jnp.float32)
    triples = tokens.reshape(micro_count, lane_count, unit_rows, 3, features)
    tail_tokens = triples[:, :, -1, 1:3]
    arrived = passed_along(tail_tokens, "seq", 1)
    lane_pick = jnp.arange(lane_count, dtype=jnp.int32) == lane_rank
    head_pick = jnp.arange(head_count, dtype=jnp.int32) == head_rank
    head_slope = jnp.sum(jnp.where(head_pick, slopes, 0.0))
    positions = jnp.arange(lane_units, dtype=jnp.int32)
    gain_grad = jnp.zeros((2, features), jnp.float32)
    bias_grad = jnp.zeros((2, features), jnp.float32)
    slope_grad = jnp.zeros((), jnp.float32)
    summed = None
    mixed_parts = []
    grad_parts = []
    outgoing = []
    for micro in range(micro_count):
        triple_now = triples[micro]
        keep_now = keep_mask[micro]
        earlier = jnp.concatenate([arrived[micro][:, None], triple_now[:, :-1, 1:3]], 1) * keep_now[
            :, :, None, None
        ].astype(jnp.bfloat16)
        pool_input = jnp.concatenate([earlier, triple_now[:, :, 0:1]], 2).reshape(
            unit_total, 3 * features
        )
        pooled = jnp.dot(pool_input, pool_weight, preferred_element_type=jnp.float32)
        normed = layer_norm(pooled, ln_gain[0], ln_bias[0]).astype(jnp.bfloat16)
        projected = jnp.dot(normed, qkv_weight, preferred_element_type=jnp.float32).astype(
            jnp.bfloat16
        )
        outbound = (
            projected.reshape(lane_count, unit_rows, 3, head_count, head_width)
            .transpose(0, 3, 1, 2, 4)
            .reshape(lane_count * head_count, unit_rows * 3 * head_width)
        )
        received = lax.all_to_all(outbound, "seq", split_axis=0, concat_axis=1, tiled=True).reshape(
            lane_units, 3, head_width
        )
        queries = received[:, 0]
        key_rows = received[:, 1]
        values = received[:, 2]
        lengths = jnp.sum(jnp.where(lane_pick[:, None], doc_lengths[micro], 0), 0)
        lane_ends = jnp.cumsum(lengths)
        segment = jnp.sum((positions[:, None] >= lane_ends[None, :-1]).astype(jnp.int32), 1)
        attended, log_totals = attend(queries, key_rows, values, segment, head_slope, block_rows)
        returned = lax.all_to_all(
            attended.astype(jnp.bfloat16).reshape(1, lane_units * head_width),
            "seq",
            split_axis=1,
            concat_axis=0,
            tiled=True,
        )
        merged = (
            returned.reshape(lane_count, head_count, unit_rows, head_width)
            .transpose(0, 2, 1, 3)
            .reshape(unit_total, features)
        )
        residual = pooled + jnp.dot(merged, out_weight, preferred_element_type=jnp.float32)
        normed_two = layer_norm(residual, ln_gain[1], ln_bias[1]).astype(jnp.bfloat16)
        hidden = jnp.dot(normed_two, in_weight, preferred_element_type=jnp.float32)
        activated = gelu_tanh(hidden).astype(jnp.bfloat16)
        shortened = residual + jnp.dot(activated, back_weight, preferred_element_type=jnp.float32)
        short_low = shortened.astype(jnp.bfloat16)
        upward = jnp.dot(short_low, up_weight, preferred_element_type=jnp.float32).reshape(
            lane_count, unit_rows * 3, features
        )
        mixed_parts.append(tokens[micro].astype(jnp.float32) + upward)
        grad_upward = cotangent[micro].reshape(unit_total, 3 * features)
        sum_up = jnp.dot(short_low.T, grad_upward, preferred_element_type=jnp.float32)
        grad_short = jnp.dot(grad_upward, up_weight.T, preferred_element_type=jnp.float32)
        grad_short_low = grad_short.astype(jnp.bfloat16)
        sum_back = jnp.dot(activated.T, grad_short_low, preferred_element_type=jnp.float32)
        grad_activated = jnp.dot(grad_short_low, back_weight.T, preferred_element_type=jnp.float32)
        grad_hidden = jax.vjp(gelu_tanh, hidden)[1](grad_activated)[0].astype(jnp.bfloat16)
        sum_in = jnp.dot(normed_two.T, grad_hidden, preferred_element_type=jnp.float32)
        grad_normed_two = jnp.dot(grad_hidden, in_weight.T, preferred_element_type=jnp.float32)
        norm_two_back = jax.vjp(layer_norm, residual, ln_gain[1], ln_bias[1])[1]
        grad_resid_norm, grad_gain_two, grad_bias_two = norm_two_back(grad_normed_two)
        grad_residual = grad_short + grad_resid_norm
        grad_resid_low = grad_residual.astype(jnp.bfloat16)
        sum_out = jnp.dot(merged.T, grad_resid_low, preferred_element_type=jnp.float32)
        grad_merged = jnp.dot(
            grad_resid_low, out_weight.T, preferred_element_type=jnp.float32
        ).astype(jnp.bfloat16)
        back_outbound = (
            grad_merged.reshape(lane_count, unit_rows, head_count, head_width)
            .transpose(0, 2, 1, 3)
            .reshape(lane_count * head_count, unit_rows * head_width)
        )
        grad_attended = lax.all_to_all(
            back_outbound, "seq", split_axis=0, concat_axis=1, tiled=True
        ).reshape(lane_units, head_width)
        grad_queries, grad_keys, grad_values, grad_slope = attend_back(
            queries, key_rows, values, segment, head_slope, log_totals, grad_attended, block_rows
        )
        grad_heads = (
            jnp.stack([grad_queries, grad_keys, grad_values], 1)
            .astype(jnp.bfloat16)
            .reshape(1, lane_units * 3 * head_width)
        )
        grad_arrived = lax.all_to_all(grad_heads, "seq", split_axis=1, concat_axis=0, tiled=True)
        grad_projected = (
            grad_arrived.reshape(lane_count, head_count, unit_rows, 3, head_width)
            .transpose(0, 2, 3, 1, 4)
            .reshape(unit_total, 3 * features)
        )
        sum_qkv = jnp.dot(normed.T, grad_projected, preferred_element_type=jnp.float32)
        grad_normed = jnp.dot(grad_projected, qkv_weight.T, preferred_element_type=jnp.float32)
        norm_one_back = jax.vjp(layer_norm, pooled, ln_gain[0], ln_bias[0])[1]
        grad_pool_norm, grad_gain_one, grad_bias_one = norm_one_back(grad_normed)
        grad_pooled_low = (grad_residual + grad_pool_norm).astype(jnp.bfloat16)
        sum_pool = jnp.dot(pool_input.T, grad_pooled_low, preferred_element_type=jnp.float32)
        grad_pieces = jnp.dot(
            grad_pooled_low, pool_weight.T, preferred_element_type=jnp.float32
        ).reshape(lane_count, unit_rows, 3, features)
        grad_earlier = grad_pieces[:, :, 0:2] * keep_now[:, :, None, None]
        outgoing.append(grad_earlier[:, 0])
        following = jnp.concatenate(
            [grad_earlier[:, 1:], jnp.zeros((lane_count, 1, 2, features), jnp.float32)], 1
        )
        token_grad = jnp.concatenate([grad_pieces[:, :, 2:3], following], 2).reshape(
            lane_count, unit_rows * 3, features
        )
        grad_parts.append(cotangent[micro].astype(jnp.float32) + token_grad)
        gain_grad = gain_grad + jnp.stack([grad_gain_one, grad_gain_two])
        bias_grad = bias_grad + jnp.stack([grad_bias_one, grad_bias_two])
        slope_grad = slope_grad + grad_slope
        micro_grads = [sum_pool, sum_qkv, sum_out, sum_in, sum_back, sum_up]
        summed = (
            micro_grads
            if summed is None
            else [left + right for left, right in zip(summed, micro_grads)]
        )
    reduced = lax.psum_scatter(all_blocks(summed, features), "seq", scatter_dimension=1, tiled=True)
    incoming = passed_along(jnp.stack(outgoing).astype(jnp.bfloat16), "seq", -1).astype(jnp.float32)
    grad_tokens = jnp.stack(grad_parts).reshape(micro_count, lane_count, unit_rows, 3, features)
    grad_tokens = grad_tokens.at[:, :, -1, 1:3].add(incoming).reshape(tokens.shape)
    reduced_all = lax.psum(reduced, "batch")
    norm_grad, slopes_grad = lax.psum(
        (jnp.concatenate([gain_grad, bias_grad], 0), jnp.where(head_pick, slope_grad, 0.0)),
        ("batch", "seq"),
    )
    slot_map = slot_table(owners, batch_rank, sizes, slot_count)
    is_owned = jnp.sum(slot_map, -1)[:, None, None] > 0.5
    slot_grads = jnp.einsum("jb,brc->jrc", slot_map, reduced_all, precision=lax.Precision.HIGHEST)
    step_float = jnp.float32(STEP)
    fix_first = 1.0 - jnp.power(jnp.float32(beta_one), step_float)
    fix_second = 1.0 - jnp.power(jnp.float32(beta_two), step_float)
    new_weight, new_first, new_second = adam_update(
        master[0],
        slot_grads,
        first_moment[0],
        second_moment[0],
        fix_first,
        fix_second,
        rate_matrix,
        decay_rate,
    )
    new_weight = jnp.where(is_owned, new_weight, master[0])
    new_first = jnp.where(is_owned, new_first, first_moment[0])
    new_second = jnp.where(is_owned, new_second, second_moment[0])
    norm_now = jnp.concatenate([ln_gain, ln_bias], 0)
    new_norm, new_norm_m, new_norm_v = adam_update(
        norm_now, norm_grad, norm_m, norm_v, fix_first, fix_second, rate_norm, 0.0
    )
    new_slopes, new_slope_m, new_slope_v = adam_update(
        slopes, slopes_grad, slope_m, slope_v, fix_first, fix_second, rate_slope, 0.0
    )
    return (
        jnp.stack(mixed_parts),
        grad_tokens,
        new_weight[None],
        new_first[None],
        new_second[None],
        new_weight[None].astype(jnp.bfloat16),
        new_norm,
        new_norm_m,
        new_norm_v,
        new_slopes,
        new_slope_m,
        new_slope_v,
    )


def solution(mesh):
    in_specs = (
        P("batch", None, "seq", None),
        P("batch", None, "seq", None),
        P("batch", None, None),
        P(),
        P("batch", None, "seq", None),
        P("batch", None, "seq", None),
        P("batch", None, "seq", None),
        P(),
        P(),
        P(),
        P(),
        P(),
        P(),
        P(),
    )
    out_specs = (
        P("batch", None, "seq", None),
        P("batch", None, "seq", None),
        P("batch", None, "seq", None),
        P("batch", None, "seq", None),
        P("batch", None, "seq", None),
        P("batch", None, "seq", None),
        P(),
        P(),
        P(),
        P(),
        P(),
        P(),
    )
    return jax.shard_map(body, mesh=mesh, in_specs=in_specs, out_specs=out_specs, check_vma=False)
```

profile of v0, /device:TPU:0, one launch (start us, length us, event | category | flops | bytes accessed | tf_op | source)
XLA Modules:
  0.0 1103.6 jit_solution(6913971049612212684)
XLA Ops:
  35.5 41.2 %all-reduce.10.cloned.1.call-done = (bf16[3,64,512]{2,1,0:T(8,128)(2,1)}, bf16[3,64,512]{2,1,0:T(8,128)(2,1)}, bf16[1,64,512]{2,1,0:T(8,128)(2,1)}, bf16[4,64,51...) async-done(((bf16[3,64,512]{2,1,0:T(8,128)(2,1)}, bf16[3,64,512]{2,1,0:T(8,128)(2,1)}, bf16[1,64,512]{2,1,0:T(8,128)(2,1)}, ...) | async-done | bytes 1179664 | tf_op jit(solution)/shard_map/psum | solution.py:24
  78.6 3.4 collective-permute-start
  88.6 34.4 %all_gather.20 = bf16[1,512,512]{2,1,0:T(8,128)(2,1)} all-gather(bf16[1,64,512]{2,1,0:T(8,128)(2,1)S(1)} %copy-done.58), channel_id=1, replica_groups=mesh['batch'=4,'seq'=8] {'seq'}, dimensions={1}, use_global_device_ids=true | all-gather | bytes 589824 | tf_op jit(solution)/shard_map/all_gather | solution.py:218
  123.0 4.0 all-gather.8.cloned.1.call-done
  128.7 43.6 %all-gather.6.cloned.1.call-done = bf16[3,512,512]{2,1,0:T(8,128)(2,1)} async-done(((bf16[3,64,512]{2,1,0:T(8,128)(2,1)}), bf16[3,512,512]{2,1,0:T(8,128)(2,1)}) %all-gather.6.cloned.1.call-update) | async-done | bytes 1572880 | tf_op jit(solution)/shard_map/all_gather | solution.py:218
  178.7 4.0 all-to-all-start
  182.8 35.8 %all-gather.14.cloned.1.call-done = bf16[3,512,512]{2,1,0:T(8,128)(2,1)} async-done(((bf16[3,64,512]{2,1,0:T(8,128)(2,1)}), bf16[3,512,512]{2,1,0:T(8,128)(2,1)}) %all-gather.14.cloned.1.call-update) | async-done | bytes 1572880 | tf_op jit(solution)/shard_map/all_gather | solution.py:218
  230.2 3.7 all-to-all-start.2
  240.5 3.5 all-to-all-done.2
  244.0 3.3 all-to-all-start.1
  254.5 4.4 all-to-all-start.3
  259.5 6.2 all-to-all-done.3
  278.2 43.3 %all-gather.12.cloned.1.call-done = bf16[4,512,512]{2,1,0:T(8,128)(2,1)} async-done(((bf16[4,64,512]{2,1,0:T(8,128)(2,1)}), bf16[4,512,512]{2,1,0:T(8,128)(2,1)}) %all-gather.12.cloned.1.call-update) | async-done | bytes 2097168 | tf_op jit(solution)/shard_map/all_gather | solution.py:218
  321.6 2.9 fusion.5
  337.5 4.4 all-to-all-start.6
  343.7 5.1 convolution_add_fusion.4
  357.1 6.0 reshape.828
  363.1 6.8 copy.248
  369.9 3.5 copy.244
  373.5 5.2 copy.245
  378.6 6.1 all-to-all-start.4
  391.5 5.3 all-to-all-start.7
  404.2 3.7 all-to-all-start.5
  410.2 5.2 all-to-all-done.5
  420.3 4.1 copy.246
  429.1 3.5 copy.243
  432.6 184.1 %concatenate.74 = f32[18,512,512]{2,0,1:T(8,128)} concatenate(f32[3,512,512]{2,0,1:T(4,128)} %copy.246, f32[3,512,512]{2,0,1:T(4,128)} %bitcast.318, f32[1,512,512]{2,0,1:T(1,128)} %copy.247, f32[4,512,512]{2,0,1:T(4,128)} %bitcast.319, f32[4,512,512]{2,0,1:T(4,128)} %copy.248, f32[3,512,512]{2,0,1:T(4,128)} %bitcast.317), dimensions={0} | concatenate | bytes 37748736 | tf_op jit(solution)/shard_map/concatenate | solution.py:101
  627.2 43.9 %all-reduce.3 = (f32[4,512]{1,0:T(4,128)S(1)}, f32[8]{0:T(128)S(1)}) all-reduce(f32[4,512]{1,0:T(4,128)S(1)} %pad_maximum_fusion.8, f32[8]{0:T(128)S(1)} %compare_select_fusion), channel_id=1, replica_groups=mesh['batch'=4,'seq'=8] {'batch','seq'}, use_global_device_ids=true, to_apply=%region_46.47 | all-reduce | flops 2056 | bytes 16448 | tf_op jit(solution)/shard_map/psum | solution.py:366
  671.6 348.0 %reduce-scatter.2.cloned.1.call-done = f32[18,64,512]{2,0,1:T(8,128)} async-done(((f32[18,512,512]{2,0,1:T(8,128)}), f32[18,64,512]{2,0,1:T(8,128)}) %reduce-scatter.2.cloned.1.call-update) | async-done | bytes 2359312 | tf_op jit(solution)/shard_map/reduce_scatter | solution.py:361
  1026.0 63.5 %all-reduce.8.cloned.1.call-done = f32[18,64,512]{2,0,1:T(8,128)} async-done(((f32[18,64,512]{2,0,1:T(8,128)}), f32[18,64,512]{2,0,1:T(8,128)}) %all-reduce.8.cloned.1.call-update) | async-done | bytes 2359312 | tf_op jit(solution)/shard_map/psum | solution.py:365
  1089.5 3.6 fusion.87
  1093.1 3.4 convert_bitcast_fusion
  (469 shorter events, 119.8 us)
Async XLA Ops:
  7.2 69.5 %all-reduce.10.cloned.1.call-start = ((), (), s32[]{:S(2)}) async-start(), calls=%async_computation.16 | async-start | bytes 2359296 | tf_op jit(solution)/shard_map/psum | solution.py:24
  34.6 50.3 %copy-start.59 = (f32[2,512]{1,0:T(2,128)S(1)}, f32[2,512]{1,0:T(2,128)}, u32[]{:S(2)}) copy-start(f32[2,512]{1,0:T(2,128)} %param.24) | copy-start | bytes 12292
  34.6 50.3 %copy-start.60 = (f32[2,512]{1,0:T(2,128)S(1)}, f32[2,512]{1,0:T(2,128)}, u32[]{:S(2)}) copy-start(f32[2,512]{1,0:T(2,128)} %param.23) | copy-start | bytes 12292
  34.6 50.4 %copy-start.49 = (bf16[2,1,144,512]{3,2,1,0:T(8,128)(2,1)S(1)}, bf16[2,1,144,512]{3,2,1,0:T(8,128)(2,1)}, u32[]{:S(2)}) copy-start(bf16[2,1,144,512]{3,2,1,0:T(8,128)(2,1)} %param.17) | copy-start | bytes 884740
  35.4 91.5 %all-gather.8.cloned.1.call-start = ((), (), s32[]{:S(2)}) async-start(), calls=%async_computation.10 | async-start | bytes 1769472 | tf_op jit(solution)/shard_map/all_gather | solution.py:218
  76.7 95.6 %all-gather.6.cloned.1.call-start = ((), (), s32[]{:S(2)}) async-start(), calls=%async_computation.9 | async-start | bytes 1769472 | tf_op jit(solution)/shard_map/all_gather | solution.py:218
  77.4 141.2 %all-gather.14.cloned.1.call-start = ((), (), s32[]{:S(2)}) async-start(), calls=%async_computation.13 | async-start | bytes 1769472 | tf_op jit(solution)/shard_map/all_gather | solution.py:218
  78.0 193.8 %all-gather.10.cloned.1.call-start = ((), (), s32[]{:S(2)}) async-start(), calls=%async_computation.11 | async-start | bytes 2359296 | tf_op jit(solution)/shard_map/all_gather | solution.py:218
  78.6 243.0 %all-gather.12.cloned.1.call-start = ((), (), s32[]{:S(2)}) async-start(), calls=%async_computation.12 | async-start | bytes 2359296 | tf_op jit(solution)/shard_map/all_gather | solution.py:218
  78.6 8.4 collective-permute-start
  86.3 141.8 %copy-start.22 = (bf16[48,1536]{1,0:T(8,128)(2,1)}, bf16[48,1536]{1,0:T(8,128)(2,1)S(1)}, u32[]{:S(2)}) copy-start(bf16[48,1536]{1,0:T(8,128)(2,1)S(1)} %reshape_squeeze.7) | copy-start | bytes 442372
  87.6 84.7 %copy-start.27 = (bf16[6,8,3,512]{3,1,2,0:T(8,128)(2,1)}, bf16[6,8,3,512]{3,1,2,0:T(8,128)(2,1)S(1)}, u32[]{:S(2)}) copy-start(bf16[6,8,3,512]{3,1,2,0:T(8,128)(2,1)S(1)} %copy.257) | copy-start | bytes 442372
  128.7 94.5 %copy-start = (bf16[512,3,512]{0,2,1:T(8,128)(2,1)}, bf16[512,3,512]{0,2,1:T(8,128)(2,1)S(1)}, u32[]{:S(2)}) copy-start(bf16[512,3,512]{0,2,1:T(8,128)(2,1)S(1)} %copy.208) | copy-start | bytes 4718596
  174.2 92.0 %copy-start.9 = (f32[48,512]{1,0:T(8,128)}, f32[48,512]{1,0:T(8,128)S(1)}, u32[]{:S(2)}) copy-start(f32[48,512]{1,0:T(8,128)S(1)} %get-tuple-element.304) | copy-start | bytes 294916
  178.7 51.4 %all-to-all-start = ((bf16[8,2,4608]{2,1,0:T(2,128)(2,1)}), bf16[8,2,4608]{2,1,0:T(2,128)(2,1)}, u32[]{:S(2)}, u32[]{:S(2)}) async-start(bf16[8,2,4608]{2,1,0:T(2,128)(2,1)} %reshape.861), calls=%async_computation | async-start | bytes 294912 | tf_op jit(solution)/shard_map/all_to_all | solution.py:263
  230.2 13.8 %all-to-all-start.2 = ((bf16[8,2,4608]{2,1,0:T(2,128)(2,1)}), bf16[8,2,4608]{2,1,0:T(2,128)(2,1)S(1)}, u32[]{:S(2)}, u32[]{:S(2)}) async-start(bf16[8,2,4608]{2,1,0:T(2,128)(2,1)} %reshape.857), calls=%async_computation.2 | async-start | bytes 294912 | tf_op jit(solution)/shard_map/all_to_all | solution.py:263
  244.0 10.5 all-to-all-start.1
  254.5 11.1 %all-to-all-start.3 = ((bf16[8,2,1536]{2,1,0:T(2,128)(2,1)}), bf16[8,2,1536]{2,1,0:T(2,128)(2,1)S(1)}, u32[]{:S(2)}, u32[]{:S(2)}) async-start(bf16[8,2,1536]{2,1,0:T(2,128)(2,1)} %reshape.859), calls=%async_computation.3 | async-start | bytes 98304 | tf_op jit(solution)/shard_map/all_to_all | solution.py:273
  337.5 41.1 %all-to-all-start.6 = ((bf16[8,2,1536]{2,1,0:T(2,128)(2,1)}), bf16[8,2,1536]{2,1,0:T(2,128)(2,1)}, u32[]{:S(2)}, u32[]{:S(2)}) async-start(bf16[8,2,1536]{2,1,0:T(2,128)(2,1)} %reshape.865), calls=%async_computation.6 | async-start | bytes 98304 | tf_op jit(solution)/shard_map/all_to_all | solution.py:317
  378.6 12.9 %all-to-all-start.4 = ((bf16[8,2,1536]{2,1,0:T(2,128)(2,1)}), bf16[8,2,1536]{2,1,0:T(2,128)(2,1)S(1)}, u32[]{:S(2)}, u32[]{:S(2)}) async-start(bf16[8,2,1536]{2,1,0:T(2,128)(2,1)} %reshape.869), calls=%async_computation.4 | async-start | bytes 98304 | tf_op jit(solution)/shard_map/all_to_all | solution.py:317
  391.5 12.7 %all-to-all-start.7 = ((bf16[8,2,4608]{2,1,0:T(2,128)(2,1)}), bf16[8,2,4608]{2,1,0:T(2,128)(2,1)S(1)}, u32[]{:S(2)}, u32[]{:S(2)}) async-start(bf16[8,2,4608]{2,1,0:T(2,128)(2,1)} %reshape.867), calls=%async_computation.7 | async-start | bytes 294912 | tf_op jit(solution)/shard_map/all_to_all | solution.py:328
  404.2 11.1 %all-to-all-start.5 = ((bf16[8,2,4608]{2,1,0:T(2,128)(2,1)}), bf16[8,2,4608]{2,1,0:T(2,128)(2,1)S(1)}, u32[]{:S(2)}, u32[]{:S(2)}) async-start(bf16[8,2,4608]{2,1,0:T(2,128)(2,1)} %reshape.871), calls=%async_computation.5 | async-start | bytes 294912 | tf_op jit(solution)/shard_map/all_to_all | solution.py:328
  407.9 611.6 %reduce-scatter.2.cloned.1.call-start = ((), (), s32[]{:S(2)}) async-start(), calls=%async_computation.14 | async-start | bytes 28311552 | tf_op jit(solution)/shard_map/reduce_scatter | solution.py:361
  616.7 472.8 %all-reduce.8.cloned.1.call-start = ((), (), s32[]{:S(2)}) async-start(), calls=%async_computation.15 | async-start | bytes 6291456 | tf_op jit(solution)/shard_map/psum | solution.py:365
  626.7 394.2 %copy-start.79 = (f32[4,512]{1,0:T(4,128)S(1)}, f32[4,512]{1,0:T(4,128)}, u32[]{:S(2)}) copy-start(f32[4,512]{1,0:T(4,128)} %param.26) | copy-start | bytes 24580
  626.7 394.2 %copy-start.80 = (f32[4,512]{1,0:T(4,128)S(1)}, f32[4,512]{1,0:T(4,128)}, u32[]{:S(2)}) copy-start(f32[4,512]{1,0:T(4,128)} %param.25) | copy-start | bytes 24580
  626.7 394.8 %copy-start.32 = (bf16[1,1,144,512]{3,2,1,0:T(8,128)(2,1)S(1)}, bf16[1,1,144,512]{3,2,1,0:T(8,128)(2,1)}, u32[]{:S(2)}) copy-start(bf16[1,1,144,512]{3,2,1,0:T(8,128)(2,1)} %copy-done.31) | copy-start | bytes 442372
  627.0 394.8 %copy-start.30 = (bf16[1,1,144,512]{3,2,1,0:T(8,128)(2,1)S(1)}, bf16[1,1,144,512]{3,2,1,0:T(8,128)(2,1)}, u32[]{:S(2)}) copy-start(bf16[1,1,144,512]{3,2,1,0:T(8,128)(2,1)} %copy-done.29) | copy-start | bytes 442372
  1019.6 5.5 collective-permute-start.1
  1026.0 67.1 %copy-start.14 = (f32[1,8,64,512]{3,2,1,0:T(8,128)S(1)}, f32[1,8,64,512]{3,2,1,0:T(8,128)}, u32[]{:S(2)}) copy-start(f32[1,8,64,512]{3,2,1,0:T(8,128)} %param.20) | copy-start | bytes 3145732
  1026.0 67.1 %copy-start.33 = (f32[1,8,64,512]{3,2,1,0:T(8,128)S(1)}, f32[1,8,64,512]{3,2,1,0:T(8,128)}, u32[]{:S(2)}) copy-start(f32[1,8,64,512]{3,2,1,0:T(8,128)} %param.22) | copy-start | bytes 3145732
  1026.0 67.1 %copy-start.34 = (f32[1,8,64,512]{3,2,1,0:T(8,128)S(1)}, f32[1,8,64,512]{3,2,1,0:T(8,128)}, u32[]{:S(2)}) copy-start(f32[1,8,64,512]{3,2,1,0:T(8,128)} %param.21) | copy-start | bytes 3145732
  (88 other events, 696.6 us)
Sparse Core Ops, SparseCore 0:
  35.6 41.0 all-reduce.9
  78.8 48.0 all-gather.7
  129.1 43.1 all-gather.5
  174.3 44.2 all-gather.13
  220.6 51.0 all-gather.9
  273.8 47.7 all-gather.11
  616.8 402.6 reduce-scatter.1
  1021.9 67.5 all-reduce.7
where the time goes:
time: 1120 us; the launch traced here: 1100 us
  waiting for transfers between devices  606 us (54%)
  local copies, waits for them, and re-layouts  252 us (22%)
  blocking collectives  78.2 us (7%)
  matrix products  52.5 us (5%)
  between operations  44.8 us (4%)
  starting transfers between devices  40.1 us (4%)
  other arithmetic  30.2 us (3%)
    reduce_scatter x1, waiting for transfers between devices, body(): lax.psum_scatter(all_blocks(summed, features), 'seq', scatter_dimension=1...  348 us
    concatenate x1, local copies, waits for them, and re-layouts, all_blocks(): jnp.concatenate([to_blocks(matrices[matrix_id], row_kinds[matrix_id], fea...  184 us
    all_gather x5, waiting for transfers between devices, body(): lax.all_gather(for_sending(tuple(fetched)), 'seq', axis=1, tiled=True)  130 us
    psum x1, waiting for transfers between devices, body(): reduced_all = lax.psum(reduced, 'batch')  63.5 us
    psum x1, blocking collectives, body(): lax.psum((jnp.concatenate([gain_grad, bias_grad], 0), jnp.where(head_pick...  43.9 us
    psum x1, waiting for transfers between devices, broadcast(): return lax.psum(kept, axis)  41.2 us
    all_gather x1, blocking collectives, body(): lax.all_gather(for_sending(tuple(fetched)), 'seq', axis=1, tiled=True)  34.4 us
  transfers between devices with their start and end apart: 18, of which 15 were waited for; matrix products, arithmetic and copies ran while one was open for 9% of the time, Pallas kernels for 0%

commit v1 on v0

--- a/solution.py
+++ b/solution.py
@@ -22,6 +22,14 @@
 def broadcast(value, axis, source):
     kept = jnp.where(lax.axis_index(axis) == source, value, 0).astype(value.dtype)
     return lax.psum(kept, axis)
+
+
+def running_total(lengths):
+    count = lengths.shape[-1]
+    ends = [lengths[..., 0]]
+    for index in range(1, count):
+        ends.append(ends[-1] + lengths[..., index])
+    return jnp.stack(ends, -1)
 
 
 def for_sending(value):
@@ -219,7 +227,7 @@
     pool_weight, qkv_weight, out_weight, in_weight, back_weight, up_weight = [
         to_matrix(gathered[matrix_id], row_kinds[matrix_id]) for matrix_id in range(6)
     ]
-    doc_ends = jnp.cumsum(doc_lengths, -1)
+    doc_ends = running_total(doc_lengths)
     doc_starts = jnp.concatenate(
         [jnp.zeros((micro_count, lane_count, 1), jnp.int32), doc_ends[..., :-1]], -1
     )
@@ -267,7 +275,7 @@
         key_rows = received[:, 1]
         values = received[:, 2]
         lengths = jnp.sum(jnp.where(lane_pick[:, None], doc_lengths[micro], 0), 0)
-        lane_ends = jnp.cumsum(lengths)
+        lane_ends = running_total(lengths)
         segment = jnp.sum((positions[:, None] >= lane_ends[None, :-1]).astype(jnp.int32), 1)
         attended, log_totals = attend(queries, key_rows, values, segment, head_slope, block_rows)
         returned = lax.all_to_all(

time: 1120 us -> 1120 us (level)
  transfers between devices with their start and end apart: 18 -> 18, of which waited for: 15 -> 14; matrix products, arithmetic and copies ran while one was open for 9% -> 9% of each run, Pallas kernels for 0% -> 0%
where the time goes in v1:
time: 1120 us; the launch traced here: 1110 us
  waiting for transfers between devices  602 us (54%)
  local copies, waits for them, and re-layouts  252 us (22%)
  blocking collectives  78.4 us (7%)
  matrix products  52.6 us (5%)
  between operations  48.9 us (4%)
  starting transfers between devices  39.9 us (4%)
  other arithmetic  30.8 us (3%)
    reduce_scatter x1, waiting for transfers between devices, body(): lax.psum_scatter(all_blocks(summed, features), 'seq', scatter_dimension=1...  348 us
    concatenate x1, local copies, waits for them, and re-layouts, all_blocks(): jnp.concatenate([to_blocks(matrices[matrix_id], row_kinds[matrix_id], fea...  184 us
    all_gather x5, waiting for transfers between devices, body(): lax.all_gather(for_sending(tuple(fetched)), 'seq', axis=1, tiled=True)  126 us
    psum x1, waiting for transfers between devices, body(): reduced_all = lax.psum(reduced, 'batch')  63.5 us
    psum x1, blocking collectives, body(): lax.psum((jnp.concatenate([gain_grad, bias_grad], 0), jnp.where(head_pick...  43.9 us
    psum x1, waiting for transfers between devices, broadcast(): return lax.psum(kept, axis)  41.2 us
    all_gather x1, blocking collectives, body(): lax.all_gather(for_sending(tuple(fetched)), 'seq', axis=1, tiled=True)  34.5 us
  transfers between devices with their start and end apart: 18, of which 14 were waited for; matrix products, arithmetic and copies ran while one was open for 9% of the time, Pallas kernels for 0%

profile of v1, /device:TPU:0, one launch (start us, length us, event | category | flops | bytes accessed | tf_op | source)
XLA Modules:
  0.0 1105.1 jit_solution(8457415753307224663)
XLA Ops:
  35.7 41.2 %all-reduce.9.cloned.1.call-done = (bf16[3,64,512]{2,1,0:T(8,128)(2,1)}, bf16[3,64,512]{2,1,0:T(8,128)(2,1)}, bf16[1,64,512]{2,1,0:T(8,128)(2,1)}, bf16[4,64,512...) async-done(((bf16[3,64,512]{2,1,0:T(8,128)(2,1)}, bf16[3,64,512]{2,1,0:T(8,128)(2,1)}, bf16[1,64,512]{2,1,0:T(8,128)(2,1)}, ...) | async-done | bytes 1179664 | tf_op jit(solution)/shard_map/psum | solution.py:24
  78.6 3.4 collective-permute-start
  93.9 34.5 %all_gather.20 = bf16[1,512,512]{2,1,0:T(8,128)(2,1)} all-gather(bf16[1,64,512]{2,1,0:T(8,128)(2,1)S(1)} %copy-done.58), channel_id=1, replica_groups=mesh['batch'=4,'seq'=8] {'seq'}, dimensions={1}, use_global_device_ids=true | all-gather | bytes 589824 | tf_op jit(solution)/shard_map/all_gather | solution.py:226
  130.2 43.4 %all-gather.6.cloned.1.call-done = bf16[3,512,512]{2,1,0:T(8,128)(2,1)} async-done(((bf16[3,64,512]{2,1,0:T(8,128)(2,1)}), bf16[3,512,512]{2,1,0:T(8,128)(2,1)}) %all-gather.6.cloned.1.call-update) | async-done | bytes 1572880 | tf_op jit(solution)/shard_map/all_gather | solution.py:226
  180.0 4.0 all-to-all-start
  184.1 35.8 %all-gather.14.cloned.1.call-done = bf16[3,512,512]{2,1,0:T(8,128)(2,1)} async-done(((bf16[3,64,512]{2,1,0:T(8,128)(2,1)}), bf16[3,512,512]{2,1,0:T(8,128)(2,1)}) %all-gather.14.cloned.1.call-update) | async-done | bytes 1572880 | tf_op jit(solution)/shard_map/all_gather | solution.py:226
  231.4 3.7 all-to-all-start.2
  241.7 3.5 all-to-all-done.2
  245.2 3.3 all-to-all-start.1
  255.8 4.2 all-to-all-start.3
  260.6 6.3 all-to-all-done.3
  270.1 3.2 all-gather.10.cloned.1.call-done
  279.8 43.2 %all-gather.12.cloned.1.call-done = bf16[4,512,512]{2,1,0:T(8,128)(2,1)} async-done(((bf16[4,64,512]{2,1,0:T(8,128)(2,1)}), bf16[4,512,512]{2,1,0:T(8,128)(2,1)}) %all-gather.12.cloned.1.call-update) | async-done | bytes 2097168 | tf_op jit(solution)/shard_map/all_gather | solution.py:226
  323.0 2.9 fusion.5
  339.0 4.4 all-to-all-start.6
  345.1 5.1 convolution_add_fusion.4
  358.6 6.0 reshape.846
  364.6 6.8 copy.248
  371.4 3.5 copy.244
  375.0 5.2 copy.245
  380.1 6.1 all-to-all-start.4
  393.0 5.2 all-to-all-start.7
  405.7 3.7 all-to-all-start.5
  411.6 5.2 all-to-all-done.5
  421.7 4.1 copy.246
  430.5 3.5 copy.243
  434.1 184.1 %concatenate.74 = f32[18,512,512]{2,0,1:T(8,128)} concatenate(f32[3,512,512]{2,0,1:T(4,128)} %copy.246, f32[3,512,512]{2,0,1:T(4,128)} %bitcast.320, f32[1,512,512]{2,0,1:T(1,128)} %copy.247, f32[4,512,512]{2,0,1:T(4,128)} %bitcast.321, f32[4,512,512]{2,0,1:T(4,128)} %copy.248, f32[3,512,512]{2,0,1:T(4,128)} %bitcast.319), dimensions={0} | concatenate | bytes 37748736 | tf_op jit(solution)/shard_map/concatenate | solution.py:109
  628.6 43.9 %all-reduce.2 = (f32[4,512]{1,0:T(4,128)S(1)}, f32[8]{0:T(128)S(1)}) all-reduce(f32[4,512]{1,0:T(4,128)S(1)} %pad_maximum_fusion.8, f32[8]{0:T(128)S(1)} %compare_select_fusion), channel_id=1, replica_groups=mesh['batch'=4,'seq'=8] {'batch','seq'}, use_global_device_ids=true, to_apply=%region_43.44 | all-reduce | flops 2056 | bytes 16448 | tf_op jit(solution)/shard_map/psum | solution.py:374
  673.1 347.9 %reduce-scatter.2.cloned.1.call-done = f32[18,64,512]{2,0,1:T(8,128)} async-done(((f32[18,512,512]{2,0,1:T(8,128)}), f32[18,64,512]{2,0,1:T(8,128)}) %reduce-scatter.2.cloned.1.call-update) | async-done | bytes 2359312 | tf_op jit(solution)/shard_map/reduce_scatter | solution.py:369
  1027.5 63.5 %all-reduce.7.cloned.1.call-done = f32[18,64,512]{2,0,1:T(8,128)} async-done(((f32[18,64,512]{2,0,1:T(8,128)}), f32[18,64,512]{2,0,1:T(8,128)}) %all-reduce.7.cloned.1.call-update) | async-done | bytes 2359312 | tf_op jit(solution)/shard_map/psum | solution.py:373
  1090.9 3.6 fusion.87
  1094.6 3.4 convert_bitcast_fusion
  (469 shorter events, 118.2 us)
Async XLA Ops:
  7.2 69.7 %all-reduce.9.cloned.1.call-start = ((), (), s32[]{:S(2)}) async-start(), calls=%async_computation.16 | async-start | bytes 2359296 | tf_op jit(solution)/shard_map/psum | solution.py:24
  34.8 55.4 %copy-start.59 = (f32[2,512]{1,0:T(2,128)S(1)}, f32[2,512]{1,0:T(2,128)}, u32[]{:S(2)}) copy-start(f32[2,512]{1,0:T(2,128)} %param.24) | copy-start | bytes 12292
  34.8 55.4 %copy-start.60 = (f32[2,512]{1,0:T(2,128)S(1)}, f32[2,512]{1,0:T(2,128)}, u32[]{:S(2)}) copy-start(f32[2,512]{1,0:T(2,128)} %param.23) | copy-start | bytes 12292
  34.8 55.5 %copy-start.49 = (bf16[2,1,144,512]{3,2,1,0:T(8,128)(2,1)S(1)}, bf16[2,1,144,512]{3,2,1,0:T(8,128)(2,1)}, u32[]{:S(2)}) copy-start(bf16[2,1,144,512]{3,2,1,0:T(8,128)(2,1)} %param.17) | copy-start | bytes 884740
  35.6 92.8 %all-gather.8.cloned.1.call-start = ((), (), s32[]{:S(2)}) async-start(), calls=%async_computation.10 | async-start | bytes 1769472 | tf_op jit(solution)/shard_map/all_gather | solution.py:226
  76.9 96.7 %all-gather.6.cloned.1.call-start = ((), (), s32[]{:S(2)}) async-start(), calls=%async_computation.9 | async-start | bytes 1769472 | tf_op jit(solution)/shard_map/all_gather | solution.py:226
  77.6 142.2 %all-gather.14.cloned.1.call-start = ((), (), s32[]{:S(2)}) async-start(), calls=%async_computation.13 | async-start | bytes 1769472 | tf_op jit(solution)/shard_map/all_gather | solution.py:226
  78.2 195.1 %all-gather.10.cloned.1.call-start = ((), (), s32[]{:S(2)}) async-start(), calls=%async_computation.11 | async-start | bytes 2359296 | tf_op jit(solution)/shard_map/all_gather | solution.py:226
  78.6 13.8 %collective-permute-start = (bf16[2,1,2,512]{3,0,2,1:T(2,128)(2,1)S(1)}, bf16[2,1,2,512]{3,0,2,1:T(2,128)(2,1)S(1)}, u32[]{:S(2)}, u32[]{:S(2)}) collective-permute-start(bf16[2,1,2,512]{3,0,2,1:T(2,128)(2,1)S(1)} %slice_bitcast_fusion), channel_id=1, source_target_pairs={{0,1},{1,2},{2,3},{3,4},{4,5},{5,6},{6,7},{8,9},{9,10},{10,11},{11... | collective-permute-start | bytes 12296 | tf_op jit(solution)/shard_map/ppermute | solution.py:46
  82.0 241.0 %all-gather.12.cloned.1.call-start = ((), (), s32[]{:S(2)}) async-start(), calls=%async_computation.12 | async-start | bytes 2359296 | tf_op jit(solution)/shard_map/all_gather | solution.py:226
  91.6 137.7 %copy-start.22 = (bf16[48,1536]{1,0:T(8,128)(2,1)}, bf16[48,1536]{1,0:T(8,128)(2,1)S(1)}, u32[]{:S(2)}) copy-start(bf16[48,1536]{1,0:T(8,128)(2,1)S(1)} %reshape_squeeze.7) | copy-start | bytes 442372
  93.0 80.6 %copy-start.27 = (bf16[6,8,3,512]{3,1,2,0:T(8,128)(2,1)}, bf16[6,8,3,512]{3,1,2,0:T(8,128)(2,1)S(1)}, u32[]{:S(2)}) copy-start(bf16[6,8,3,512]{3,1,2,0:T(8,128)(2,1)S(1)} %copy.257) | copy-start | bytes 442372
  130.2 94.2 %copy-start = (bf16[512,3,512]{0,2,1:T(8,128)(2,1)}, bf16[512,3,512]{0,2,1:T(8,128)(2,1)S(1)}, u32[]{:S(2)}) copy-start(bf16[512,3,512]{0,2,1:T(8,128)(2,1)S(1)} %copy.208) | copy-start | bytes 4718596
  175.4 92.1 %copy-start.9 = (f32[48,512]{1,0:T(8,128)}, f32[48,512]{1,0:T(8,128)S(1)}, u32[]{:S(2)}) copy-start(f32[48,512]{1,0:T(8,128)S(1)} %get-tuple-element.313) | copy-start | bytes 294916
  180.0 51.3 %all-to-all-start = ((bf16[8,2,4608]{2,1,0:T(2,128)(2,1)}), bf16[8,2,4608]{2,1,0:T(2,128)(2,1)}, u32[]{:S(2)}, u32[]{:S(2)}) async-start(bf16[8,2,4608]{2,1,0:T(2,128)(2,1)} %reshape.880), calls=%async_computation | async-start | bytes 294912 | tf_op jit(solution)/shard_map/all_to_all | solution.py:271
  231.4 13.8 %all-to-all-start.2 = ((bf16[8,2,4608]{2,1,0:T(2,128)(2,1)}), bf16[8,2,4608]{2,1,0:T(2,128)(2,1)S(1)}, u32[]{:S(2)}, u32[]{:S(2)}) async-start(bf16[8,2,4608]{2,1,0:T(2,128)(2,1)} %reshape.876), calls=%async_computation.2 | async-start | bytes 294912 | tf_op jit(solution)/shard_map/all_to_all | solution.py:271
  245.2 10.6 all-to-all-start.1
  255.8 11.1 %all-to-all-start.3 = ((bf16[8,2,1536]{2,1,0:T(2,128)(2,1)}), bf16[8,2,1536]{2,1,0:T(2,128)(2,1)S(1)}, u32[]{:S(2)}, u32[]{:S(2)}) async-start(bf16[8,2,1536]{2,1,0:T(2,128)(2,1)} %reshape.878), calls=%async_computation.3 | async-start | bytes 98304 | tf_op jit(solution)/shard_map/all_to_all | solution.py:281
  339.0 41.2 %all-to-all-start.6 = ((bf16[8,2,1536]{2,1,0:T(2,128)(2,1)}), bf16[8,2,1536]{2,1,0:T(2,128)(2,1)}, u32[]{:S(2)}, u32[]{:S(2)}) async-start(bf16[8,2,1536]{2,1,0:T(2,128)(2,1)} %reshape.884), calls=%async_computation.6 | async-start | bytes 98304 | tf_op jit(solution)/shard_map/all_to_all | solution.py:325
  380.1 12.9 %all-to-all-start.4 = ((bf16[8,2,1536]{2,1,0:T(2,128)(2,1)}), bf16[8,2,1536]{2,1,0:T(2,128)(2,1)S(1)}, u32[]{:S(2)}, u32[]{:S(2)}) async-start(bf16[8,2,1536]{2,1,0:T(2,128)(2,1)} %reshape.888), calls=%async_computation.4 | async-start | bytes 98304 | tf_op jit(solution)/shard_map/all_to_all | solution.py:325
  393.0 12.6 %all-to-all-start.7 = ((bf16[8,2,4608]{2,1,0:T(2,128)(2,1)}), bf16[8,2,4608]{2,1,0:T(2,128)(2,1)S(1)}, u32[]{:S(2)}, u32[]{:S(2)}) async-start(bf16[8,2,4608]{2,1,0:T(2,128)(2,1)} %reshape.886), calls=%async_computation.7 | async-start | bytes 294912 | tf_op jit(solution)/shard_map/all_to_all | solution.py:336
  405.7 11.1 %all-to-all-start.5 = ((bf16[8,2,4608]{2,1,0:T(2,128)(2,1)}), bf16[8,2,4608]{2,1,0:T(2,128)(2,1)S(1)}, u32[]{:S(2)}, u32[]{:S(2)}) async-start(bf16[8,2,4608]{2,1,0:T(2,128)(2,1)} %reshape.890), calls=%async_computation.5 | async-start | bytes 294912 | tf_op jit(solution)/shard_map/all_to_all | solution.py:336
  409.4 611.6 %reduce-scatter.2.cloned.1.call-start = ((), (), s32[]{:S(2)}) async-start(), calls=%async_computation.14 | async-start | bytes 28311552 | tf_op jit(solution)/shard_map/reduce_scatter | solution.py:369
  618.2 472.7 %all-reduce.7.cloned.1.call-start = ((), (), s32[]{:S(2)}) async-start(), calls=%async_computation.15 | async-start | bytes 6291456 | tf_op jit(solution)/shard_map/psum | solution.py:373
  628.1 394.2 %copy-start.80 = (f32[4,512]{1,0:T(4,128)S(1)}, f32[4,512]{1,0:T(4,128)}, u32[]{:S(2)}) copy-start(f32[4,512]{1,0:T(4,128)} %param.26) | copy-start | bytes 24580
  628.1 394.2 %copy-start.81 = (f32[4,512]{1,0:T(4,128)S(1)}, f32[4,512]{1,0:T(4,128)}, u32[]{:S(2)}) copy-start(f32[4,512]{1,0:T(4,128)} %param.25) | copy-start | bytes 24580
  628.2 394.8 %copy-start.32 = (bf16[1,1,144,512]{3,2,1,0:T(8,128)(2,1)S(1)}, bf16[1,1,144,512]{3,2,1,0:T(8,128)(2,1)}, u32[]{:S(2)}) copy-start(bf16[1,1,144,512]{3,2,1,0:T(8,128)(2,1)} %copy-done.31) | copy-start | bytes 442372
  628.5 394.8 %copy-start.30 = (bf16[1,1,144,512]{3,2,1,0:T(8,128)(2,1)S(1)}, bf16[1,1,144,512]{3,2,1,0:T(8,128)(2,1)}, u32[]{:S(2)}) copy-start(bf16[1,1,144,512]{3,2,1,0:T(8,128)(2,1)} %copy-done.29) | copy-start | bytes 442372
  1021.0 5.5 collective-permute-start.1
  1027.4 67.1 %copy-start.14 = (f32[1,8,64,512]{3,2,1,0:T(8,128)S(1)}, f32[1,8,64,512]{3,2,1,0:T(8,128)}, u32[]{:S(2)}) copy-start(f32[1,8,64,512]{3,2,1,0:T(8,128)} %param.20) | copy-start | bytes 3145732
  1027.5 67.1 %copy-start.33 = (f32[1,8,64,512]{3,2,1,0:T(8,128)S(1)}, f32[1,8,64,512]{3,2,1,0:T(8,128)}, u32[]{:S(2)}) copy-start(f32[1,8,64,512]{3,2,1,0:T(8,128)} %param.22) | copy-start | bytes 3145732
  1027.5 67.1 %copy-start.34 = (f32[1,8,64,512]{3,2,1,0:T(8,128)S(1)}, f32[1,8,64,512]{3,2,1,0:T(8,128)}, u32[]{:S(2)}) copy-start(f32[1,8,64,512]{3,2,1,0:T(8,128)} %param.21) | copy-start | bytes 3145732
  (88 other events, 704.5 us)
Sparse Core Ops, SparseCore 0:
  35.8 41.0 all-reduce.8
  79.0 48.8 all-gather.7
  130.2 43.3 all-gather.5
  175.6 44.2 all-gather.13
  221.9 51.3 all-gather.9
  275.3 47.6 all-gather.11
  618.3 402.6 reduce-scatter.1
  1023.3 67.5 all-reduce.6

commit v2 on v1

--- a/solution.py
+++ b/solution.py
@@ -1,6 +1,10 @@
+import math
+
 import jax
 import jax.numpy as jnp
 from jax import lax
+from jax.experimental import pallas as pl
+from jax.experimental.pallas import tpu as pltpu
 from jax.sharding import PartitionSpec as P
 
 FF = 2048
@@ -417,6 +421,930 @@
     )
 
 
+MESH = pl.DeviceIdType.MESH
+LOW = jnp.bfloat16
+WIDE = jnp.float32
+TILE = 128
+
+
+class Plan:
+    def __init__(self):
+        self.tasks = {}
+
+    def add(self, name, run, deps=(), waits=(), sends=(), cost=0.1, rank=0):
+        assert name not in self.tasks
+        self.tasks[name] = (run, tuple(deps), tuple(waits), tuple(sends), cost, rank)
+
+    def order(self):
+        now, done, arrival, free, listed = 0.0, set(), {}, {}, []
+        left = list(self.tasks)
+        while left:
+            best = None
+            for place, name in enumerate(left):
+                run, deps, waits, sends, cost, rank = self.tasks[name]
+                if any(d not in done for d in deps) or any(w not in arrival for w in waits):
+                    continue
+                begin = max([now] + [arrival[w] for w in waits])
+                key = (begin, rank, place)
+                if best is None or key < best[0]:
+                    best = (key, name)
+            name = best[1]
+            run, deps, waits, sends, cost, rank = self.tasks[name]
+            now = best[0][0] + cost
+            for message, link, size in sends:
+                rate, delay = LINKS[link]
+                begin = max(now, free.get(link, 0.0))
+                free[link] = begin + size / rate
+                arrival[message] = free[link] + delay
+            done.add(name)
+            left.remove(name)
+            listed.append((name, now))
+        return listed
+
+
+LINKS = {
+    "c": (400e3, 1.0),
+    "x": (52e3, 2.3),
+    "r": (52e3, 2.3),
+    "l": (52e3, 2.3),
+    "f": (60e3, 4.0),
+}
+
+
+def start_of(owners, matrix_id, sizes):
+    shared = jnp.int32(0)
+    for earlier_id in range(matrix_id):
+        shared = shared + jnp.where(owners[earlier_id] == owners[matrix_id], sizes[earlier_id], 0)
+    return shared
+
+
+def over_last(fn, value):
+    return fn(value, axis=-1, keepdims=True)
+
+
+def contract(left, right, left_dim, right_dim):
+    return lax.dot_general(
+        left, right, (((left_dim,), (right_dim,)), ((), ())), preferred_element_type=WIDE
+    )
+
+
+def gelu_parts(value):
+    scale = math.sqrt(2.0 / math.pi)
+    inner = jnp.tanh(scale * (value + 0.044715 * (value * value * value)))
+    return inner, scale * (1.0 + 3 * 0.044715 * value * value)
+
+
+def main_kernel(dims, refs):
+    units, features, hidden_width, heads, micros, sizes = dims
+    owners, docs, slopes, gain, bias, tok_hbm, cot_hbm, master_hbm = refs[:8]
+    mixed_hbm, grad_hbm, red, small = refs[8:12]
+    (
+        w, masters, mine, other, core_in, both, x_in, tok, cot, tail_in, wide_tok, wide_cot, x_pool, x_norm, x_att,
+        x_two, x_act, x_short, d_up, d_low, d_inner, d_res, d_qkv, d_pool, pooled, hat_one, hat_two, root_one, root_two,
+        resid, hidden, short_grad, res_grad, q_out, q_in, a_out, a_in, da_out, da_in, dq_out, dq_in, probs, mixed, grad,
+        wide_up, wide_grad, edge_in, g, right_in, left_in, fin_out, fin_in, co_out, co_in, sums, sums_in, sends, recvs, local,
+    ) = refs[12:]
+    half = features // 2
+    width = features // heads
+    rows_of = masters.shape[1]
+    count = heads
+    tokens = 3 * units
+    own = micros * units
+    pair_width = 2 * width
+    b, s = lax.axis_index("batch"), lax.axis_index("seq")
+    x, c = b // 2, b % 2
+    z, y = s // 2, s % 2
+    spot = y * (7 - 2 * z) + z
+
+    def seq_of(position):
+        far = position // 4
+        return 2 * (position + far * (7 - 2 * position)) + far
+
+    def at(offset):
+        return lax.rem(spot + offset + 2 * count, count)
+
+    def rows_at(offset, part=0, length=rows_of):
+        return pl.ds(pl.multiple_of(seq_of(at(offset)) * rows_of + part, 16), length)
+
+    my_half = pl.ds(pl.multiple_of(c * half, half), half)
+    other_half = pl.ds(pl.multiple_of((1 - c) * half, half), half)
+    core_peer = (x * 2 + 1 - c, s)
+    x_peer = ((1 - x) * 2 + c, s)
+    right_peer = (b, seq_of(at(1)))
+    left_peer = (b, seq_of(at(-1)))
+    plan = Plan()
+    flying = {}
+
+    def send(name, source, target, device):
+        index = len(flying)
+        flying[name] = pltpu.make_async_remote_copy(
+            src_ref=source,
+            dst_ref=target,
+            send_sem=sends.at[index],
+            recv_sem=recvs.at[index],
+            device_id=device,
+            device_id_type=MESH,
+        )
+        flying[name].start()
+
+    def nothing():
+        pass
+
+    loads = [
+        pltpu.make_async_copy(master_hbm, masters, local.at[0]),
+        pltpu.make_async_copy(tok_hbm, tok, local.at[1]),
+        pltpu.make_async_copy(cot_hbm, cot, local.at[2]),
+    ]
+    for copy in loads:
+        copy.start()
+    barrier = pltpu.get_barrier_semaphore()
+    for step in range(1, count):
+        pl.semaphore_signal(
+            barrier, inc=1, device_id=(b, lax.rem(s + step, count)), device_id_type=MESH
+        )
+    for device in (core_peer, x_peer):
+        pl.semaphore_signal(barrier, inc=1, device_id=device, device_id_type=MESH)
+    pl.semaphore_wait(barrier, count + 1)
+
+    chunks, first = [], 0
+    for size in sizes:
+        chunks.append((first, first + size))
+        first += size
+    gather_order = (0, 1, 2, 3, 5, 4)
+    plan.add("ms", loads[0].wait, cost=0.5)
+
+    def contribute(k):
+        def run():
+            lo, hi = chunks[k]
+            mask = (owners[k] == b).astype(WIDE)
+            begin = start_of(owners, k, sizes)
+            for block in range(lo, hi):
+                slot = jnp.minimum(begin + (block - lo), masters.shape[0] - 1)
+                mine[block] = (masters[slot, :, my_half] * mask).astype(LOW)
+                other[block] = (masters[slot, :, other_half] * mask).astype(LOW)
+            send(("g0", k), other.at[lo:hi], core_in.at[lo:hi], core_peer)
+
+        return run
+
+    def join_cores(k):
+        def run():
+            lo, hi = chunks[k]
+            flying[("g0", k)].wait_recv()
+            both[lo:hi] = mine[lo:hi] + core_in[lo:hi]
+            send(("g1", k), both.at[lo:hi], x_in.at[lo:hi], x_peer)
+
+        return run
+
+    def piece(k, offset, part=0, length=rows_of):
+        lo, hi = chunks[k]
+        return w.at[lo:hi, c, rows_at(offset, part, length)]
+
+    def join_x(k):
+        def run():
+            lo, hi = chunks[k]
+            flying[("g1", k)].wait_recv()
+            w[lo:hi, c, rows_at(0)] = both[lo:hi] + x_in[lo:hi]
+            send(("R", 1, k), piece(k, 0), piece(k, 0), right_peer)
+            send(("L", 1, k), piece(k, 0), piece(k, 0), left_peer)
+
+        return run
+
+    def forward_piece(k, side, step):
+        def run():
+            flying[(side, step - 1, k)].wait_recv()
+            if step == 5:
+                return
+            offset = (1 - step) if side == "R" else (step - 1)
+            part = piece(k, offset)
+            if step == 4:
+                part = piece(k, offset, 0 if side == "R" else rows_of // 2, rows_of // 2)
+            send((side, step, k), part, part, right_peer if side == "R" else left_peer)
+
+        return run
+
+    def distribute(k):
+        def run():
+            lo, hi = chunks[k]
+            send(("D", k), w.at[lo:hi, c], w.at[lo:hi, c], core_peer)
+
+        return run
+
+    def arrive(*names):
+        def run():
+            for name in names:
+                flying[name].wait_recv()
+
+        return run
+
+    piece_bytes = rows_of * half * 2
+    for k in gather_order:
+        lo, hi = chunks[k]
+        load = (hi - lo) * piece_bytes
+        plan.add(
+            ("co", k), contribute(k), ["ms"], sends=[(("g0", k), "c", load)], cost=0.15 * (hi - lo)
+        )
+        plan.add(
+            ("cs", k), join_cores(k), [("co", k)], [("g0", k)], [(("g1", k), "x", load)], 0.05 * (hi - lo)
+        )
+        plan.add(
+            ("x", k), join_x(k), [("cs", k)], [("g1", k)],
+            [(("R", 1, k), "r", load), (("L", 1, k), "l", load)], 0.05 * (hi - lo),
+        )
+        for step in (2, 3, 4, 5):
+            for side, link in (("R", "r"), ("L", "l")):
+                out = [((side, step, k), link, load if step < 4 else load // 2)] if step < 5 else []
+                before = ("x", k) if step == 2 else (side, step - 1, "f", k)
+                plan.add(
+                    (side, step, "f", k), forward_piece(k, side, step), [before], [(side, step - 1, k)], out, 0.05
+                )
+        plan.add(
+            ("di", k), distribute(k), [("R", 5, "f", k), ("L", 5, "f", k)], sends=[(("D", k), "c", 8 * load)], cost=0.05
+        )
+        plan.add(("h", k), arrive(("D", k)), [("di", k)], [("D", k)], cost=0.02)
+
+    def exchange(name, buffer):
+        send(name, buffer.at[0:own], buffer.at[own : 2 * own], core_peer)
+
+    def shared(name, columns):
+        return (name, "c", own * columns * 2)
+
+    lead = 16
+    tiles = range(features // TILE)
+
+    def columns_at(tile, base=0):
+        return slice(base + tile * TILE, base + (tile + 1) * TILE)
+
+    def ends_of(micro):
+        ends = []
+        total = jnp.int32(0)
+        for index in range(docs.shape[1] - 1):
+            total = total + docs[micro, index]
+            ends.append(total)
+        return ends
+
+    def kept(micro):
+        ids = s * units + lax.broadcasted_iota(jnp.int32, (units, 1), 0)
+        starts = (ids == 0).astype(jnp.int32)
+        for end in ends_of(micro):
+            starts = starts | (ids == end).astype(jnp.int32)
+        return starts == 0
+
+    def load_tokens():
+        loads[1].wait()
+        send("tl", tok.at[:, tokens - lead :], tail_in, (b, lax.rem(s + 1, count)))
+        for micro in range(micros):
+            for tile in tiles:
+                wide_tok[micro, tile, lead:] = tok[micro, :, columns_at(tile)].astype(WIDE)
+
+    def load_cotangent():
+        loads[2].wait()
+        for micro in range(micros):
+            for tile in tiles:
+                wide_cot[micro, tile] = cot[micro, :, columns_at(tile)].astype(WIDE)
+                for r in range(3):
+                    d_up[micro * units : (micro + 1) * units, columns_at(tile, r * features)] = wide_cot[
+                        micro, tile, pl.ds(r, units, stride=3), :
+                    ].astype(LOW)
+        exchange("eu", d_up)
+
+    def make_pieces():
+        flying["tl"].wait_recv()
+        for micro in range(micros):
+            keep = kept(micro)
+            for tile in tiles:
+                wide_tok[micro, tile, :lead] = tail_in[micro, :, columns_at(tile)].astype(WIDE)
+                for r in range(3):
+                    part = wide_tok[micro, tile, pl.ds(lead - 2 + r, units, stride=3), :]
+                    if r < 2:
+                        part = jnp.where(keep, part, 0.0)
+                    x_pool[micro * units : (micro + 1) * units, columns_at(tile, r * features)] = part.astype(LOW)
+        exchange("ep", x_pool)
+
+    plan.add("tok", load_tokens, sends=[("tl", "f", 2 * lead * features * 2)], cost=0.3, rank=1)
+    plan.add(
+        "pc", make_pieces, ["tok"], ["tl"], [shared("ep", 3 * features)], 0.5, rank=1
+    )
+    plan.add("cot", load_cotangent, (), (), [shared("eu", 3 * features)], 0.5, rank=2)
+
+    def normal(value, which, hat, root):
+        centred = value - over_last(jnp.mean, value)
+        scale = lax.rsqrt(over_last(jnp.mean, centred * centred) + ln_eps)
+        unit = centred * scale
+        hat[...] = unit
+        root[...] = scale
+        return (unit * gain[which : which + 1, :] + bias[which : which + 1, :]).astype(LOW)
+
+    def both_halves(make):
+        return jnp.concatenate([make(0), make(1)], axis=1)
+
+    def pool():
+        def side(h):
+            total = None
+            for r in range(3):
+                term = contract(x_pool[0:own, r * features : (r + 1) * features], w[r, h], 1, 0)
+                total = term if total is None else total + term
+            return total
+
+        value = both_halves(side)
+        pooled[...] = value
+        x_norm[0:own] = normal(value, 0, hat_one, root_one)
+        exchange("en", x_norm)
+
+    lane = lambda: lax.broadcasted_iota(jnp.int32, (1, pair_width), 1)
+
+    def swap(value):
+        return pltpu.roll(value, width, axis=1)
+
+    def to_heads(tile, target, pair, row):
+        low_lanes = lane() < width
+        first, second = tile[:units], tile[units:]
+        target[2 * pair, row : row + units] = jnp.where(low_lanes, first, swap(second)).astype(LOW)
+        target[2 * pair + 1, row : row + units] = jnp.where(low_lanes, swap(first), second).astype(LOW)
+
+    def from_heads(source, pair, row):
+        low_lanes = lane() < width
+        even = source[2 * pair, row : row + units].astype(WIDE)
+        odd = source[2 * pair + 1, row : row + units].astype(WIDE)
+        return jnp.where(low_lanes, even, swap(odd)).astype(LOW), jnp.where(low_lanes, swap(even), odd).astype(LOW)
+
+    def spread(name, source, target):
+        for step in range(1, count):
+            there = lax.rem(s + step, count)
+            send((name, step), source.at[there], target.at[s], (b, there))
+        target[s] = source[s]
+
+    def spread_names(name):
+        return [(name, step) for step in range(1, count)]
+
+    def spread_sends(name, rows):
+        return [((name, step), "f", rows * pair_width * 2) for step in range(1, count)]
+
+    def project():
+        for part in range(3):
+            for h in range(2):
+                value = contract(x_norm[0:own], w[3 + part, h], 1, 0)
+                for tile in range(half // pair_width):
+                    to_heads(
+                        value[:, tile * pair_width : (tile + 1) * pair_width],
+                        q_out,
+                        h * (half // pair_width) + tile,
+                        part * units,
+                    )
+        spread("q", q_out, q_in)
+
+    lane_units = units * count
+
+    def heads_of(source, part):
+        return source[:, part * units : (part + 1) * units, :].reshape(lane_units, pair_width)
+
+    def lanes_of(micro):
+        return (lane() // width == micro).astype(WIDE).astype(LOW)
+
+    def distances():
+        row_ids = lax.broadcasted_iota(jnp.int32, (lane_units, lane_units), 0)
+        col_ids = lax.broadcasted_iota(jnp.int32, (lane_units, lane_units), 1)
+        return row_ids - col_ids
+
+    def attend_now():
+        arrive(*spread_names("q"))()
+        queries, keys, values = (heads_of(q_in, part) for part in range(3))
+        slope = slopes[s]
+        total = None
+        for micro in range(micros):
+            gap = distances()
+            row_seg = jnp.zeros((lane_units, 1), jnp.int32)
+            col_seg = jnp.zeros((1, lane_units), jnp.int32)
+            for end in ends_of(micro):
+                row_seg += (lax.broadcasted_iota(jnp.int32, (lane_units, 1), 0) >= end).astype(jnp.int32)
+                col_seg += (lax.broadcasted_iota(jnp.int32, (1, lane_units), 1) >= end).astype(jnp.int32)
+            allowed = (row_seg == col_seg) & (gap >= 0)
+            mask = lanes_of(micro)
+            raw = contract(queries * mask, keys, 1, 1) * 0.125 - slope * gap.astype(WIDE)
+            scores = jnp.where(allowed, raw, masked_score)
+            raised = jnp.exp(scores - over_last(jnp.max, scores))
+            probability = raised / over_last(jnp.sum, raised)
+            probs[micro] = probability
+            term = contract(probability.astype(LOW), values * mask, 1, 0)
+            total = term if total is None else total + term
+        a_out[...] = total.astype(LOW).reshape(count, units, pair_width)
+        spread("a", a_out, a_in)
+
+    def merge():
+        arrive(*spread_names("a"))()
+        for pair in range(heads // 2):
+            columns = slice(pair * pair_width, (pair + 1) * pair_width)
+            first, second = from_heads(a_in, pair, 0)
+            x_att[0:units, columns] = first
+            x_att[units:own, columns] = second
+        exchange("ea", x_att)
+
+    def project_out():
+        value = pooled[...] + both_halves(lambda h: contract(x_att[0:own], w[6, h], 1, 0))
+        resid[...] = value
+        x_two[0:own] = normal(value, 1, hat_two, root_two)
+        exchange("et", x_two)
+
+    hidden_blocks = hidden_width // features
+    in_base = 7
+    back_base = in_base + hidden_blocks
+    up_base = back_base + hidden_blocks
+
+    def widen(j):
+        def run():
+            for h in range(2):
+                columns = slice(j * features + h * half, j * features + (h + 1) * half)
+                value = contract(x_two[0:own], w[in_base + j, h], 1, 0)
+                hidden[:, columns] = value
+                inner, _ = gelu_parts(value)
+                x_act[0:own, columns] = (0.5 * value * (1.0 + inner)).astype(LOW)
+            if j == hidden_blocks - 1:
+                exchange("ec", x_act)
+
+        return run
+
+    def narrow():
+        def side(h):
+            total = resid[:, h * half : (h + 1) * half]
+            for j in range(hidden_blocks):
+                total = total + contract(
+                    x_act[0:own, j * features : (j + 1) * features], w[back_base + j, h], 1, 0
+                )
+            return total
+
+        x_short[0:own] = both_halves(side).astype(LOW)
+        exchange("es", x_short)
+
+    outs = [
+        pltpu.make_async_copy(mixed, mixed_hbm, local.at[3]),
+        pltpu.make_async_copy(grad, grad_hbm, local.at[4]),
+    ]
+
+    def lift(r):
+        def run():
+            for h in range(2):
+                value = contract(x_short[0:own], w[up_base + r, h], 1, 0)
+                for micro in range(micros):
+                    for tile in range(half // TILE):
+                        wide_up[micro, h * (half // TILE) + tile, pl.ds(r, units, stride=3), :] = value[
+                            micro * units : (micro + 1) * units, columns_at(tile)
+                        ]
+            if r == 2:
+                for micro in range(micros):
+                    for tile in tiles:
+                        columns = columns_at(tile)
+                        mixed[micro, :, columns] = tok[micro, :, columns].astype(WIDE) + wide_up[micro, tile]
+                outs[0].start()
+
+        return run
+
+    plan.add("po", pool, ["pc", ("h", 0)], (), [shared("en", features)], 1.0, rank=3)
+    plan.add("pr", project, ["po", ("h", 1)], (), spread_sends("q", 3 * units), 1.5, rank=3)
+    plan.add("at", attend_now, ["pr"], spread_names("q"), spread_sends("a", units), 3.0, rank=3)
+    plan.add("me", merge, ["at"], spread_names("a"), [shared("ea", features)], 0.3, rank=3)
+    plan.add("ou", project_out, ["me", ("h", 2)], (), [shared("et", features)], 0.6, rank=3)
+    for j in range(hidden_blocks):
+        last = j == hidden_blocks - 1
+        plan.add(
+            ("wi", j), widen(j), ["ou", ("h", 3)] + ([("wi", i) for i in range(j)] if last else []), (),
+            [shared("ec", hidden_width)] if last else (), 0.5, rank=3,
+        )
+    plan.add(
+        "na", narrow, [("wi", j) for j in range(hidden_blocks)] + [("h", 4)], (), [shared("es", features)], 1.0,
+        rank=3,
+    )
+    for r in range(3):
+        plan.add(
+            ("li", r), lift(r), ["na", ("h", 5), "tok"] + ([("li", i) for i in range(r)]), (), (), 0.4, rank=8
+        )
+
+    def back_short():
+        total = None
+        for r in range(3):
+            for h in range(2):
+                begin = r * features + h * half
+                term = contract(d_up[0:own, begin : begin + half], w[up_base + r, h], 1, 1)
+                total = term if total is None else total + term
+        short_grad[...] = total
+        d_low[0:own] = total.astype(LOW)
+        exchange("el", d_low)
+
+    def back_widen(j):
+        def run():
+            total = contract(d_low[0:own, 0:half], w[back_base + j, 0], 1, 1)
+            total = total + contract(d_low[0:own, half:features], w[back_base + j, 1], 1, 1)
+            columns = slice(j * features, (j + 1) * features)
+            value = hidden[:, columns]
+            inner, slope = gelu_parts(value)
+            factor = 0.5 * (1.0 + inner) + 0.5 * value * (1.0 - inner * inner) * slope
+            d_inner[0:own, columns] = (total * factor).astype(LOW)
+            if j == hidden_blocks - 1:
+                exchange("ei", d_inner)
+
+        return run
+
+    def back_normal(value, which, hat, root):
+        unit = hat[...]
+        sums[which : which + 1, :] = jnp.sum(value * unit, axis=0, keepdims=True)
+        sums[2 + which : 3 + which, :] = jnp.sum(value, axis=0, keepdims=True)
+        scaled = value * gain[which : which + 1, :]
+        return root[...] * (
+            scaled - over_last(jnp.mean, scaled) - unit * over_last(jnp.mean, scaled * unit)
+        )
+
+    def back_two():
+        total = None
+        for j in range(hidden_blocks):
+            for h in range(2):
+                begin = j * features + h * half
+                term = contract(d_inner[0:own, begin : begin + half], w[in_base + j, h], 1, 1)
+                total = term if total is None else total + term
+        value = short_grad[...] + back_normal(total, 1, hat_two, root_two)
+        res_grad[...] = value
+        d_res[0:own] = value.astype(LOW)
+        exchange("er", d_res)
+
+    def back_out():
+        value = contract(d_res[0:own, 0:half], w[6, 0], 1, 1)
+        value = value + contract(d_res[0:own, half:features], w[6, 1], 1, 1)
+        for pair in range(heads // 2):
+            to_heads(value[:, pair * pair_width : (pair + 1) * pair_width], da_out, pair, 0)
+        spread("da", da_out, da_in)
+
+    def back_attend():
+        arrive(*spread_names("da"))()
+        queries, keys, values = (heads_of(q_in, part) for part in range(3))
+        grads = da_in[...].reshape(lane_units, pair_width)
+        totals = [None, None, None]
+        slope_total = jnp.zeros((1, 1), WIDE)
+        for micro in range(micros):
+            mask = lanes_of(micro)
+            own_grads = grads * mask
+            probability = probs[micro]
+            grad_prob = contract(own_grads, values, 1, 1)
+            scaled = probability * grad_prob
+            score = scaled - probability * over_last(jnp.sum, scaled)
+            low_score = score.astype(LOW)
+            gap = distances().astype(WIDE)
+            slope_total = slope_total - jnp.sum(
+                jnp.sum(low_score.astype(WIDE) * gap, axis=0, keepdims=True), axis=1, keepdims=True
+            )
+            terms = (
+                contract(low_score, keys * mask, 1, 0) * 0.125,
+                contract(low_score, queries * mask, 0, 0) * 0.125,
+                contract(probability.astype(LOW), own_grads, 0, 0),
+            )
+            totals = [term if total is None else total + term for total, term in zip(totals, terms)]
+        for part in range(3):
+            dq_out[:, part * units : (part + 1) * units, :] = (
+                totals[part].astype(LOW).reshape(count, units, pair_width)
+            )
+        spread("dq", dq_out, dq_in)
+        places = lax.broadcasted_iota(jnp.int32, (1, features), 1)
+        sums[4:5, :] = jnp.where(places == s, slope_total, 0.0)
+        sums[5:8, :] = jnp.zeros((3, features), WIDE)
+
+    def back_project():
+        arrive(*spread_names("dq"))()
+        for part in range(3):
+            for pair in range(heads // 2):
+                begin = part * features + pair * pair_width
+                first, second = from_heads(dq_in, pair, part * units)
+                d_qkv[0:units, begin : begin + pair_width] = first
+                d_qkv[units:own, begin : begin + pair_width] = second
+        exchange("eq", d_qkv)
+
+    def back_one():
+        total = None
+        for part in range(3):
+            for h in range(2):
+                begin = part * features + h * half
+                term = contract(d_qkv[0:own, begin : begin + half], w[3 + part, h], 1, 1)
+                total = term if total is None else total + term
+        value = res_grad[...] + back_normal(total, 0, hat_one, root_one)
+        d_pool[0:own] = value.astype(LOW)
+        exchange("ed1", d_pool)
+
+    def back_pieces():
+        for r in range(3):
+            value = contract(d_pool[0:own, 0:half], w[r, 0], 1, 1)
+            value = value + contract(d_pool[0:own, half:features], w[r, 1], 1, 1)
+            for micro in range(micros):
+                part = value[micro * units : (micro + 1) * units]
+                if r < 2:
+                    part = jnp.where(kept(micro), part, 0.0)
+                for tile in tiles:
+                    wide_grad[micro, tile, pl.ds(6 + r, units, stride=3), :] = part[:, columns_at(tile)]
+        send("ed", wide_grad.at[:, :, 0:8], edge_in, (b, lax.rem(s + count - 1, count)))
+
+    def finish_grad():
+        flying["ed"].wait_recv()
+        inside = (s < count - 1).astype(WIDE)
+        for micro in range(micros):
+            for tile in tiles:
+                columns = columns_at(tile)
+                wide_grad[micro, tile, 6 + tokens : 8 + tokens, :] = edge_in[micro, tile, 6:8, :] * inside
+                grad[micro, :, columns] = cot[micro, :, columns].astype(WIDE) + wide_grad[micro, tile, 8 : 8 + tokens]
+        outs[1].start()
+
+    plan.add("bs", back_short, ["cot", ("h", 5)], (), [shared("el", features)], 1.0, rank=4)
+    for j in range(hidden_blocks):
+        last = j == hidden_blocks - 1
+        plan.add(
+            ("bw", j), back_widen(j),
+            ["bs", ("h", 4), ("wi", j)] + ([("bw", i) for i in range(j)] if last else []), (),
+            [shared("ei", hidden_width)] if last else (), 0.5, rank=4,
+        )
+    plan.add(
+        "b2", back_two, [("bw", j) for j in range(hidden_blocks)] + [("h", 3)], (),
+        [shared("er", features)], 1.2, rank=4,
+    )
+    plan.add("bo", back_out, ["b2", ("h", 2)], (), spread_sends("da", units), 0.6, rank=4)
+    plan.add("ba", back_attend, ["bo", "at"], spread_names("da"), spread_sends("dq", 3 * units), 4.0, rank=4)
+    plan.add("bp", back_project, ["ba"], spread_names("dq"), [shared("eq", 3 * features)], 0.5, rank=4)
+    plan.add("b1", back_one, ["bp"], (), [shared("ed1", features)], 1.2, rank=4)
+    plan.add("bx", back_pieces, ["b1"], (), [("ed", "f", 2 * 8 * features * 4)], 1.0, rank=9)
+    plan.add("fg", finish_grad, ["bx", "cot"], ["ed"], (), 0.3, rank=9)
+
+    def add_pair(step, device):
+        def run():
+            if step > 0:
+                flying[("s", step - 1)].wait_recv()
+                sums[8 * step : 8 * step + 8] = sums[8 * step - 8 : 8 * step] + sums_in[8 * step - 8 : 8 * step]
+            if device is not None:
+                send(("s", step), sums.at[8 * step : 8 * step + 8], sums_in.at[8 * step : 8 * step + 8], device)
+            else:
+                small[...] = sums[8 * step : 8 * step + 8]
+
+        return run
+
+    partners = [
+        core_peer,
+        x_peer,
+        (b, 2 * z + 1 - y),
+        (b, 2 * (z + 1 - 2 * (z % 2)) + y),
+        (b, 2 * lax.rem(z + 2, 4) + y),
+        None,
+    ]
+    for step, device in enumerate(partners):
+        plan.add(
+            ("sum", step), add_pair(step, device), ["b1", "ba"] if step == 0 else [("sum", step - 1)],
+            [("s", step - 1)] if step else (), [(("s", step), "f", 8 * features * 4)] if device is not None else (), 0.1,
+            rank=0,
+        )
+
+    for name, columns in (
+        ("ep", "pc"), ("en", "po"), ("ea", "me"), ("et", "ou"), ("ec", ("wi", hidden_blocks - 1)),
+        ("es", "na"), ("eu", "cot"), ("el", "bs"), ("ei", ("bw", hidden_blocks - 1)),
+        ("er", "b2"), ("eq", "bp"), ("ed1", "b1"),
+    ):
+        plan.add(("got", name), arrive(name), [columns], [name], cost=0.02)
+
+    def columns_of(block):
+        return pl.ds(pl.multiple_of(block * features + c * half, half), half)
+
+    def outer(block, left, left_block, right, right_block):
+        def run():
+            rows = left[:, left_block * features : (left_block + 1) * features]
+            g[block] = contract(rows, right[:, columns_of(right_block)], 0, 0).astype(LOW)
+
+        return run
+
+    weight_grads = []
+    for r in range(3):
+        weight_grads.append((r, x_pool, r, d_pool, 0, [("got", "ep"), ("got", "ed1")]))
+        weight_grads.append((3 + r, x_norm, 0, d_qkv, r, [("got", "en"), ("got", "eq")]))
+        weight_grads.append((up_base + r, x_short, 0, d_up, r, [("got", "es"), ("got", "eu")]))
+    weight_grads.append((6, x_att, 0, d_res, 0, [("got", "ea"), ("got", "er")]))
+    for j in range(hidden_blocks):
+        weight_grads.append((in_base + j, x_two, 0, d_inner, j, [("got", "et"), ("got", "ei")]))
+        weight_grads.append((back_base + j, x_act, j, d_low, 0, [("got", "ec"), ("got", "el")]))
+    for block, left, left_block, right, right_block, deps in weight_grads:
+        plan.add(("gr", block), outer(block, left, left_block, right, right_block), deps, cost=0.5, rank=5)
+
+    def first_step(k, side):
+        def run():
+            lo, hi = chunks[k]
+            part = 0 if side == "R" else rows_of // 2
+            source = g.at[lo:hi, rows_at(4, part, rows_of // 2)]
+            inbox = right_in if side == "R" else left_in
+            send(
+                (side, "s", 1, k), source, inbox.at[0, lo:hi, part : part + rows_of // 2],
+                right_peer if side == "R" else left_peer,
+            )
+
+        return run
+
+    def next_step(k, side, step):
+        def run():
+            lo, hi = chunks[k]
+            inbox = right_in if side == "R" else left_in
+            offset = (5 - step) if side == "R" else (step - 5)
+            flying[(side, "s", step - 1, k)].wait_recv()
+            part, length = 0, rows_of
+            if step == 2:
+                part, length = (0 if side == "R" else rows_of // 2), rows_of // 2
+            rows = rows_at(offset, part, length)
+            g[lo:hi, rows] = g[lo:hi, rows] + inbox[step - 2, lo:hi, part : part + length]
+            send(
+                (side, "s", step, k), g.at[lo:hi, rows_at(offset)], inbox.at[step - 1, lo:hi],
+                right_peer if side == "R" else left_peer,
+            )
+
+        return run
+
+    def finish(k):
+        def run():
+            lo, hi = chunks[k]
+            flying[("R", "s", 4, k)].wait_recv()
+            flying[("L", "s", 4, k)].wait_recv()
+            total = g[lo:hi, rows_at(0)].astype(WIDE) + right_in[3, lo:hi].astype(WIDE) + left_in[3, lo:hi].astype(WIDE)
+            fin_out[lo:hi] = total.astype(LOW)
+            send(("rx", k), fin_out.at[lo:hi], fin_in.at[lo:hi], x_peer)
+
+        return run
+
+    def finish_x(k):
+        def run():
+            lo, hi = chunks[k]
+            flying[("rx", k)].wait_recv()
+            total = (fin_out[lo:hi].astype(WIDE) + fin_in[lo:hi].astype(WIDE)).astype(LOW)
+            co_out[lo:hi] = total
+            red[lo:hi, :, my_half] = total
+            send(("rc", k), co_out.at[lo:hi], co_in.at[lo:hi], core_peer)
+
+        return run
+
+    def finish_core(k):
+        def run():
+            lo, hi = chunks[k]
+            flying[("rc", k)].wait_recv()
+            red[lo:hi, :, other_half] = co_in[lo:hi]
+
+        return run
+
+    for k in (5, 4, 3, 2, 1, 0):
+        lo, hi = chunks[k]
+        load = (hi - lo) * piece_bytes
+        for side, link in (("R", "r"), ("L", "l")):
+            plan.add(
+                (side, "r", 1, k), first_step(k, side), [("gr", block) for block in range(lo, hi)], (),
+                [((side, "s", 1, k), link, load // 2)], 0.05,
+            )
+        for step in (2, 3, 4):
+            for side, link in (("R", "r"), ("L", "l")):
+                plan.add(
+                    (side, "r", step, k), next_step(k, side, step), [(side, "r", step - 1, k)], [(side, "s", step - 1, k)],
+                    [((side, "s", step, k), link, load)], 0.05 * (hi - lo),
+                )
+        plan.add(
+            ("fi", k), finish(k), [("R", "r", 4, k), ("L", "r", 4, k)], [("R", "s", 4, k), ("L", "s", 4, k)], [(("rx", k), "x", load)],
+            0.05 * (hi - lo),
+        )
+        plan.add(
+            ("fx", k), finish_x(k), [("fi", k)], [("rx", k)], [(("rc", k), "c", load)], 0.05 * (hi - lo)
+        )
+        plan.add(("fc", k), finish_core(k), [("fx", k)], [("rc", k)], (), 0.03 * (hi - lo))
+
+    for name, _ in plan.order():
+        plan.tasks[name][0]()
+    for name, copy in flying.items():
+        copy.wait_send()
+    for copy in outs:
+        copy.wait()
+
+
+def adam_kernel(sizes, refs):
+    owners, red, small, norm, norm_m, norm_v, slope, slope_m, slope_v, master, first, second, mixed, grad = refs[:14]
+    (
+        new_w, new_m, new_v, new_low, norm_out, norm_m_out, norm_v_out, slope_out, slope_m_out, slope_v_out, mixed_out,
+        grad_out, sems,
+    ) = refs[14:]
+    step = pl.program_id(0)
+    copies = [
+        pltpu.make_async_copy(mixed, mixed_out, sems.at[0]),
+        pltpu.make_async_copy(grad, grad_out, sems.at[1]),
+    ]
+    fix_first = 1.0 - beta_one**STEP
+    fix_second = 1.0 - beta_two**STEP
+
+    @pl.when(step == 0)
+    def _():
+        for copy in copies:
+            copy.start()
+        norm_out[...], norm_m_out[...], norm_v_out[...] = adam_update(
+            norm[...], small[0:4], norm_m[...], norm_v[...], fix_first, fix_second, rate_norm, 0.0
+        )
+        heads = slope.shape[1]
+        slope_out[...], slope_m_out[...], slope_v_out[...] = adam_update(
+            slope[...], small[4:5, 0:heads], slope_m[...], slope_v[...], fix_first, fix_second, rate_slope, 0.0
+        )
+
+    me = lax.axis_index("batch")
+    block, held, base = jnp.int32(0), jnp.int32(0), 0
+    for matrix_id, size in enumerate(sizes):
+        begin = start_of(owners, matrix_id, sizes)
+        inside = (owners[matrix_id] == me) & (step >= begin) & (step < begin + size)
+        block = jnp.where(inside, base + step - begin, block)
+        held = jnp.where(inside, 1, held)
+        base += size
+    gradient = red[block].astype(WIDE)
+    values = adam_update(
+        master[0], gradient, first[0], second[0], fix_first, fix_second, rate_matrix, decay_rate
+    )
+    keep = jnp.full(gradient.shape, held, jnp.int32) > 0
+    weight = jnp.where(keep, values[0], master[0])
+    new_w[0] = weight
+    new_m[0] = jnp.where(keep, values[1], first[0])
+    new_v[0] = jnp.where(keep, values[2], second[0])
+    new_low[0] = weight.astype(LOW)
+
+    @pl.when(step == pl.num_programs(0) - 1)
+    def _():
+        for copy in copies:
+            copy.wait()
+
+
+def fused_body(tokens, cotangent, doc_lengths, owners, master, first_moment, second_moment, ln_gain, ln_bias, norm_m, norm_v, slopes, slope_m, slope_v):
+    micros, _, tok_rows, features = tokens.shape
+    units, heads, width = tok_rows // 3, slopes.shape[0], features // slopes.shape[0]
+    sizes = tuple(block_counts(features, FF))
+    blocks, own, half = sum(sizes), micros * units, features // 2
+    slots, rows = master.shape[1], master.shape[2]
+    lane_units = units * heads
+    split = features // TILE
+    hbm, vmem, smem = (pl.BlockSpec(memory_space=m) for m in (pl.ANY, pltpu.VMEM, pltpu.SMEM))
+    low = lambda *shape: pltpu.VMEM(shape, LOW)
+    wide = lambda *shape: pltpu.VMEM(shape, WIDE)
+    pieces = lambda: low(blocks, rows, half)
+    both = lambda columns: low(2 * own, columns)
+    scratch = [
+        low(blocks, 2, features, half), wide(slots, rows, features), pieces(), pieces(), pieces(), pieces(), pieces(),
+        low(micros, tok_rows, features), low(micros, tok_rows, features), low(micros, 16, features),
+        wide(micros, split, 16 + tok_rows, TILE), wide(micros, split, tok_rows, TILE),
+        both(3 * features), both(features), both(features), both(features), both(FF), both(features),
+        both(3 * features), both(features), both(FF), both(features), both(3 * features), both(features),
+        wide(own, features), wide(own, features), wide(own, features), wide(own, 1), wide(own, 1),
+        wide(own, features), wide(own, FF), wide(own, features), wide(own, features),
+        low(heads, 3 * units, 2 * width), low(heads, 3 * units, 2 * width), low(heads, units, 2 * width),
+        low(heads, units, 2 * width), low(heads, units, 2 * width), low(heads, units, 2 * width),
+        low(heads, 3 * units, 2 * width), low(heads, 3 * units, 2 * width),
+        wide(micros, lane_units, lane_units), wide(micros, tok_rows, features), wide(micros, tok_rows, features),
+        wide(micros, split, tok_rows, TILE), wide(micros, split, 8 + tok_rows, TILE), wide(micros, split, 8, TILE), low(blocks, features, half), low(4, blocks, rows, half), low(4, blocks, rows, half),
+        pieces(), pieces(), pieces(), pieces(), wide(48, features), wide(40, features),
+        pltpu.SemaphoreType.DMA((200,)), pltpu.SemaphoreType.DMA((200,)), pltpu.SemaphoreType.DMA((5,)),
+    ]
+    token_shape = (micros, tok_rows, features)
+    dims = (units, features, FF, heads, micros, sizes)
+    mixed, grad, red, small = pl.pallas_call(
+        lambda *refs: main_kernel(dims, refs),
+        out_shape=(
+            jax.ShapeDtypeStruct(token_shape, WIDE),
+            jax.ShapeDtypeStruct(token_shape, WIDE),
+            jax.ShapeDtypeStruct((blocks, rows, features), LOW),
+            jax.ShapeDtypeStruct((8, features), WIDE),
+        ),
+        in_specs=[smem, smem, smem, vmem, vmem, hbm, hbm, hbm],
+        out_specs=(hbm, hbm, vmem, vmem),
+        scratch_shapes=scratch,
+        compiler_params=pltpu.CompilerParams(
+            collective_id=0, has_side_effects=True, vmem_limit_bytes=60 * 2**20
+        ),
+        name="block",
+    )(
+        owners, doc_lengths[:, 0], slopes, ln_gain, ln_bias, tokens[:, 0], cotangent[:, 0], master[0]
+    )
+    slot = pl.BlockSpec((1, rows, features), lambda j: (j, 0, 0))
+    moment_shape = jax.ShapeDtypeStruct((slots, rows, features), WIDE)
+    norm_shape = jax.ShapeDtypeStruct((4, features), WIDE)
+    slope_shape = jax.ShapeDtypeStruct((1, heads), WIDE)
+    out = pl.pallas_call(
+        lambda *refs: adam_kernel(sizes, refs),
+        grid=(slots,),
+        out_shape=(
+            moment_shape, moment_shape, moment_shape, jax.ShapeDtypeStruct((slots, rows, features), LOW),
+            norm_shape, norm_shape, norm_shape, slope_shape, slope_shape, slope_shape,
+            jax.ShapeDtypeStruct(token_shape, WIDE), jax.ShapeDtypeStruct(token_shape, WIDE),
+        ),
+        in_specs=[smem] + [vmem] * 8 + [slot] * 3 + [hbm] * 2,
+        out_specs=(slot, slot, slot, slot, vmem, vmem, vmem, vmem, vmem, vmem, hbm, hbm),
+        scratch_shapes=[pltpu.SemaphoreType.DMA((2,))],
+        compiler_params=pltpu.CompilerParams(dimension_semantics=("arbitrary",)),
+        name="adam",
+    )(
+        owners, red, small, jnp.concatenate([ln_gain, ln_bias], 0), norm_m, norm_v, slopes[None], slope_m[None],
+        slope_v[None], master[0], first_moment[0], second_moment[0], mixed, grad,
+    )
+    new_w, new_m, new_v, new_low, norm, norm_m, norm_v, slope, slope_m, slope_v, mixed, grad = out
+    return (
+        mixed[:, None], grad[:, None], new_w[None], new_m[None], new_v[None], new_low[None], norm, norm_m, norm_v,
+        slope[0], slope_m[0], slope_v[0],
+    )
+
+
+def fits(mesh, shapes):
+    return mesh.shape["batch"] == 4 and mesh.shape["seq"] == 8 and shapes[0].shape[1] == 1
+
+
 def solution(mesh):
     in_specs = (
         P("batch", None, "seq", None),
@@ -448,4 +1376,11 @@
         P(),
         P(),
     )
-    return jax.shard_map(body, mesh=mesh, in_specs=in_specs, out_specs=out_specs, check_vma=False)
+
+    def whole(*args):
+        part = fused_body if fits(mesh, args) else body
+        return jax.shard_map(
+            part, mesh=mesh, in_specs=in_specs, out_specs=out_specs, check_vma=False
+        )(*args)
+
+    return whole

time: 1120 us -> 183 us (0.16); the launches traced: 1110 us -> 183 us
  waiting for transfers between devices: 602 us -> 0 us
  local copies, waits for them, and re-layouts: 252 us -> 0 us
  Pallas kernels: 0 us -> 181 us
  blocking collectives: 78.4 us -> 0 us
  matrix products: 52.6 us -> 0 us
  between operations: 48.9 us -> 0.65 us
  starting transfers between devices: 39.9 us -> 0 us
  other arithmetic: 30.8 us -> 1.3 us
    reduce_scatter x1 -> x0, waiting for transfers between devices: 348 us -> none  [body(): lax.psum_scatter(all_blocks(summed, features), 'seq', scatter_dimension=1...]
    concatenate x4 -> x0, local copies, waits for them, and re-layouts: 185 us -> none  [the longest x1 184 us: all_blocks(): jnp.concatenate([to_blocks(matrices[matrix_id], row_kinds[matrix_id], fea...]
    pallas_call x0 -> x2, Pallas kernels: none -> 181 us  [the longest x1 142 us: fused_body(): pl.pallas_call(lambda *refs: main_kernel(dims, refs), out_shape=(jax.Shap...]
    all_gather x5 -> x0, waiting for transfers between devices: 126 us -> none  [body(): lax.all_gather(for_sending(tuple(fetched)), 'seq', axis=1, tiled=True)]
    psum x2 -> x0, waiting for transfers between devices: 105 us -> none  [the longest x1 63.5 us: body(): reduced_all = lax.psum(reduced, 'batch')]
    dot_general x49 -> x0, matrix products: 52.6 us -> none  [the longest x2 7.91 us: body(): jnp.dot(normed_two.T, grad_hidden, preferred_element_type=jnp.float32)]
    psum x1 -> x0, blocking collectives: 43.9 us -> none  [body(): lax.psum((jnp.concatenate([gain_grad, bias_grad], 0), jnp.where(head_pick...]
    all_to_all x8 -> x0, starting transfers between devices: 34.7 us -> none  [the longest x2 10.5 us: body(): lax.all_to_all(back_outbound, 'seq', split_axis=0, concat_axis=1, tiled=T...]
  transfers between devices with their start and end apart: 18 -> 0, of which waited for: 14 -> 0; matrix products, arithmetic and copies ran while one was open for 9% -> 0% of each run, Pallas kernels for 0% -> 0%
where the time goes in v2:
time: 183 us
  Pallas kernels  181 us (99%)
    pallas_call x1, Pallas kernels, fused_body(): pl.pallas_call(lambda *refs: main_kernel(dims, refs), out_shape=(jax.Shap...  142 us
    pallas_call x1, Pallas kernels, fused_body(): pl.pallas_call(lambda *refs: adam_kernel(sizes, refs), grid=(slots,), out...  39.4 us

profile of v2, /device:TPU:0, one launch (start us, length us, event | category | flops | bytes accessed | tf_op | source)
XLA Modules:
  0.0 182.9 jit_solution(6399610646115999507)
XLA Ops:
  0.6 1.3 pad_maximum_fusion.refs_3_
  1.9 141.6 %block.1 = (f32[2,144,512]{2,1,0:T(8,128)}, f32[2,144,512]{2,1,0:T(8,128)}, bf16[18,64,512]{2,1,0:T(8,128)(2,1)}, f32[8,512]{1,0:T(8,128)}) custom-call(s32[6]{0:T(128)} %refs_0_.3, s32[2,4]{1,0:T(2,128)} %bitcast.29, f32[8]{0:T(128)} %refs_2_.1, f32[2,512]{1,0:T(2,128)} %refs_3_.1, f32[2,512]{1,0:T(2,128)} %refs_4_.2, bf16[2,144,512]{2,1,0:T(8,128)(2,1)} %bitcast.26, ...), custom_call_target="tpu_custom_call" | custom-call | tf_op jit(solution)/shard_map/block/pallas_call | solution.py:1298
  143.5 39.4 %adam.1 = (f32[8,64,512]{2,1,0:T(8,128)}, f32[8,64,512]{2,1,0:T(8,128)}, f32[8,64,512]{2,1,0:T(8,128)}, bf16[8,64,512]{2,1,0:T(8,128)(2,1)}, f32[4,512]{1,0:T(4,...) custom-call(s32[6]{0:T(128)} %refs_0_.3, ...), custom_call_target="tpu_custom_call" | custom-call | tf_op jit(solution)/shard_map/adam/pallas_call | solution.py:1320

commit v3 on v2

--- a/solution.py
+++ b/solution.py
@@ -444,7 +444,7 @@
                 run, deps, waits, sends, cost, rank = self.tasks[name]
                 if any(d not in done for d in deps) or any(w not in arrival for w in waits):
                     continue
-                begin = max([now] + [arrival[w] for w in waits])
+                begin = max([now] + [arrival[w] for w in waits] + [free.get(m[1], 0.0) - SLACK for m in sends])
                 key = (begin, rank, place)
                 if best is None or key < best[0]:
                     best = (key, name)
@@ -462,6 +462,7 @@
         return listed
 
 
+SLACK = 1.5
 LINKS = {
     "c": (400e3, 1.0),
     "x": (52e3, 2.3),
@@ -502,7 +503,7 @@
         w, masters, mine, other, core_in, both, x_in, tok, cot, tail_in, wide_tok, wide_cot, x_pool, x_norm, x_att,
         x_two, x_act, x_short, d_up, d_low, d_inner, d_res, d_qkv, d_pool, pooled, hat_one, hat_two, root_one, root_two,
         resid, hidden, short_grad, res_grad, q_out, q_in, a_out, a_in, da_out, da_in, dq_out, dq_in, probs, mixed, grad,
-        wide_up, wide_grad, edge_in, g, right_in, left_in, fin_out, fin_in, co_out, co_in, sums, sums_in, sends, recvs, local,
+        wide_up, wide_grad, edge_in, x_near, x_wide, g, right_in, left_in, fin_out, fin_in, co_out, co_in, sums, sums_in, sends, recvs, local,
     ) = refs[12:]
     half = features // 2
     width = features // heads
@@ -566,16 +567,19 @@
         pl.semaphore_signal(barrier, inc=1, device_id=device, device_id_type=MESH)
     pl.semaphore_wait(barrier, count + 1)
 
-    chunks, first = [], 0
+    spans, first = [], 0
     for size in sizes:
-        chunks.append((first, first + size))
+        spans.append((first, first + size))
         first += size
-    gather_order = (0, 1, 2, 3, 5, 4)
+    in_base, back_base, up_base = spans[3][0], spans[4][0], spans[5][0]
+    hidden_blocks = sizes[3]
+    ours = in_base + x * hidden_blocks
+    theirs = in_base + (1 - x) * hidden_blocks
     plan.add("ms", loads[0].wait, cost=0.5)
 
     def contribute(k):
         def run():
-            lo, hi = chunks[k]
+            lo, hi = spans[k]
             mask = (owners[k] == b).astype(WIDE)
             begin = start_of(owners, k, sizes)
             for block in range(lo, hi):
@@ -588,46 +592,99 @@
 
     def join_cores(k):
         def run():
-            lo, hi = chunks[k]
+            lo, hi = spans[k]
             flying[("g0", k)].wait_recv()
             both[lo:hi] = mine[lo:hi] + core_in[lo:hi]
-            send(("g1", k), both.at[lo:hi], x_in.at[lo:hi], x_peer)
 
         return run
 
-    def piece(k, offset, part=0, length=rows_of):
-        lo, hi = chunks[k]
-        return w.at[lo:hi, c, rows_at(offset, part, length)]
-
-    def join_x(k):
-        def run():
-            lo, hi = chunks[k]
-            flying[("g1", k)].wait_recv()
-            w[lo:hi, c, rows_at(0)] = both[lo:hi] + x_in[lo:hi]
-            send(("R", 1, k), piece(k, 0), piece(k, 0), right_peer)
-            send(("L", 1, k), piece(k, 0), piece(k, 0), left_peer)
-
-        return run
-
-    def forward_piece(k, side, step):
-        def run():
-            flying[(side, step - 1, k)].wait_recv()
-            if step == 5:
-                return
-            offset = (1 - step) if side == "R" else (step - 1)
-            part = piece(k, offset)
-            if step == 4:
-                part = piece(k, offset, 0 if side == "R" else rows_of // 2, rows_of // 2)
-            send((side, step, k), part, part, right_peer if side == "R" else left_peer)
-
-        return run
-
-    def distribute(k):
-        def run():
-            lo, hi = chunks[k]
-            send(("D", k), w.at[lo:hi, c], w.at[lo:hi, c], core_peer)
-
-        return run
+    part = hidden_blocks // 2
+    gathers = [
+        ("p", (0,), spans[0][0], None, sizes[0]),
+        ("q", (1,), spans[1][0], None, sizes[1]),
+        ("F", (3, 4), ours, theirs, part),
+        ("G", (3, 4), ours + part, theirs + part, part),
+        ("o", (2,), spans[2][0], None, sizes[2]),
+        ("u", (5,), up_base, None, sizes[5]),
+    ]
+    piece_bytes = rows_of * half * 2
+
+    def gather_chunk(order, name, parents, here, there, size):
+        split = there is not None
+        load = size * piece_bytes
+        blocks = pl.ds(here, size)
+        away = pl.ds(there, size) if split else blocks
+
+        def piece(offset, part=0, length=rows_of):
+            return w.at[blocks, c, rows_at(offset, part, length)]
+
+        def join_here():
+            send(("g1", name), both.at[away], x_in.at[away], x_peer)
+
+        def join_x():
+            flying[("g1", name)].wait_recv()
+            w[blocks, c, rows_at(0)] = both[blocks] + x_in[blocks]
+            send(("R", 1, name), piece(0), piece(0), right_peer)
+            send(("L", 1, name), piece(0), piece(0), left_peer)
+
+        def onward(side, step):
+            def run():
+                flying[(side, step - 1, name)].wait_recv()
+                if step == 5:
+                    return
+                offset = (1 - step) if side == "R" else (step - 1)
+                part = piece(offset)
+                if step == 4:
+                    part = piece(offset, 0 if side == "R" else rows_of // 2, rows_of // 2)
+                send((side, step, name), part, part, right_peer if side == "R" else left_peer)
+
+            return run
+
+        def across(side, step):
+            def run():
+                offset = -step if side == "R" else step
+                part = piece(offset)
+                if step == 4:
+                    part = piece(offset, 0 if side == "R" else rows_of // 2, rows_of // 2)
+                send(("X", side, step, name), part, part, x_peer)
+
+            return run
+
+        def distribute(which, span):
+            def run():
+                send((which, name), w.at[span, c], w.at[span, c], core_peer)
+
+            return run
+
+        rank = order * 0.1
+        plan.add(("cx", name), join_here, [("cs", k) for k in parents], (), [(("g1", name), "x", load)], 0.05, rank)
+        plan.add(
+            ("x", name), join_x, [("cx", name)], [("g1", name)],
+            [(("R", 1, name), "r", load), (("L", 1, name), "l", load)], 0.05, rank,
+        )
+        crossing = []
+
+        def cross(side, step, after):
+            message = ("X", side, step, name)
+            plan.add(message, across(side, step), [after], (), [(message, "x", load if step < 4 else load // 2)], 0.05, rank + 0.05)
+            crossing.append(message)
+
+        if split:
+            cross("R", 0, ("x", name))
+        for step in (2, 3, 4, 5):
+            for side, link in (("R", "r"), ("L", "l")):
+                out = [((side, step, name), link, load if step < 4 else load // 2)] if step < 5 else []
+                before = ("x", name) if step == 2 else (side, step - 1, "f", name)
+                plan.add((side, step, "f", name), onward(side, step), [before], [(side, step - 1, name)], out, 0.05, rank)
+                if split:
+                    cross(side, step - 1, (side, step, "f", name))
+        ends = [("R", 5, "f", name), ("L", 5, "f", name)]
+        plan.add(("di", name), distribute("D", blocks), ends, (), [(("D", name), "c", 8 * load)], 0.05, rank)
+        plan.add(("h", name), arrive(("D", name)), [("di", name)], [("D", name)], (), 0.02, rank)
+        if split:
+            plan.add(("xw", name), arrive(*crossing), crossing, crossing, (), 0.05, rank)
+            plan.add(("dy", name), distribute("E", away), [("xw", name)], (), [(("E", name), "c", 8 * load)], 0.05, rank)
+            plan.add(("hy", name), arrive(("E", name)), [("dy", name)], [("E", name)], (), 0.02, rank)
 
     def arrive(*names):
         def run():
@@ -636,31 +693,13 @@
 
         return run
 
-    piece_bytes = rows_of * half * 2
-    for k in gather_order:
-        lo, hi = chunks[k]
+    for k in (0, 1, 3, 4, 2, 5):
+        lo, hi = spans[k]
         load = (hi - lo) * piece_bytes
-        plan.add(
-            ("co", k), contribute(k), ["ms"], sends=[(("g0", k), "c", load)], cost=0.15 * (hi - lo)
-        )
-        plan.add(
-            ("cs", k), join_cores(k), [("co", k)], [("g0", k)], [(("g1", k), "x", load)], 0.05 * (hi - lo)
-        )
-        plan.add(
-            ("x", k), join_x(k), [("cs", k)], [("g1", k)],
-            [(("R", 1, k), "r", load), (("L", 1, k), "l", load)], 0.05 * (hi - lo),
-        )
-        for step in (2, 3, 4, 5):
-            for side, link in (("R", "r"), ("L", "l")):
-                out = [((side, step, k), link, load if step < 4 else load // 2)] if step < 5 else []
-                before = ("x", k) if step == 2 else (side, step - 1, "f", k)
-                plan.add(
-                    (side, step, "f", k), forward_piece(k, side, step), [before], [(side, step - 1, k)], out, 0.05
-                )
-        plan.add(
-            ("di", k), distribute(k), [("R", 5, "f", k), ("L", 5, "f", k)], sends=[(("D", k), "c", 8 * load)], cost=0.05
-        )
-        plan.add(("h", k), arrive(("D", k)), [("di", k)], [("D", k)], cost=0.02)
+        plan.add(("co", k), contribute(k), ["ms"], (), [(("g0", k), "c", load)], 0.04 * (hi - lo), 0.1)
+        plan.add(("cs", k), join_cores(k), [("co", k)], [("g0", k)], (), 0.02 * (hi - lo), 0.1)
+    for order, chunk in enumerate(gathers):
+        gather_chunk(order, *chunk)
 
     def exchange(name, buffer):
         send(name, buffer.at[0:own], buffer.at[own : 2 * own], core_peer)
@@ -844,10 +883,6 @@
         x_two[0:own] = normal(value, 1, hat_two, root_two)
         exchange("et", x_two)
 
-    hidden_blocks = hidden_width // features
-    in_base = 7
-    back_base = in_base + hidden_blocks
-    up_base = back_base + hidden_blocks
 
     def widen(j):
         def run():
@@ -897,24 +932,24 @@
 
         return run
 
-    plan.add("po", pool, ["pc", ("h", 0)], (), [shared("en", features)], 1.0, rank=3)
-    plan.add("pr", project, ["po", ("h", 1)], (), spread_sends("q", 3 * units), 1.5, rank=3)
-    plan.add("at", attend_now, ["pr"], spread_names("q"), spread_sends("a", units), 3.0, rank=3)
-    plan.add("me", merge, ["at"], spread_names("a"), [shared("ea", features)], 0.3, rank=3)
-    plan.add("ou", project_out, ["me", ("h", 2)], (), [shared("et", features)], 0.6, rank=3)
+    plan.add("po", pool, ["pc", ("h", "p")], (), [shared("en", features)], 0.6, rank=3)
+    plan.add("pr", project, ["po", ("h", "q")], (), spread_sends("q", 3 * units), 0.6, rank=3)
+    plan.add("at", attend_now, ["pr"], spread_names("q"), spread_sends("a", units), 1.1, rank=3)
+    plan.add("me", merge, ["at"], spread_names("a"), [shared("ea", features)], 0.15, rank=3)
+    plan.add("ou", project_out, ["me", ("h", "o")], (), [shared("et", features)], 0.45, rank=3)
     for j in range(hidden_blocks):
         last = j == hidden_blocks - 1
         plan.add(
-            ("wi", j), widen(j), ["ou", ("h", 3)] + ([("wi", i) for i in range(j)] if last else []), (),
-            [shared("ec", hidden_width)] if last else (), 0.5, rank=3,
+            ("wi", j), widen(j), ["ou", ("h", "F"), ("hy", "F"), ("h", "G"), ("hy", "G")] + ([("wi", i) for i in range(j)] if last else []), (),
+            [shared("ec", hidden_width)] if last else (), 0.3, rank=3,
         )
     plan.add(
-        "na", narrow, [("wi", j) for j in range(hidden_blocks)] + [("h", 4)], (), [shared("es", features)], 1.0,
+        "na", narrow, [("wi", j) for j in range(hidden_blocks)] + [("h", "F"), ("hy", "F"), ("h", "G"), ("hy", "G")], (), [shared("es", features)], 0.5,
         rank=3,
     )
     for r in range(3):
         plan.add(
-            ("li", r), lift(r), ["na", ("h", 5), "tok"] + ([("li", i) for i in range(r)]), (), (), 0.4, rank=8
+            ("li", r), lift(r), ["na", ("h", "u"), "tok"] + ([("li", i) for i in range(r)]), (), (), 0.3, rank=8
         )
 
     def back_short():
@@ -1046,23 +1081,23 @@
                 grad[micro, :, columns] = cot[micro, :, columns].astype(WIDE) + wide_grad[micro, tile, 8 : 8 + tokens]
         outs[1].start()
 
-    plan.add("bs", back_short, ["cot", ("h", 5)], (), [shared("el", features)], 1.0, rank=4)
+    plan.add("bs", back_short, ["cot", ("h", "u")], (), [shared("el", features)], 0.65, rank=4)
     for j in range(hidden_blocks):
         last = j == hidden_blocks - 1
         plan.add(
             ("bw", j), back_widen(j),
-            ["bs", ("h", 4), ("wi", j)] + ([("bw", i) for i in range(j)] if last else []), (),
-            [shared("ei", hidden_width)] if last else (), 0.5, rank=4,
+            ["bs", ("h", "F"), ("hy", "F"), ("h", "G"), ("hy", "G"), ("wi", j)] + ([("bw", i) for i in range(j)] if last else []), (),
+            [shared("ei", hidden_width)] if last else (), 0.35, rank=4,
         )
     plan.add(
-        "b2", back_two, [("bw", j) for j in range(hidden_blocks)] + [("h", 3)], (),
-        [shared("er", features)], 1.2, rank=4,
-    )
-    plan.add("bo", back_out, ["b2", ("h", 2)], (), spread_sends("da", units), 0.6, rank=4)
-    plan.add("ba", back_attend, ["bo", "at"], spread_names("da"), spread_sends("dq", 3 * units), 4.0, rank=4)
-    plan.add("bp", back_project, ["ba"], spread_names("dq"), [shared("eq", 3 * features)], 0.5, rank=4)
-    plan.add("b1", back_one, ["bp"], (), [shared("ed1", features)], 1.2, rank=4)
-    plan.add("bx", back_pieces, ["b1"], (), [("ed", "f", 2 * 8 * features * 4)], 1.0, rank=9)
+        "b2", back_two, [("bw", j) for j in range(hidden_blocks)] + [("h", "F"), ("hy", "F"), ("h", "G"), ("hy", "G")], (),
+        [shared("er", features)], 0.9, rank=4,
+    )
+    plan.add("bo", back_out, ["b2", ("h", "o")], (), spread_sends("da", units), 0.45, rank=4)
+    plan.add("ba", back_attend, ["bo", "at"], spread_names("da"), spread_sends("dq", 3 * units), 1.4, rank=4)
+    plan.add("bp", back_project, ["ba"], spread_names("dq"), [shared("eq", 3 * features)], 0.2, rank=4)
+    plan.add("b1", back_one, ["bp"], (), [shared("ed1", features)], 0.75, rank=4)
+    plan.add("bx", back_pieces, ["b1"], (), [("ed", "f", 2 * 8 * features * 4)], 0.65, rank=9)
     plan.add("fg", finish_grad, ["bx", "cot"], ["ed"], (), 0.3, rank=9)
 
     def add_pair(step, device):
@@ -1109,101 +1144,172 @@
 
         return run
 
+    def send_either(name, first_source, second_source, target):
+        index = len(flying)
+        copies = [
+            pltpu.make_async_remote_copy(
+                src_ref=source, dst_ref=target, send_sem=sends.at[index], recv_sem=recvs.at[index], device_id=x_peer,
+                device_id_type=MESH,
+            )
+            for source in (first_source, second_source)
+        ]
+        flying[name] = copies[0]
+        for plane in range(2):
+            pl.when(x == plane)(copies[plane].start)
+
+    def near_away():
+        send_either("sn", d_low.at[0:own], x_two.at[0:own], x_near.at[0:own])
+
+    def near_core():
+        arrive("sn")()
+        exchange("cn", x_near)
+
+    def wide_away(j):
+        columns = slice(j * features, (j + 1) * features)
+
+        def run():
+            source = (x_act.at[0:own, columns], d_inner.at[0:own, columns])
+            send_either(("sw", j), *source, x_wide.at[0:own, columns])
+
+        return run
+
+    def wide_core(j):
+        columns = slice(j * features, (j + 1) * features)
+
+        def run():
+            arrive(("sw", j))()
+            send(("cw", j), x_wide.at[0:own, columns], x_wide.at[own : 2 * own, columns], core_peer)
+
+        return run
+
+    def outer_split(j):
+        columns = slice(j * features, (j + 1) * features)
+
+        def run():
+            @pl.when(x == 0)
+            def _():
+                total = contract(x_two[...], d_inner[:, columns_of(j)], 0, 0)
+                g[in_base + j] = (total + contract(x_near[...], x_wide[:, columns_of(j)], 0, 0)).astype(LOW)
+
+            @pl.when(x == 1)
+            def _():
+                total = contract(x_act[:, columns], d_low[:, my_half], 0, 0)
+                g[back_base + j] = (total + contract(x_wide[:, columns], x_near[:, my_half], 0, 0)).astype(LOW)
+
+        return run
+
+    lump = own * features * 2
+    plan.add("sn", near_away, ["bs", "ou"], (), [("sn", "x", lump)], 0.05, 2)
+    plan.add("nc", near_core, ["sn"], ["sn"], [("cn", "c", lump)], 0.05, 2)
+    plan.add(("got", "cn"), arrive("cn"), ["nc"], ["cn"], (), 0.02, 2)
+    for j in range(hidden_blocks):
+        plan.add(("sw", j), wide_away(j), [("wi", j), ("bw", j)], (), [(("sw", j), "x", lump)], 0.05, 2)
+        plan.add(("wc", j), wide_core(j), [("sw", j)], [("sw", j)], [(("cw", j), "c", lump)], 0.05, 2)
+        plan.add(("got", "cw", j), arrive(("cw", j)), [("wc", j)], [("cw", j)], (), 0.02, 2)
+        deps = [("got", e) for e in ("et", "ec", "el", "ei", "cn")] + [("got", "cw", j)]
+        plan.add(("gr", j, "s"), outer_split(j), deps, cost=0.6, rank=4.5)
     weight_grads = []
     for r in range(3):
         weight_grads.append((r, x_pool, r, d_pool, 0, [("got", "ep"), ("got", "ed1")]))
         weight_grads.append((3 + r, x_norm, 0, d_qkv, r, [("got", "en"), ("got", "eq")]))
         weight_grads.append((up_base + r, x_short, 0, d_up, r, [("got", "es"), ("got", "eu")]))
     weight_grads.append((6, x_att, 0, d_res, 0, [("got", "ea"), ("got", "er")]))
-    for j in range(hidden_blocks):
-        weight_grads.append((in_base + j, x_two, 0, d_inner, j, [("got", "et"), ("got", "ei")]))
-        weight_grads.append((back_base + j, x_act, j, d_low, 0, [("got", "ec"), ("got", "el")]))
     for block, left, left_block, right, right_block, deps in weight_grads:
-        plan.add(("gr", block), outer(block, left, left_block, right, right_block), deps, cost=0.5, rank=5)
-
-    def first_step(k, side):
-        def run():
-            lo, hi = chunks[k]
-            part = 0 if side == "R" else rows_of // 2
-            source = g.at[lo:hi, rows_at(4, part, rows_of // 2)]
-            inbox = right_in if side == "R" else left_in
-            send(
-                (side, "s", 1, k), source, inbox.at[0, lo:hi, part : part + rows_of // 2],
-                right_peer if side == "R" else left_peer,
-            )
-
-        return run
-
-    def next_step(k, side, step):
-        def run():
-            lo, hi = chunks[k]
-            inbox = right_in if side == "R" else left_in
-            offset = (5 - step) if side == "R" else (step - 5)
-            flying[(side, "s", step - 1, k)].wait_recv()
-            part, length = 0, rows_of
-            if step == 2:
-                part, length = (0 if side == "R" else rows_of // 2), rows_of // 2
-            rows = rows_at(offset, part, length)
-            g[lo:hi, rows] = g[lo:hi, rows] + inbox[step - 2, lo:hi, part : part + length]
-            send(
-                (side, "s", step, k), g.at[lo:hi, rows_at(offset)], inbox.at[step - 1, lo:hi],
-                right_peer if side == "R" else left_peer,
-            )
-
-        return run
-
-    def finish(k):
-        def run():
-            lo, hi = chunks[k]
-            flying[("R", "s", 4, k)].wait_recv()
-            flying[("L", "s", 4, k)].wait_recv()
-            total = g[lo:hi, rows_at(0)].astype(WIDE) + right_in[3, lo:hi].astype(WIDE) + left_in[3, lo:hi].astype(WIDE)
-            fin_out[lo:hi] = total.astype(LOW)
-            send(("rx", k), fin_out.at[lo:hi], fin_in.at[lo:hi], x_peer)
-
-        return run
-
-    def finish_x(k):
-        def run():
-            lo, hi = chunks[k]
-            flying[("rx", k)].wait_recv()
-            total = (fin_out[lo:hi].astype(WIDE) + fin_in[lo:hi].astype(WIDE)).astype(LOW)
-            co_out[lo:hi] = total
-            red[lo:hi, :, my_half] = total
-            send(("rc", k), co_out.at[lo:hi], co_in.at[lo:hi], core_peer)
-
-        return run
-
-    def finish_core(k):
-        def run():
-            lo, hi = chunks[k]
-            flying[("rc", k)].wait_recv()
-            red[lo:hi, :, other_half] = co_in[lo:hi]
-
-        return run
-
-    for k in (5, 4, 3, 2, 1, 0):
-        lo, hi = chunks[k]
-        load = (hi - lo) * piece_bytes
-        for side, link in (("R", "r"), ("L", "l")):
-            plan.add(
-                (side, "r", 1, k), first_step(k, side), [("gr", block) for block in range(lo, hi)], (),
-                [((side, "s", 1, k), link, load // 2)], 0.05,
-            )
+        plan.add(("gr", block), outer(block, left, left_block, right, right_block), deps, cost=0.3, rank=5)
+
+    def scatter_chunk(order, name, here, there, size, deps):
+        split = there is not None
+        blocks = pl.ds(here, size)
+        load = size * piece_bytes
+        rank = 1 + order * 0.1
+
+        def first_step(side):
+            def run():
+                part = 0 if side == "R" else rows_of // 2
+                inbox = right_in if side == "R" else left_in
+                send(
+                    (side, "s", 1, name), g.at[blocks, rows_at(4, part, rows_of // 2)],
+                    inbox.at[0, blocks, part : part + rows_of // 2], right_peer if side == "R" else left_peer,
+                )
+
+            return run
+
+        def next_step(side, step):
+            def run():
+                inbox = right_in if side == "R" else left_in
+                offset = (5 - step) if side == "R" else (step - 5)
+                flying[(side, "s", step - 1, name)].wait_recv()
+                part, length = 0, rows_of
+                if step == 2:
+                    part, length = (0 if side == "R" else rows_of // 2), rows_of // 2
+                rows = rows_at(offset, part, length)
+                g[blocks, rows] = g[blocks, rows] + inbox[step - 2, blocks, part : part + length]
+                send(
+                    (side, "s", step, name), g.at[blocks, rows_at(offset)], inbox.at[step - 1, blocks],
+                    right_peer if side == "R" else left_peer,
+                )
+
+            return run
+
+        def finish():
+            arrive(("R", "s", 4, name), ("L", "s", 4, name))()
+            total = g[blocks, rows_at(0)].astype(WIDE) + right_in[3, blocks].astype(WIDE) + left_in[3, blocks].astype(WIDE)
+            fin_out[blocks] = total.astype(LOW)
+            send(("rx", name), fin_out.at[blocks], fin_in.at[blocks], x_peer)
+            if split:
+                red[blocks, :, my_half] = fin_out[blocks]
+                send(("rc", name), fin_out.at[blocks], co_in.at[blocks], core_peer)
+
+        def finish_x():
+            arrive(("rx", name))()
+            if split:
+                away = pl.ds(there, size)
+                red[away, :, my_half] = fin_in[away]
+                send(("rd", name), fin_in.at[away], co_in.at[away], core_peer)
+            else:
+                total = (fin_out[blocks].astype(WIDE) + fin_in[blocks].astype(WIDE)).astype(LOW)
+                co_out[blocks] = total
+                red[blocks, :, my_half] = total
+                send(("rc", name), co_out.at[blocks], co_in.at[blocks], core_peer)
+
+        def finish_core():
+            arrive(("rc", name))()
+            red[blocks, :, other_half] = co_in[blocks]
+            if split:
+                arrive(("rd", name))()
+                away = pl.ds(there, size)
+                red[away, :, other_half] = co_in[away]
+
+        sides = (("R", "r"), ("L", "l"))
+        for side, link in sides:
+            plan.add((side, "r", 1, name), first_step(side), deps, (), [((side, "s", 1, name), link, load // 2)], 0.05, rank)
         for step in (2, 3, 4):
-            for side, link in (("R", "r"), ("L", "l")):
+            for side, link in sides:
                 plan.add(
-                    (side, "r", step, k), next_step(k, side, step), [(side, "r", step - 1, k)], [(side, "s", step - 1, k)],
-                    [((side, "s", step, k), link, load)], 0.05 * (hi - lo),
+                    (side, "r", step, name), next_step(side, step), [(side, "r", step - 1, name)],
+                    [(side, "s", step - 1, name)], [((side, "s", step, name), link, load)], 0.02 * size, rank,
                 )
+        own_out = [(("rc", name), "c", load)]
         plan.add(
-            ("fi", k), finish(k), [("R", "r", 4, k), ("L", "r", 4, k)], [("R", "s", 4, k), ("L", "s", 4, k)], [(("rx", k), "x", load)],
-            0.05 * (hi - lo),
-        )
+            ("fi", name), finish, [("R", "r", 4, name), ("L", "r", 4, name)], [("R", "s", 4, name), ("L", "s", 4, name)],
+            [(("rx", name), "x", load)] + (own_out if split else []), 0.02 * size, rank,
+        )
+        late_out = [(("rd", name), "c", load)] if split else own_out
+        plan.add(("fx", name), finish_x, [("fi", name)], [("rx", name)], late_out, 0.02 * size, rank)
         plan.add(
-            ("fx", k), finish_x(k), [("fi", k)], [("rx", k)], [(("rc", k), "c", load)], 0.05 * (hi - lo)
-        )
-        plan.add(("fc", k), finish_core(k), [("fx", k)], [("rc", k)], (), 0.03 * (hi - lo))
+            ("fc", name), finish_core, [("fx", name)], [("rc", name)] + ([("rd", name)] if split else []), (), 0.02 * size, rank
+        )
+
+    scatters = [("u", up_base, None, sizes[5], [("gr", up_base + r) for r in range(3)])]
+    scatters.append(("F", ours, theirs, part, [("gr", j, "s") for j in range(part)]))
+    scatters.append(("G", ours + part, theirs + part, part, [("gr", j, "s") for j in range(part, 2 * part)]))
+    scatters.append(("o", spans[2][0], None, 1, [("gr", spans[2][0])]))
+    for block in range(spans[1][0], spans[1][1]):
+        scatters.append((block, block, None, 1, [("gr", block)]))
+    for block in range(spans[0][0], spans[0][1]):
+        scatters.append((block, block, None, 1, [("gr", block)]))
+    for order, chunk in enumerate(scatters):
+        scatter_chunk(order, *chunk)
 
     for name, _ in plan.order():
         plan.tasks[name][0]()
@@ -1214,54 +1320,49 @@
 
 
 def adam_kernel(sizes, refs):
-    owners, red, small, norm, norm_m, norm_v, slope, slope_m, slope_v, master, first, second, mixed, grad = refs[:14]
+    owners, red, small, gain, bias, norm_m, norm_v, slope, slope_m, slope_v, master, first, second, mixed, grad = refs[:15]
     (
         new_w, new_m, new_v, new_low, norm_out, norm_m_out, norm_v_out, slope_out, slope_m_out, slope_v_out, mixed_out,
-        grad_out, sems,
-    ) = refs[14:]
+        grad_out,
+    ) = refs[15:]
     step = pl.program_id(0)
-    copies = [
-        pltpu.make_async_copy(mixed, mixed_out, sems.at[0]),
-        pltpu.make_async_copy(grad, grad_out, sems.at[1]),
-    ]
     fix_first = 1.0 - beta_one**STEP
     fix_second = 1.0 - beta_two**STEP
+    mixed_out[...] = mixed[...]
+    grad_out[...] = grad[...]
 
     @pl.when(step == 0)
     def _():
-        for copy in copies:
-            copy.start()
-        norm_out[...], norm_m_out[...], norm_v_out[...] = adam_update(
-            norm[...], small[0:4], norm_m[...], norm_v[...], fix_first, fix_second, rate_norm, 0.0
-        )
+        for begin, values in ((0, gain), (2, bias)):
+            rows = slice(begin, begin + 2)
+            norm_out[rows], norm_m_out[rows], norm_v_out[rows] = adam_update(
+                values[...], small[rows], norm_m[rows], norm_v[rows], fix_first, fix_second, rate_norm, 0.0
+            )
         heads = slope.shape[1]
         slope_out[...], slope_m_out[...], slope_v_out[...] = adam_update(
             slope[...], small[4:5, 0:heads], slope_m[...], slope_v[...], fix_first, fix_second, rate_slope, 0.0
         )
 
     me = lax.axis_index("batch")
-    block, held, base = jnp.int32(0), jnp.int32(0), 0
-    for matrix_id, size in enumerate(sizes):
-        begin = start_of(owners, matrix_id, sizes)
-        inside = (owners[matrix_id] == me) & (step >= begin) & (step < begin + size)
-        block = jnp.where(inside, base + step - begin, block)
-        held = jnp.where(inside, 1, held)
-        base += size
-    gradient = red[block].astype(WIDE)
-    values = adam_update(
-        master[0], gradient, first[0], second[0], fix_first, fix_second, rate_matrix, decay_rate
-    )
-    keep = jnp.full(gradient.shape, held, jnp.int32) > 0
-    weight = jnp.where(keep, values[0], master[0])
-    new_w[0] = weight
-    new_m[0] = jnp.where(keep, values[1], first[0])
-    new_v[0] = jnp.where(keep, values[2], second[0])
-    new_low[0] = weight.astype(LOW)
-
-    @pl.when(step == pl.num_programs(0) - 1)
-    def _():
-        for copy in copies:
-            copy.wait()
+    for place in range(master.shape[0]):
+        slot = step * master.shape[0] + place
+        block, held, base = jnp.int32(0), jnp.int32(0), 0
+        for matrix_id, size in enumerate(sizes):
+            begin = start_of(owners, matrix_id, sizes)
+            inside = (owners[matrix_id] == me) & (slot >= begin) & (slot < begin + size)
+            block = jnp.where(inside, base + slot - begin, block)
+            held = jnp.where(inside, 1, held)
+            base += size
+        gradient = red[block].astype(WIDE)
+        values = adam_update(
+            master[place], gradient, first[place], second[place], fix_first, fix_second, rate_matrix, decay_rate
+        )
+        keep = jnp.full(gradient.shape, held, jnp.int32) > 0
+        weight = jnp.where(keep, values[0], master[place])
+        new_w[place] = weight
+        new_m[place] = jnp.where(keep, values[1], first[place])
+        new_v[place] = jnp.where(keep, values[2], second[place])
+        new_low[place] = weight.astype(LOW)
 
 
 def fused_body(tokens, cotangent, doc_lengths, owners, master, first_moment, second_moment, ln_gain, ln_bias, norm_m, norm_v, slopes, slope_m, slope_v):
@@ -1289,9 +1390,10 @@
         low(heads, units, 2 * width), low(heads, units, 2 * width), low(heads, units, 2 * width),
         low(heads, 3 * units, 2 * width), low(heads, 3 * units, 2 * width),
         wide(micros, lane_units, lane_units), wide(micros, tok_rows, features), wide(micros, tok_rows, features),
-        wide(micros, split, tok_rows, TILE), wide(micros, split, 8 + tok_rows, TILE), wide(micros, split, 8, TILE), low(blocks, features, half), low(4, blocks, rows, half), low(4, blocks, rows, half),
+        wide(micros, split, tok_rows, TILE), wide(micros, split, 8 + tok_rows, TILE), wide(micros, split, 8, TILE),
+        low(2 * own, features), low(2 * own, FF), low(blocks, features, half), low(4, blocks, rows, half), low(4, blocks, rows, half),
         pieces(), pieces(), pieces(), pieces(), wide(48, features), wide(40, features),
-        pltpu.SemaphoreType.DMA((200,)), pltpu.SemaphoreType.DMA((200,)), pltpu.SemaphoreType.DMA((5,)),
+        pltpu.SemaphoreType.DMA((260,)), pltpu.SemaphoreType.DMA((260,)), pltpu.SemaphoreType.DMA((5,)),
     ]
     token_shape = (micros, tok_rows, features)
     dims = (units, features, FF, heads, micros, sizes)
@@ -1313,30 +1415,33 @@
     )(
         owners, doc_lengths[:, 0], slopes, ln_gain, ln_bias, tokens[:, 0], cotangent[:, 0], master[0]
     )
-    slot = pl.BlockSpec((1, rows, features), lambda j: (j, 0, 0))
+    steps = 4
+    slot = pl.BlockSpec((slots // steps, rows, features), lambda j: (j, 0, 0))
+    flat = (micros * tok_rows, features)
+    some = pl.BlockSpec((flat[0] // steps, features), lambda j: (j, 0))
     moment_shape = jax.ShapeDtypeStruct((slots, rows, features), WIDE)
     norm_shape = jax.ShapeDtypeStruct((4, features), WIDE)
     slope_shape = jax.ShapeDtypeStruct((1, heads), WIDE)
     out = pl.pallas_call(
         lambda *refs: adam_kernel(sizes, refs),
-        grid=(slots,),
+        grid=(steps,),
         out_shape=(
             moment_shape, moment_shape, moment_shape, jax.ShapeDtypeStruct((slots, rows, features), LOW),
             norm_shape, norm_shape, norm_shape, slope_shape, slope_shape, slope_shape,
-            jax.ShapeDtypeStruct(token_shape, WIDE), jax.ShapeDtypeStruct(token_shape, WIDE),
+            jax.ShapeDtypeStruct(flat, WIDE), jax.ShapeDtypeStruct(flat, WIDE),
         ),
-        in_specs=[smem] + [vmem] * 8 + [slot] * 3 + [hbm] * 2,
-        out_specs=(slot, slot, slot, slot, vmem, vmem, vmem, vmem, vmem, vmem, hbm, hbm),
-        scratch_shapes=[pltpu.SemaphoreType.DMA((2,))],
+        in_specs=[smem] + [vmem] * 9 + [slot] * 3 + [some] * 2,
+        out_specs=(slot, slot, slot, slot, vmem, vmem, vmem, vmem, vmem, vmem, some, some),
         compiler_params=pltpu.CompilerParams(dimension_semantics=("arbitrary",)),
         name="adam",
     )(
-        owners, red, small, jnp.concatenate([ln_gain, ln_bias], 0), norm_m, norm_v, slopes[None], slope_m[None],
-        slope_v[None], master[0], first_moment[0], second_moment[0], mixed, grad,
+        owners, red, small, ln_gain, ln_bias, norm_m, norm_v, slopes[None], slope_m[None],
+        slope_v[None], master[0], first_moment[0], second_moment[0],
+        mixed.reshape(flat), grad.reshape(flat),
     )
     new_w, new_m, new_v, new_low, norm, norm_m, norm_v, slope, slope_m, slope_v, mixed, grad = out
     return (
-        mixed[:, None], grad[:, None], new_w[None], new_m[None], new_v[None], new_low[None], norm, norm_m, norm_v,
+        mixed.reshape(tokens.shape), grad.reshape(tokens.shape), new_w[None], new_m[None], new_v[None], new_low[None], norm, norm_m, norm_v,
         slope[0], slope_m[0], slope_v[0],
     )
 

time: 183 us -> 129 us (0.70)
  Pallas kernels: 181 us -> 128 us
    pallas_call x1, Pallas kernels: 39.4 us -> 5.95 us  [fused_body(): pl.pallas_call(lambda *refs: adam_kernel(sizes, refs), grid=(steps,), out...]
    pallas_call x1, Pallas kernels: 142 us -> 122 us  [fused_body(): pl.pallas_call(lambda *refs: main_kernel(dims, refs), out_shape=(jax.Shap...]
where the time goes in v3:
time: 129 us
  Pallas kernels  128 us (99%)
    pallas_call x1, Pallas kernels, fused_body(): pl.pallas_call(lambda *refs: main_kernel(dims, refs), out_shape=(jax.Shap...  122 us
    pallas_call x1, Pallas kernels, fused_body(): pl.pallas_call(lambda *refs: adam_kernel(sizes, refs), grid=(steps,), out...  5.95 us

profile of v3, /device:TPU:0, one launch (start us, length us, event | category | flops | bytes accessed | tf_op | source)
XLA Modules:
  0.0 128.8 jit_solution(7827220929559709013)
XLA Ops:
  0.6 122.1 %block.1 = (f32[2,144,512]{2,1,0:T(8,128)}, f32[2,144,512]{2,1,0:T(8,128)}, bf16[18,64,512]{2,1,0:T(8,128)(2,1)}, f32[8,512]{1,0:T(8,128)}) custom-call(s32[6]{0:T(128)} %refs_0_.3, s32[2,4]{1,0:T(2,128)} %bitcast.33, f32[8]{0:T(128)} %refs_2_.1, f32[2,512]{1,0:T(2,128)} %refs_3_.3, f32[2,512]{1,0:T(2,128)} %refs_4_.3, bf16[2,144,512]{2,1,0:T(8,128)(2,1)} %bitcast.30, ...), custom_call_target="tpu_custom_call" | custom-call | tf_op jit(solution)/shard_map/block/pallas_call | solution.py:1400
  122.7 6.0 %adam.1 = (f32[8,64,512]{2,1,0:T(8,128)}, f32[8,64,512]{2,1,0:T(8,128)}, f32[8,64,512]{2,1,0:T(8,128)}, bf16[8,64,512]{2,1,0:T(8,128)(2,1)}, f32[4,512]{1,0:T(4,...) custom-call(s32[6]{0:T(128)} %refs_0_.3, ...), custom_call_target="tpu_custom_call" | custom-call | tf_op jit(solution)/shard_map/adam/pallas_call | solution.py:1425

commit v4 on v3

--- a/solution.py
+++ b/solution.py
@@ -453,9 +453,10 @@
             now = best[0][0] + cost
             for message, link, size in sends:
                 rate, delay = LINKS[link]
-                begin = max(now, free.get(link, 0.0))
-                free[link] = begin + size / rate
-                arrival[message] = free[link] + delay
+                lanes = ("f", "r", "l") if link == "f" else (link,)
+                end = max([now] + [free.get(lane, 0.0) for lane in lanes]) + size / rate
+                free.update({lane: end for lane in lanes})
+                arrival[message] = end + delay
             done.add(name)
             left.remove(name)
             listed.append((name, now))
@@ -463,12 +464,36 @@
 
 
 SLACK = 1.5
+SENDS, RECEIVES = 48, 172
+GATHERS = (
+    (0, 0, 1, 0.0),
+    (0, 1, 1, 0.01),
+    (0, 2, 1, 0.02),
+    (1, 0, 1, 0.1),
+    (1, 1, 1, 0.11),
+    (1, 2, 1, 0.12),
+    (3, 0, 2, 0.2),
+    (3, 2, 2, 0.22),
+    (2, 0, 1, 0.3),
+    (5, 0, 3, 0.4),
+)
+TURN = {5: 0, 1: 1}
+SCATTERS = (
+    (5, 0, 3, 1.0),
+    (3, 0, 2, 1.1),
+    (3, 2, 2, 1.2),
+    (2, 0, 1, 1.3),
+    (0, 0, 1, 0.7),
+    (0, 1, 1, 0.71),
+    (0, 2, 1, 0.72),
+    (1, 0, 3, 0.8),
+)
 LINKS = {
     "c": (400e3, 1.0),
     "x": (52e3, 2.3),
     "r": (52e3, 2.3),
     "l": (52e3, 2.3),
-    "f": (60e3, 4.0),
+    "f": (46e3, 3.3),
 }
 
 
@@ -503,7 +528,7 @@
         w, masters, mine, other, core_in, both, x_in, tok, cot, tail_in, wide_tok, wide_cot, x_pool, x_norm, x_att,
         x_two, x_act, x_short, d_up, d_low, d_inner, d_res, d_qkv, d_pool, pooled, hat_one, hat_two, root_one, root_two,
         resid, hidden, short_grad, res_grad, q_out, q_in, a_out, a_in, da_out, da_in, dq_out, dq_in, probs, mixed, grad,
-        wide_up, wide_grad, edge_in, x_near, x_wide, g, right_in, left_in, fin_out, fin_in, co_out, co_in, sums, sums_in, sends, recvs, local,
+        wide_up, wide_grad, edge_in, x_near, x_wide, t_left, t_out, t_in, g, right_in, left_in, fin_out, fin_in, co_out, co_in, sums, sums_in, sends, recvs, local,
     ) = refs[12:]
     half = features // 2
     width = features // heads
@@ -534,22 +559,33 @@
     right_peer = (b, seq_of(at(1)))
     left_peer = (b, seq_of(at(-1)))
     plan = Plan()
-    flying = {}
-
-    def send(name, source, target, device):
-        index = len(flying)
-        flying[name] = pltpu.make_async_remote_copy(
+    flying, started, boxes = {}, [], {}
+
+    def launch(name, copies, starts, group):
+        if len(started) >= SENDS:
+            started[len(started) - SENDS].wait_send()
+        started.append(copies[0])
+        flying[name] = copies[0]
+        for start in starts:
+            start()
+
+    def describe(source, target, device, group):
+        box = boxes.setdefault(group, len(boxes))
+        return pltpu.make_async_remote_copy(
             src_ref=source,
             dst_ref=target,
-            send_sem=sends.at[index],
-            recv_sem=recvs.at[index],
+            send_sem=sends.at[len(started) % SENDS],
+            recv_sem=recvs.at[box],
             device_id=device,
             device_id_type=MESH,
         )
-        flying[name].start()
-
-    def nothing():
-        pass
+
+    def send(name, source, target, device, group=None):
+        copy = describe(source, target, device, group or name)
+        launch(name, [copy], [copy.start], group or name)
+
+    def gather_up(group, whole):
+        describe(whole, whole, core_peer, group).wait_recv()
 
     loads = [
         pltpu.make_async_copy(master_hbm, masters, local.at[0]),
@@ -598,18 +634,19 @@
 
         return run
 
-    part = hidden_blocks // 2
-    gathers = [
-        ("p", (0,), spans[0][0], None, sizes[0]),
-        ("q", (1,), spans[1][0], None, sizes[1]),
-        ("F", (3, 4), ours, theirs, part),
-        ("G", (3, 4), ours + part, theirs + part, part),
-        ("o", (2,), spans[2][0], None, sizes[2]),
-        ("u", (5,), up_base, None, sizes[5]),
-    ]
+    have = {k: [] for k in range(6)}
+    gathers = []
+    for k, offset, size, rank in GATHERS:
+        name = ("w", k, offset)
+        if k == 3:
+            gathers.append((rank, name, (3, 4), ours + offset, theirs + offset, size))
+            have[3] += [("h", name), ("hy", name)]
+        else:
+            gathers.append((rank, name, (k,), spans[k][0] + offset, None, size))
+            have[k] += [("h", name)]
     piece_bytes = rows_of * half * 2
 
-    def gather_chunk(order, name, parents, here, there, size):
+    def gather_chunk(rank, name, parents, here, there, size):
         split = there is not None
         load = size * piece_bytes
         blocks = pl.ds(here, size)
@@ -624,29 +661,30 @@
         def join_x():
             flying[("g1", name)].wait_recv()
             w[blocks, c, rows_at(0)] = both[blocks] + x_in[blocks]
-            send(("R", 1, name), piece(0), piece(0), right_peer)
-            send(("L", 1, name), piece(0), piece(0), left_peer)
-
-        def onward(side, step):
+            send(("R", 1, name), piece(0), piece(0), right_peer, (1, name))
+            send(("L", 1, name), piece(0), piece(0), left_peer, (1, name))
+
+        def onward(step):
             def run():
-                flying[(side, step - 1, name)].wait_recv()
+                gather_up((step - 1, name), w.at[blocks, c, 0 : rows_of * (2 if step < 5 else 1)])
                 if step == 5:
                     return
-                offset = (1 - step) if side == "R" else (step - 1)
-                part = piece(offset)
-                if step == 4:
-                    part = piece(offset, 0 if side == "R" else rows_of // 2, rows_of // 2)
-                send((side, step, name), part, part, right_peer if side == "R" else left_peer)
+                for side, offset, peer in (("R", 1 - step, right_peer), ("L", step - 1, left_peer)):
+                    part = piece(offset)
+                    if step == 4:
+                        part = piece(offset, 0 if side == "R" else rows_of // 2, rows_of // 2)
+                    send((side, step, name), part, part, peer, (step, name))
 
             return run
 
-        def across(side, step):
+        def across(step):
             def run():
-                offset = -step if side == "R" else step
-                part = piece(offset)
-                if step == 4:
-                    part = piece(offset, 0 if side == "R" else rows_of // 2, rows_of // 2)
-                send(("X", side, step, name), part, part, x_peer)
+                for side, offset in (("R", -step), ("L", step)):
+                    part = piece(offset)
+                    if step == 4:
+                        part = piece(offset, 0 if side == "R" else rows_of // 2, rows_of // 2)
+                    if step > 0 or side == "R":
+                        send(("X", side, step, name), part, part, x_peer, ("X", name))
 
             return run
 
@@ -656,7 +694,6 @@
 
             return run
 
-        rank = order * 0.1
         plan.add(("cx", name), join_here, [("cs", k) for k in parents], (), [(("g1", name), "x", load)], 0.05, rank)
         plan.add(
             ("x", name), join_x, [("cx", name)], [("g1", name)],
@@ -664,25 +701,28 @@
         )
         crossing = []
 
-        def cross(side, step, after):
-            message = ("X", side, step, name)
-            plan.add(message, across(side, step), [after], (), [(message, "x", load if step < 4 else load // 2)], 0.05, rank + 0.05)
-            crossing.append(message)
+        def cross(step, after):
+            messages = [("X", side, step, name) for side in ("RL" if step else "R")]
+            size_of = load if step < 4 else load // 2
+            plan.add(("X", step, name), across(step), [after], (), [(m, "x", size_of) for m in messages], 0.05, rank + 0.05)
+            crossing.extend(messages)
 
         if split:
-            cross("R", 0, ("x", name))
+            cross(0, ("x", name))
         for step in (2, 3, 4, 5):
-            for side, link in (("R", "r"), ("L", "l")):
-                out = [((side, step, name), link, load if step < 4 else load // 2)] if step < 5 else []
-                before = ("x", name) if step == 2 else (side, step - 1, "f", name)
-                plan.add((side, step, "f", name), onward(side, step), [before], [(side, step - 1, name)], out, 0.05, rank)
-                if split:
-                    cross(side, step - 1, (side, step, "f", name))
-        ends = [("R", 5, "f", name), ("L", 5, "f", name)]
-        plan.add(("di", name), distribute("D", blocks), ends, (), [(("D", name), "c", 8 * load)], 0.05, rank)
+            size_of = load if step < 4 else load // 2
+            out = [((side, step, name), link, size_of) for side, link in (("R", "r"), ("L", "l"))] if step < 5 else []
+            before = ("x", name) if step == 2 else (step - 1, "f", name)
+            waits = [(side, step - 1, name) for side in "RL"]
+            plan.add((step, "f", name), onward(step), [before], waits, out, 0.05, rank)
+            if split:
+                cross(step - 1, (step, "f", name))
+        plan.add(("di", name), distribute("D", blocks), [(5, "f", name)], (), [(("D", name), "c", 8 * load)], 0.05, rank)
         plan.add(("h", name), arrive(("D", name)), [("di", name)], [("D", name)], (), 0.02, rank)
         if split:
-            plan.add(("xw", name), arrive(*crossing), crossing, crossing, (), 0.05, rank)
+            whole = w.at[pl.ds(there, size), c]
+            last = [("X", step, name) for step in range(5)]
+            plan.add(("xw", name), lambda: gather_up(("X", name), whole), last, crossing, (), 0.05, rank)
             plan.add(("dy", name), distribute("E", away), [("xw", name)], (), [(("E", name), "c", 8 * load)], 0.05, rank)
             plan.add(("hy", name), arrive(("E", name)), [("dy", name)], [("E", name)], (), 0.02, rank)
 
@@ -698,8 +738,8 @@
         load = (hi - lo) * piece_bytes
         plan.add(("co", k), contribute(k), ["ms"], (), [(("g0", k), "c", load)], 0.04 * (hi - lo), 0.1)
         plan.add(("cs", k), join_cores(k), [("co", k)], [("g0", k)], (), 0.02 * (hi - lo), 0.1)
-    for order, chunk in enumerate(gathers):
-        gather_chunk(order, *chunk)
+    for chunk in gathers:
+        gather_chunk(*chunk)
 
     def exchange(name, buffer):
         send(name, buffer.at[0:own], buffer.at[own : 2 * own], core_peer)
@@ -809,7 +849,7 @@
     def spread(name, source, target):
         for step in range(1, count):
             there = lax.rem(s + step, count)
-            send((name, step), source.at[there], target.at[s], (b, there))
+            send((name, step), source.at[there], target.at[s], (b, there), name)
         target[s] = source[s]
 
     def spread_names(name):
@@ -845,7 +885,7 @@
         return row_ids - col_ids
 
     def attend_now():
-        arrive(*spread_names("q"))()
+        gather_up("q", q_in.at[0 : count - 1])
         queries, keys, values = (heads_of(q_in, part) for part in range(3))
         slope = slopes[s]
         total = None
@@ -869,7 +909,7 @@
         spread("a", a_out, a_in)
 
     def merge():
-        arrive(*spread_names("a"))()
+        gather_up("a", a_in.at[0 : count - 1])
         for pair in range(heads // 2):
             columns = slice(pair * pair_width, (pair + 1) * pair_width)
             first, second = from_heads(a_in, pair, 0)
@@ -932,24 +972,24 @@
 
         return run
 
-    plan.add("po", pool, ["pc", ("h", "p")], (), [shared("en", features)], 0.6, rank=3)
-    plan.add("pr", project, ["po", ("h", "q")], (), spread_sends("q", 3 * units), 0.6, rank=3)
+    plan.add("po", pool, ["pc", *have[0]], (), [shared("en", features)], 0.6, rank=3)
+    plan.add("pr", project, ["po", *have[1]], (), spread_sends("q", 3 * units), 0.6, rank=3)
     plan.add("at", attend_now, ["pr"], spread_names("q"), spread_sends("a", units), 1.1, rank=3)
     plan.add("me", merge, ["at"], spread_names("a"), [shared("ea", features)], 0.15, rank=3)
-    plan.add("ou", project_out, ["me", ("h", "o")], (), [shared("et", features)], 0.45, rank=3)
+    plan.add("ou", project_out, ["me", *have[2]], (), [shared("et", features)], 0.45, rank=3)
     for j in range(hidden_blocks):
         last = j == hidden_blocks - 1
         plan.add(
-            ("wi", j), widen(j), ["ou", ("h", "F"), ("hy", "F"), ("h", "G"), ("hy", "G")] + ([("wi", i) for i in range(j)] if last else []), (),
+            ("wi", j), widen(j), ["ou", *have[3]] + ([("wi", i) for i in range(j)] if last else []), (),
             [shared("ec", hidden_width)] if last else (), 0.3, rank=3,
         )
     plan.add(
-        "na", narrow, [("wi", j) for j in range(hidden_blocks)] + [("h", "F"), ("hy", "F"), ("h", "G"), ("hy", "G")], (), [shared("es", features)], 0.5,
+        "na", narrow, [("wi", j) for j in range(hidden_blocks)] + [*have[3]], (), [shared("es", features)], 0.5,
         rank=3,
     )
     for r in range(3):
         plan.add(
-            ("li", r), lift(r), ["na", ("h", "u"), "tok"] + ([("li", i) for i in range(r)]), (), (), 0.3, rank=8
+            ("li", r), lift(r), ["na", *have[5], "tok"] + ([("li", i) for i in range(r)]), (), (), 0.3, rank=8
         )
 
     def back_short():
@@ -1006,7 +1046,7 @@
         spread("da", da_out, da_in)
 
     def back_attend():
-        arrive(*spread_names("da"))()
+        gather_up("da", da_in.at[0 : count - 1])
         queries, keys, values = (heads_of(q_in, part) for part in range(3))
         grads = da_in[...].reshape(lane_units, pair_width)
         totals = [None, None, None]
@@ -1039,7 +1079,7 @@
         sums[5:8, :] = jnp.zeros((3, features), WIDE)
 
     def back_project():
-        arrive(*spread_names("dq"))()
+        gather_up("dq", dq_in.at[0 : count - 1])
         for part in range(3):
             for pair in range(heads // 2):
                 begin = part * features + pair * pair_width
@@ -1081,19 +1121,19 @@
                 grad[micro, :, columns] = cot[micro, :, columns].astype(WIDE) + wide_grad[micro, tile, 8 : 8 + tokens]
         outs[1].start()
 
-    plan.add("bs", back_short, ["cot", ("h", "u")], (), [shared("el", features)], 0.65, rank=4)
+    plan.add("bs", back_short, ["cot", *have[5]], (), [shared("el", features)], 0.65, rank=4)
     for j in range(hidden_blocks):
         last = j == hidden_blocks - 1
         plan.add(
             ("bw", j), back_widen(j),
-            ["bs", ("h", "F"), ("hy", "F"), ("h", "G"), ("hy", "G"), ("wi", j)] + ([("bw", i) for i in range(j)] if last else []), (),
+            ["bs", *have[3], ("wi", j)] + ([("bw", i) for i in range(j)] if last else []), (),
             [shared("ei", hidden_width)] if last else (), 0.35, rank=4,
         )
     plan.add(
-        "b2", back_two, [("bw", j) for j in range(hidden_blocks)] + [("h", "F"), ("hy", "F"), ("h", "G"), ("hy", "G")], (),
+        "b2", back_two, [("bw", j) for j in range(hidden_blocks)] + [*have[3]], (),
         [shared("er", features)], 0.9, rank=4,
     )
-    plan.add("bo", back_out, ["b2", ("h", "o")], (), spread_sends("da", units), 0.45, rank=4)
+    plan.add("bo", back_out, ["b2", *have[2]], (), spread_sends("da", units), 0.45, rank=4)
     plan.add("ba", back_attend, ["bo", "at"], spread_names("da"), spread_sends("dq", 3 * units), 1.4, rank=4)
     plan.add("bp", back_project, ["ba"], spread_names("dq"), [shared("eq", 3 * features)], 0.2, rank=4)
     plan.add("b1", back_one, ["bp"], (), [shared("ed1", features)], 0.75, rank=4)
@@ -1145,17 +1185,8 @@
         return run
 
     def send_either(name, first_source, second_source, target):
-        index = len(flying)
-        copies = [
-            pltpu.make_async_remote_copy(
-                src_ref=source, dst_ref=target, send_sem=sends.at[index], recv_sem=recvs.at[index], device_id=x_peer,
-                device_id_type=MESH,
-            )
-            for source in (first_source, second_source)
-        ]
-        flying[name] = copies[0]
-        for plane in range(2):
-            pl.when(x == plane)(copies[plane].start)
+        copies = [describe(source, target, x_peer, name) for source in (first_source, second_source)]
+        launch(name, copies, [lambda plane=plane: pl.when(x == plane)(copies[plane].start) for plane in range(2)], name)
 
     def near_away():
         send_either("sn", d_low.at[0:own], x_two.at[0:own], x_near.at[0:own])
@@ -1208,64 +1239,126 @@
         plan.add(("got", "cw", j), arrive(("cw", j)), [("wc", j)], [("cw", j)], (), 0.02, 2)
         deps = [("got", e) for e in ("et", "ec", "el", "ei", "cn")] + [("got", "cw", j)]
         plan.add(("gr", j, "s"), outer_split(j), deps, cost=0.6, rank=4.5)
+    quarter = half // 2
+    quartered = {5: (x_short, d_up, "na", "cot", "es", "eu"), 1: (x_norm, d_qkv, "po", "bp", "en", "eq")}
+
+    def left_away(k):
+        def run():
+            send(("tx", k), quartered[k][0].at[0:own], t_left.at[TURN[k], 0:own], x_peer)
+
+        return run
+
+    def left_core(k):
+        def run():
+            arrive(("tx", k))()
+            send(("tc", k), t_left.at[TURN[k], 0:own], t_left.at[TURN[k], own : 2 * own], core_peer)
+
+        return run
+
+    def right_away(k, r):
+        columns = slice(r * half, (r + 1) * half)
+
+        def run():
+            for core in range(2):
+                begin = r * features + core * half + (1 - x) * quarter
+                t_out[TURN[k], :, r * half + core * quarter : r * half + (core + 1) * quarter] = quartered[k][1][
+                    0:own, pl.ds(pl.multiple_of(begin, quarter), quarter)
+                ]
+            send(("ty", k, r), t_out.at[TURN[k], :, columns], t_in.at[TURN[k], 0:own, columns], x_peer)
+
+        return run
+
+    def right_core(k, r):
+        columns = slice(r * half, (r + 1) * half)
+
+        def run():
+            arrive(("ty", k, r))()
+            send(("td", k, r), t_in.at[TURN[k], 0:own, columns], t_in.at[TURN[k], own : 2 * own, columns], core_peer)
+
+        return run
+
+    def outer_quarter(k, r):
+        def run():
+            left, right = quartered[k][:2]
+            near = pl.ds(pl.multiple_of(r * features + c * half + x * quarter, quarter), quarter)
+            away = pl.ds(pl.multiple_of(r * half + c * quarter, quarter), quarter)
+            total = contract(left[...], right[:, near], 0, 0) + contract(t_left[TURN[k]], t_in[TURN[k], :, away], 0, 0)
+            g[spans[k][0] + r, :, pl.ds(pl.multiple_of(x * quarter, quarter), quarter)] = total.astype(LOW)
+
+        return run
+
+    for k, (_, _, left_dep, right_dep, left_got, right_got) in quartered.items():
+        plan.add(("tx", k), left_away(k), [left_dep], (), [(("tx", k), "x", lump)], 0.05, 2.5)
+        plan.add(("tw", k), left_core(k), [("tx", k)], [("tx", k)], [(("tc", k), "c", lump)], 0.05, 2.5)
+        plan.add(("got", "tc", k), arrive(("tc", k)), [("tw", k)], [("tc", k)], (), 0.02, 2.5)
+        for r in range(3):
+            plan.add(("ty", k, r), right_away(k, r), [right_dep], (), [(("ty", k, r), "x", lump // 2)], 0.05, 2.5)
+            plan.add(("tz", k, r), right_core(k, r), [("ty", k, r)], [("ty", k, r)], [(("td", k, r), "c", lump // 2)], 0.05, 2.5)
+            plan.add(("got", "td", k, r), arrive(("td", k, r)), [("tz", k, r)], [("td", k, r)], (), 0.02, 2.5)
+            deps = [("got", left_got), ("got", right_got), ("got", "tc", k), ("got", "td", k, r)]
+            plan.add(("gr", spans[k][0] + r), outer_quarter(k, r), deps, cost=0.4, rank=5)
     weight_grads = []
     for r in range(3):
         weight_grads.append((r, x_pool, r, d_pool, 0, [("got", "ep"), ("got", "ed1")]))
-        weight_grads.append((3 + r, x_norm, 0, d_qkv, r, [("got", "en"), ("got", "eq")]))
-        weight_grads.append((up_base + r, x_short, 0, d_up, r, [("got", "es"), ("got", "eu")]))
     weight_grads.append((6, x_att, 0, d_res, 0, [("got", "ea"), ("got", "er")]))
     for block, left, left_block, right, right_block, deps in weight_grads:
         plan.add(("gr", block), outer(block, left, left_block, right, right_block), deps, cost=0.3, rank=5)
 
-    def scatter_chunk(order, name, here, there, size, deps):
-        split = there is not None
+    def scatter_chunk(rank, name, here, there, size, deps):
+        split, quarters = there is not None, there is here
         blocks = pl.ds(here, size)
-        load = size * piece_bytes
-        rank = 1 + order * 0.1
-
-        def first_step(side):
+        load = size * piece_bytes // (2 if quarters else 1)
+        away, span, away_span, length_out = blocks, slice(None), slice(None), half
+        begin_out, away_out = c * half, c * half
+        if quarters:
+            span = pl.ds(pl.multiple_of(x * quarter, quarter), quarter)
+            away_span = pl.ds(pl.multiple_of((1 - x) * quarter, quarter), quarter)
+            length_out, begin_out, away_out = quarter, c * half + x * quarter, c * half + (1 - x) * quarter
+        elif split:
+            away = pl.ds(there, size)
+        out_span = pl.ds(pl.multiple_of(begin_out, length_out), length_out)
+        out_away = pl.ds(pl.multiple_of(away_out, length_out), length_out)
+
+        half_rows = rows_of // 2
+        sides = (("R", 0, right_in, right_peer), ("L", half_rows, left_in, left_peer))
+
+        def first_step():
+            for side, part, inbox, peer in sides:
+                source = g.at[blocks, rows_at(4, part, half_rows), span]
+                target = inbox.at[0, blocks, part : part + half_rows, span]
+                send((side, "s", 1, name), source, target, peer, ("s", 1, name))
+
+        def take(step):
+            gather_up(("s", step, name), g.at[blocks, 0 : rows_of * (1 if step == 1 else 2), span])
+
+        def next_step(step):
             def run():
-                part = 0 if side == "R" else rows_of // 2
-                inbox = right_in if side == "R" else left_in
-                send(
-                    (side, "s", 1, name), g.at[blocks, rows_at(4, part, rows_of // 2)],
-                    inbox.at[0, blocks, part : part + rows_of // 2], right_peer if side == "R" else left_peer,
-                )
+                take(step - 1)
+                for side, half_part, inbox, peer in sides:
+                    offset = (5 - step) if side == "R" else (step - 5)
+                    part, length = (half_part, half_rows) if step == 2 else (0, rows_of)
+                    rows = rows_at(offset, part, length)
+                    g[blocks, rows, span] = g[blocks, rows, span] + inbox[step - 2, blocks, part : part + length, span]
+                    source = g.at[blocks, rows_at(offset), span]
+                    send((side, "s", step, name), source, inbox.at[step - 1, blocks, :, span], peer, ("s", step, name))
 
             return run
 
-        def next_step(side, step):
-            def run():
-                inbox = right_in if side == "R" else left_in
-                offset = (5 - step) if side == "R" else (step - 5)
-                flying[(side, "s", step - 1, name)].wait_recv()
-                part, length = 0, rows_of
-                if step == 2:
-                    part, length = (0 if side == "R" else rows_of // 2), rows_of // 2
-                rows = rows_at(offset, part, length)
-                g[blocks, rows] = g[blocks, rows] + inbox[step - 2, blocks, part : part + length]
-                send(
-                    (side, "s", step, name), g.at[blocks, rows_at(offset)], inbox.at[step - 1, blocks],
-                    right_peer if side == "R" else left_peer,
-                )
-
-            return run
-
         def finish():
-            arrive(("R", "s", 4, name), ("L", "s", 4, name))()
-            total = g[blocks, rows_at(0)].astype(WIDE) + right_in[3, blocks].astype(WIDE) + left_in[3, blocks].astype(WIDE)
-            fin_out[blocks] = total.astype(LOW)
-            send(("rx", name), fin_out.at[blocks], fin_in.at[blocks], x_peer)
+            take(4)
+            total = g[blocks, rows_at(0), span].astype(WIDE)
+            total = total + right_in[3, blocks, :, span].astype(WIDE) + left_in[3, blocks, :, span].astype(WIDE)
+            fin_out[blocks, :, span] = total.astype(LOW)
+            send(("rx", name), fin_out.at[blocks, :, span], fin_in.at[blocks, :, span], x_peer)
             if split:
-                red[blocks, :, my_half] = fin_out[blocks]
-                send(("rc", name), fin_out.at[blocks], co_in.at[blocks], core_peer)
+                red[blocks, :, out_span] = fin_out[blocks, :, span]
+                send(("rc", name), fin_out.at[blocks, :, span], co_in.at[blocks, :, span], core_peer)
 
         def finish_x():
             arrive(("rx", name))()
             if split:
-                away = pl.ds(there, size)
-                red[away, :, my_half] = fin_in[away]
-                send(("rd", name), fin_in.at[away], co_in.at[away], core_peer)
+                red[away, :, out_away] = fin_in[away, :, away_span]
+                send(("rd", name), fin_in.at[away, :, away_span], co_in.at[away, :, away_span], core_peer)
             else:
                 total = (fin_out[blocks].astype(WIDE) + fin_in[blocks].astype(WIDE)).astype(LOW)
                 co_out[blocks] = total
@@ -1273,25 +1366,21 @@
                 send(("rc", name), co_out.at[blocks], co_in.at[blocks], core_peer)
 
         def finish_core():
-            arrive(("rc", name))()
+            arrive(("rc", name), *([("rd", name)] if split else []))()
             red[blocks, :, other_half] = co_in[blocks]
-            if split:
-                arrive(("rd", name))()
-                away = pl.ds(there, size)
+            if split and not quarters:
                 red[away, :, other_half] = co_in[away]
 
-        sides = (("R", "r"), ("L", "l"))
-        for side, link in sides:
-            plan.add((side, "r", 1, name), first_step(side), deps, (), [((side, "s", 1, name), link, load // 2)], 0.05, rank)
+        links = (("R", "r"), ("L", "l"))
+        out = [((side, "s", 1, name), link, load // 2) for side, link in links]
+        plan.add(("r", 1, name), first_step, deps, (), out, 0.05, rank)
         for step in (2, 3, 4):
-            for side, link in sides:
-                plan.add(
-                    (side, "r", step, name), next_step(side, step), [(side, "r", step - 1, name)],
-                    [(side, "s", step - 1, name)], [((side, "s", step, name), link, load)], 0.02 * size, rank,
-                )
+            waits = [(side, "s", step - 1, name) for side in "RL"]
+            out = [((side, "s", step, name), link, load) for side, link in links]
+            plan.add(("r", step, name), next_step(step), [("r", step - 1, name)], waits, out, 0.04 * size, rank)
         own_out = [(("rc", name), "c", load)]
         plan.add(
-            ("fi", name), finish, [("R", "r", 4, name), ("L", "r", 4, name)], [("R", "s", 4, name), ("L", "s", 4, name)],
+            ("fi", name), finish, [("r", 4, name)], [("R", "s", 4, name), ("L", "s", 4, name)],
             [(("rx", name), "x", load)] + (own_out if split else []), 0.02 * size, rank,
         )
         late_out = [(("rd", name), "c", load)] if split else own_out
@@ -1300,20 +1389,18 @@
             ("fc", name), finish_core, [("fx", name)], [("rc", name)] + ([("rd", name)] if split else []), (), 0.02 * size, rank
         )
 
-    scatters = [("u", up_base, None, sizes[5], [("gr", up_base + r) for r in range(3)])]
-    scatters.append(("F", ours, theirs, part, [("gr", j, "s") for j in range(part)]))
-    scatters.append(("G", ours + part, theirs + part, part, [("gr", j, "s") for j in range(part, 2 * part)]))
-    scatters.append(("o", spans[2][0], None, 1, [("gr", spans[2][0])]))
-    for block in range(spans[1][0], spans[1][1]):
-        scatters.append((block, block, None, 1, [("gr", block)]))
-    for block in range(spans[0][0], spans[0][1]):
-        scatters.append((block, block, None, 1, [("gr", block)]))
-    for order, chunk in enumerate(scatters):
-        scatter_chunk(order, *chunk)
+    for k, offset, size, rank in SCATTERS:
+        name = ("g", k, offset)
+        if k == 3:
+            deps = [("gr", j, "s") for j in range(offset, offset + size)]
+            scatter_chunk(rank, name, ours + offset, theirs + offset, size, deps)
+        else:
+            begin = spans[k][0] + offset
+            scatter_chunk(rank, name, begin, begin if k in quartered else None, size, [("gr", begin + j) for j in range(size)])
 
     for name, _ in plan.order():
         plan.tasks[name][0]()
-    for name, copy in flying.items():
+    for copy in started[-SENDS:]:
         copy.wait_send()
     for copy in outs:
         copy.wait()
@@ -1391,9 +1478,10 @@
         low(heads, 3 * units, 2 * width), low(heads, 3 * units, 2 * width),
         wide(micros, lane_units, lane_units), wide(micros, tok_rows, features), wide(micros, tok_rows, features),
         wide(micros, split, tok_rows, TILE), wide(micros, split, 8 + tok_rows, TILE), wide(micros, split, 8, TILE),
-        low(2 * own, features), low(2 * own, FF), low(blocks, features, half), low(4, blocks, rows, half), low(4, blocks, rows, half),
+        low(2 * own, features), low(2 * own, FF),
+        low(2, 2 * own, features), low(2, own, 3 * half), low(2, 2 * own, 3 * half), low(blocks, features, half), low(4, blocks, rows, half), low(4, blocks, rows, half),
         pieces(), pieces(), pieces(), pieces(), wide(48, features), wide(40, features),
-        pltpu.SemaphoreType.DMA((260,)), pltpu.SemaphoreType.DMA((260,)), pltpu.SemaphoreType.DMA((5,)),
+        pltpu.SemaphoreType.DMA((SENDS,)), pltpu.SemaphoreType.DMA((RECEIVES,)), pltpu.SemaphoreType.DMA((5,)),
     ]
     token_shape = (micros, tok_rows, features)
     dims = (units, features, FF, heads, micros, sizes)

time: 129 us -> 117 us (0.907)
  Pallas kernels: 128 us -> 116 us
    pallas_call x1, Pallas kernels: 122 us -> 110 us  [fused_body(): pl.pallas_call(lambda *refs: main_kernel(dims, refs), out_shape=(jax.Shap...]
where the time goes in v4:
time: 117 us
  Pallas kernels  116 us (99%)
    pallas_call x1, Pallas kernels, fused_body(): pl.pallas_call(lambda *refs: main_kernel(dims, refs), out_shape=(jax.Shap...  110 us
    pallas_call x1, Pallas kernels, fused_body(): pl.pallas_call(lambda *refs: adam_kernel(sizes, refs), grid=(steps,), out...  5.95 us

profile of v4, /device:TPU:0, one launch (start us, length us, event | category | flops | bytes accessed | tf_op | source)
XLA Modules:
  0.0 116.8 jit_solution(13328589489797329279)
XLA Ops:
  0.6 110.0 %block.1 = (f32[2,144,512]{2,1,0:T(8,128)}, f32[2,144,512]{2,1,0:T(8,128)}, bf16[18,64,512]{2,1,0:T(8,128)(2,1)}, f32[8,512]{1,0:T(8,128)}) custom-call(s32[6]{0:T(128)} %refs_0_.3, s32[2,4]{1,0:T(2,128)} %bitcast.33, f32[8]{0:T(128)} %refs_2_.1, f32[2,512]{1,0:T(2,128)} %refs_3_.3, f32[2,512]{1,0:T(2,128)} %refs_4_.3, bf16[2,144,512]{2,1,0:T(8,128)(2,1)} %bitcast.30, ...), custom_call_target="tpu_custom_call" | custom-call | tf_op jit(solution)/shard_map/block/pallas_call | solution.py:1488
  110.7 6.0 %adam.1 = (f32[8,64,512]{2,1,0:T(8,128)}, f32[8,64,512]{2,1,0:T(8,128)}, f32[8,64,512]{2,1,0:T(8,128)}, bf16[8,64,512]{2,1,0:T(8,128)(2,1)}, f32[4,512]{1,0:T(4,...) custom-call(s32[6]{0:T(128)} %refs_0_.3, ...), custom_call_target="tpu_custom_call" | custom-call | tf_op jit(solution)/shard_map/adam/pallas_call | solution.py:1513

commit v5 on v4

--- a/solution.py
+++ b/solution.py
@@ -464,7 +464,7 @@
 
 
 SLACK = 1.5
-SENDS, RECEIVES = 48, 172
+SENDS, RECEIVES = 32, 168
 GATHERS = (
     (0, 0, 1, 0.0),
     (0, 1, 1, 0.01),
@@ -477,15 +477,15 @@
     (2, 0, 1, 0.3),
     (5, 0, 3, 0.4),
 )
-TURN = {5: 0, 1: 1}
+QUARTERS = {5: 0, 1: 3, 0: 6}
+GATHER_QUARTERS = ()
+AFTER = {}
 SCATTERS = (
     (5, 0, 3, 1.0),
     (3, 0, 2, 1.1),
     (3, 2, 2, 1.2),
     (2, 0, 1, 1.3),
-    (0, 0, 1, 0.7),
-    (0, 1, 1, 0.71),
-    (0, 2, 1, 0.72),
+    (0, 0, 3, 0.7),
     (1, 0, 3, 0.8),
 )
 LINKS = {
@@ -642,31 +642,37 @@
             gathers.append((rank, name, (3, 4), ours + offset, theirs + offset, size))
             have[3] += [("h", name), ("hy", name)]
         else:
-            gathers.append((rank, name, (k,), spans[k][0] + offset, None, size))
-            have[k] += [("h", name)]
+            begin = spans[k][0] + offset
+            gathers.append((rank, name, (k,), begin, begin if k in GATHER_QUARTERS else None, size))
+            have[k] += [("h", name)] + ([("hy", name)] if k in GATHER_QUARTERS else [])
     piece_bytes = rows_of * half * 2
 
+    quarter = half // 2
+    plane_span = pl.ds(pl.multiple_of(x * quarter, quarter), quarter)
+    plane_away = pl.ds(pl.multiple_of((1 - x) * quarter, quarter), quarter)
+
     def gather_chunk(rank, name, parents, here, there, size):
-        split = there is not None
-        load = size * piece_bytes
+        split, quarters = there is not None, there is here
+        load = size * piece_bytes // (2 if quarters else 1)
         blocks = pl.ds(here, size)
         away = pl.ds(there, size) if split else blocks
+        span, away_span = (plane_span, plane_away) if quarters else (slice(None), slice(None))
 
         def piece(offset, part=0, length=rows_of):
-            return w.at[blocks, c, rows_at(offset, part, length)]
+            return w.at[blocks, c, rows_at(offset, part, length), span]
 
         def join_here():
-            send(("g1", name), both.at[away], x_in.at[away], x_peer)
+            send(("g1", name), both.at[away, :, away_span], x_in.at[away, :, away_span], x_peer)
 
         def join_x():
             flying[("g1", name)].wait_recv()
-            w[blocks, c, rows_at(0)] = both[blocks] + x_in[blocks]
+            w[blocks, c, rows_at(0), span] = both[blocks, :, span] + x_in[blocks, :, span]
             send(("R", 1, name), piece(0), piece(0), right_peer, (1, name))
             send(("L", 1, name), piece(0), piece(0), left_peer, (1, name))
 
         def onward(step):
             def run():
-                gather_up((step - 1, name), w.at[blocks, c, 0 : rows_of * (2 if step < 5 else 1)])
+                gather_up((step - 1, name), w.at[blocks, c, 0 : rows_of * (2 if step < 5 else 1), span])
                 if step == 5:
                     return
                 for side, offset, peer in (("R", 1 - step, right_peer), ("L", step - 1, left_peer)):
@@ -688,9 +694,9 @@
 
             return run
 
-        def distribute(which, span):
+        def distribute(which, held, lanes):
             def run():
-                send((which, name), w.at[span, c], w.at[span, c], core_peer)
+                send((which, name), w.at[held, c, :, lanes], w.at[held, c, :, lanes], core_peer)
 
             return run
 
@@ -717,13 +723,13 @@
             plan.add((step, "f", name), onward(step), [before], waits, out, 0.05, rank)
             if split:
                 cross(step - 1, (step, "f", name))
-        plan.add(("di", name), distribute("D", blocks), [(5, "f", name)], (), [(("D", name), "c", 8 * load)], 0.05, rank)
+        plan.add(("di", name), distribute("D", blocks, span), [(5, "f", name)], (), [(("D", name), "c", 8 * load)], 0.05, rank)
         plan.add(("h", name), arrive(("D", name)), [("di", name)], [("D", name)], (), 0.02, rank)
         if split:
-            whole = w.at[pl.ds(there, size), c]
+            whole = w.at[away, c, :, away_span]
             last = [("X", step, name) for step in range(5)]
             plan.add(("xw", name), lambda: gather_up(("X", name), whole), last, crossing, (), 0.05, rank)
-            plan.add(("dy", name), distribute("E", away), [("xw", name)], (), [(("E", name), "c", 8 * load)], 0.05, rank)
+            plan.add(("dy", name), distribute("E", away, away_span), [("xw", name)], (), [(("E", name), "c", 8 * load)], 0.05, rank)
             plan.add(("hy", name), arrive(("E", name)), [("dy", name)], [("E", name)], (), 0.02, rank)
 
     def arrive(*names):
@@ -1239,68 +1245,87 @@
         plan.add(("got", "cw", j), arrive(("cw", j)), [("wc", j)], [("cw", j)], (), 0.02, 2)
         deps = [("got", e) for e in ("et", "ec", "el", "ei", "cn")] + [("got", "cw", j)]
         plan.add(("gr", j, "s"), outer_split(j), deps, cost=0.6, rank=4.5)
-    quarter = half // 2
-    quartered = {5: (x_short, d_up, "na", "cot", "es", "eu"), 1: (x_norm, d_qkv, "po", "bp", "en", "eq")}
-
-    def left_away(k):
+    quartered = {
+        0: (x_pool, 3, d_pool, 1, "pc", "b1", "ep", "ed1"),
+        1: (x_norm, 1, d_qkv, 3, "po", "bp", "en", "eq"),
+        2: (x_att, 1, d_res, 1, "me", "b2", "ea", "er"),
+        5: (x_short, 1, d_up, 3, "na", "cot", "es", "eu"),
+    }
+    quartered = {k: quartered[k] for k in QUARTERS}
+
+    def left_away(k, j):
+        columns = slice(j * features, (j + 1) * features)
+
         def run():
-            send(("tx", k), quartered[k][0].at[0:own], t_left.at[TURN[k], 0:own], x_peer)
+            send(("tx", k, j), quartered[k][0].at[0:own, columns], t_left.at[QUARTERS[k] + j, 0:own], x_peer)
 
         return run
 
-    def left_core(k):
+    def left_core(k, j):
+        place = QUARTERS[k] + j
+
         def run():
-            arrive(("tx", k))()
-            send(("tc", k), t_left.at[TURN[k], 0:own], t_left.at[TURN[k], own : 2 * own], core_peer)
+            arrive(("tx", k, j))()
+            send(("tc", k, j), t_left.at[place, 0:own], t_left.at[place, own : 2 * own], core_peer)
 
         return run
 
     def right_away(k, r):
-        columns = slice(r * half, (r + 1) * half)
+        place = QUARTERS[k] + r
 
         def run():
             for core in range(2):
                 begin = r * features + core * half + (1 - x) * quarter
-                t_out[TURN[k], :, r * half + core * quarter : r * half + (core + 1) * quarter] = quartered[k][1][
+                t_out[place, :, core * quarter : (core + 1) * quarter] = quartered[k][2][
                     0:own, pl.ds(pl.multiple_of(begin, quarter), quarter)
                 ]
-            send(("ty", k, r), t_out.at[TURN[k], :, columns], t_in.at[TURN[k], 0:own, columns], x_peer)
+            send(("ty", k, r), t_out.at[place], t_in.at[place, 0:own], x_peer)
 
         return run
 
     def right_core(k, r):
-        columns = slice(r * half, (r + 1) * half)
+        place = QUARTERS[k] + r
 
         def run():
             arrive(("ty", k, r))()
-            send(("td", k, r), t_in.at[TURN[k], 0:own, columns], t_in.at[TURN[k], own : 2 * own, columns], core_peer)
+            send(("td", k, r), t_in.at[place, 0:own], t_in.at[place, own : 2 * own], core_peer)
 
         return run
 
-    def outer_quarter(k, r):
+    def outer_quarter(k, j, r):
         def run():
-            left, right = quartered[k][:2]
+            left, _, right = quartered[k][:3]
             near = pl.ds(pl.multiple_of(r * features + c * half + x * quarter, quarter), quarter)
-            away = pl.ds(pl.multiple_of(r * half + c * quarter, quarter), quarter)
-            total = contract(left[...], right[:, near], 0, 0) + contract(t_left[TURN[k]], t_in[TURN[k], :, away], 0, 0)
-            g[spans[k][0] + r, :, pl.ds(pl.multiple_of(x * quarter, quarter), quarter)] = total.astype(LOW)
+            away = pl.ds(pl.multiple_of(c * quarter, quarter), quarter)
+            total = contract(left[:, j * features : (j + 1) * features], right[:, near], 0, 0)
+            total = total + contract(t_left[QUARTERS[k] + j], t_in[QUARTERS[k] + r, :, away], 0, 0)
+            g[spans[k][0] + j + r, :, plane_span] = total.astype(LOW)
 
         return run
 
-    for k, (_, _, left_dep, right_dep, left_got, right_got) in quartered.items():
-        plan.add(("tx", k), left_away(k), [left_dep], (), [(("tx", k), "x", lump)], 0.05, 2.5)
-        plan.add(("tw", k), left_core(k), [("tx", k)], [("tx", k)], [(("tc", k), "c", lump)], 0.05, 2.5)
-        plan.add(("got", "tc", k), arrive(("tc", k)), [("tw", k)], [("tc", k)], (), 0.02, 2.5)
-        for r in range(3):
+    for k, (_, lefts, _, rights, left_dep, right_dep, left_got, right_got) in quartered.items():
+        urgency = 2.6 if k == 0 else 2.5
+        for j in range(lefts):
+            plan.add(("tx", k, j), left_away(k, j), [left_dep] + list(AFTER.get(k, ())), (), [(("tx", k, j), "x", lump)], 0.05, urgency)
+            plan.add(("tw", k, j), left_core(k, j), [("tx", k, j)], [("tx", k, j)], [(("tc", k, j), "c", lump)], 0.05, urgency)
+            plan.add(("got", "tc", k, j), arrive(("tc", k, j)), [("tw", k, j)], [("tc", k, j)], (), 0.02, urgency)
+        for r in range(rights):
             plan.add(("ty", k, r), right_away(k, r), [right_dep], (), [(("ty", k, r), "x", lump // 2)], 0.05, 2.5)
             plan.add(("tz", k, r), right_core(k, r), [("ty", k, r)], [("ty", k, r)], [(("td", k, r), "c", lump // 2)], 0.05, 2.5)
             plan.add(("got", "td", k, r), arrive(("td", k, r)), [("tz", k, r)], [("td", k, r)], (), 0.02, 2.5)
-            deps = [("got", left_got), ("got", right_got), ("got", "tc", k), ("got", "td", k, r)]
-            plan.add(("gr", spans[k][0] + r), outer_quarter(k, r), deps, cost=0.4, rank=5)
+        for j in range(lefts):
+            for r in range(rights):
+                deps = [("got", left_got), ("got", right_got), ("got", "tc", k, j), ("got", "td", k, r)]
+                plan.add(("gr", spans[k][0] + j + r), outer_quarter(k, j, r), deps, cost=0.4, rank=5)
     weight_grads = []
     for r in range(3):
-        weight_grads.append((r, x_pool, r, d_pool, 0, [("got", "ep"), ("got", "ed1")]))
-    weight_grads.append((6, x_att, 0, d_res, 0, [("got", "ea"), ("got", "er")]))
+        for k, left, left_block, right, right_block, deps in (
+            (0, x_pool, r, d_pool, 0, ("ep", "ed1")), (1, x_norm, 0, d_qkv, r, ("en", "eq")),
+            (2, x_att, 0, d_res, 0, ("ea", "er")), (5, x_short, 0, d_up, r, ("es", "eu")),
+        ):
+            if k not in QUARTERS and r < sizes[k]:
+                deps = [("got", dep) for dep in deps]
+                weight_grads.append((spans[k][0] + r, left, left_block, right, right_block, deps))
     for block, left, left_block, right, right_block, deps in weight_grads:
         plan.add(("gr", block), outer(block, left, left_block, right, right_block), deps, cost=0.3, rank=5)
 
@@ -1311,8 +1336,7 @@
         away, span, away_span, length_out = blocks, slice(None), slice(None), half
         begin_out, away_out = c * half, c * half
         if quarters:
-            span = pl.ds(pl.multiple_of(x * quarter, quarter), quarter)
-            away_span = pl.ds(pl.multiple_of((1 - x) * quarter, quarter), quarter)
+            span, away_span = plane_span, plane_away
             length_out, begin_out, away_out = quarter, c * half + x * quarter, c * half + (1 - x) * quarter
         elif split:
             away = pl.ds(there, size)
@@ -1396,10 +1420,11 @@
             scatter_chunk(rank, name, ours + offset, theirs + offset, size, deps)
         else:
             begin = spans[k][0] + offset
-            scatter_chunk(rank, name, begin, begin if k in quartered else None, size, [("gr", begin + j) for j in range(size)])
+            scatter_chunk(rank, name, begin, begin if k in QUARTERS else None, size, [("gr", begin + j) for j in range(size)])
 
     for name, _ in plan.order():
         plan.tasks[name][0]()
+    assert len(boxes) <= RECEIVES
     for copy in started[-SENDS:]:
         copy.wait_send()
     for copy in outs:
@@ -1479,7 +1504,7 @@
         wide(micros, lane_units, lane_units), wide(micros, tok_rows, features), wide(micros, tok_rows, features),
         wide(micros, split, tok_rows, TILE), wide(micros, split, 8 + tok_rows, TILE), wide(micros, split, 8, TILE),
         low(2 * own, features), low(2 * own, FF),
-        low(2, 2 * own, features), low(2, own, 3 * half), low(2, 2 * own, 3 * half), low(blocks, features, half), low(4, blocks, rows, half), low(4, blocks, rows, half),
+        low(10, 2 * own, features), low(10, own, half), low(10, 2 * own, half), low(blocks, features, half), low(4, blocks, rows, half), low(4, blocks, rows, half),
         pieces(), pieces(), pieces(), pieces(), wide(48, features), wide(40, features),
         pltpu.SemaphoreType.DMA((SENDS,)), pltpu.SemaphoreType.DMA((RECEIVES,)), pltpu.SemaphoreType.DMA((5,)),
     ]
@@ -1503,7 +1528,7 @@
     )(
         owners, doc_lengths[:, 0], slopes, ln_gain, ln_bias, tokens[:, 0], cotangent[:, 0], master[0]
     )
-    steps = 4
+    steps = 2
     slot = pl.BlockSpec((slots // steps, rows, features), lambda j: (j, 0, 0))
     flat = (micros * tok_rows, features)
     some = pl.BlockSpec((flat[0] // steps, features), lambda j: (j, 0))

time: 117 us -> 113 us (0.966)
  Pallas kernels: 116 us -> 112 us
    pallas_call x1, Pallas kernels: 110 us -> 107 us  [fused_body(): pl.pallas_call(lambda *refs: main_kernel(dims, refs), out_shape=(jax.Shap...]
where the time goes in v5:
time: 113 us
  Pallas kernels  112 us (99%)
    pallas_call x1, Pallas kernels, fused_body(): pl.pallas_call(lambda *refs: main_kernel(dims, refs), out_shape=(jax.Shap...  107 us
    pallas_call x1, Pallas kernels, fused_body(): pl.pallas_call(lambda *refs: adam_kernel(sizes, refs), grid=(steps,), out...  5.13 us

profile of v5, /device:TPU:0, one launch (start us, length us, event | category | flops | bytes accessed | tf_op | source)
XLA Modules:
  0.0 113.0 jit_solution(15576940935450214002)
XLA Ops:
  0.6 107.1 %block.1 = (f32[2,144,512]{2,1,0:T(8,128)}, f32[2,144,512]{2,1,0:T(8,128)}, bf16[18,64,512]{2,1,0:T(8,128)(2,1)}, f32[8,512]{1,0:T(8,128)}) custom-call(s32[6]{0:T(128)} %refs_0_.3, s32[2,4]{1,0:T(2,128)} %bitcast.33, f32[8]{0:T(128)} %refs_2_.1, f32[2,512]{1,0:T(2,128)} %refs_3_.3, f32[2,512]{1,0:T(2,128)} %refs_4_.3, bf16[2,144,512]{2,1,0:T(8,128)(2,1)} %bitcast.30, ...), custom_call_target="tpu_custom_call" | custom-call | tf_op jit(solution)/shard_map/block/pallas_call | solution.py:1513
  107.8 5.1 %adam.1 = (f32[8,64,512]{2,1,0:T(8,128)}, f32[8,64,512]{2,1,0:T(8,128)}, f32[8,64,512]{2,1,0:T(8,128)}, bf16[8,64,512]{2,1,0:T(8,128)(2,1)}, f32[4,512]{1,0:T(4,...) custom-call(s32[6]{0:T(128)} %refs_0_.3, ...), custom_call_target="tpu_custom_call" | custom-call | tf_op jit(solution)/shard_map/adam/pallas_call | solution.py:1538

commit v6 on v5

--- a/solution.py
+++ b/solution.py
@@ -463,30 +463,32 @@
         return listed
 
 
-SLACK = 1.5
-SENDS, RECEIVES = 32, 168
+SLACK = 2.0
+SENDS, RECEIVES = 32, 180
 GATHERS = (
     (0, 0, 1, 0.0),
-    (0, 1, 1, 0.01),
-    (0, 2, 1, 0.02),
-    (1, 0, 1, 0.1),
-    (1, 1, 1, 0.11),
-    (1, 2, 1, 0.12),
-    (3, 0, 2, 0.2),
-    (3, 2, 2, 0.22),
-    (2, 0, 1, 0.3),
-    (5, 0, 3, 0.4),
+    (0, 1, 1, 0.07),
+    (0, 2, 1, 0.08),
+    (1, 0, 1, 0.21),
+    (1, 1, 1, 0.21),
+    (1, 2, 1, 0.21),
+    (3, 0, 2, 0.31),
+    (3, 2, 2, 0.33),
+    (2, 0, 1, 0.43),
+    (5, 0, 3, 0.37),
 )
 QUARTERS = {5: 0, 1: 3, 0: 6}
-GATHER_QUARTERS = ()
 AFTER = {}
+WHOLE = ()
 SCATTERS = (
-    (5, 0, 3, 1.0),
-    (3, 0, 2, 1.1),
-    (3, 2, 2, 1.2),
-    (2, 0, 1, 1.3),
-    (0, 0, 3, 0.7),
-    (1, 0, 3, 0.8),
+    (5, 0, 3, 0.93),
+    (3, 0, 2, 1.01),
+    (3, 2, 2, 0.93),
+    (2, 0, 1, 1.26),
+    (0, 0, 1, 0.43),
+    (0, 1, 1, 0.43),
+    (0, 2, 1, 0.43),
+    (1, 0, 3, 0.6),
 )
 LINKS = {
     "c": (400e3, 1.0),
@@ -528,7 +530,7 @@
         w, masters, mine, other, core_in, both, x_in, tok, cot, tail_in, wide_tok, wide_cot, x_pool, x_norm, x_att,
         x_two, x_act, x_short, d_up, d_low, d_inner, d_res, d_qkv, d_pool, pooled, hat_one, hat_two, root_one, root_two,
         resid, hidden, short_grad, res_grad, q_out, q_in, a_out, a_in, da_out, da_in, dq_out, dq_in, probs, mixed, grad,
-        wide_up, wide_grad, edge_in, x_near, x_wide, t_left, t_out, t_in, g, right_in, left_in, fin_out, fin_in, co_out, co_in, sums, sums_in, sends, recvs, local,
+        wide_up, wide_grad, edge_in, x_near, x_wide, t_left, t_out, t_in, u_out, u_in, dx_out, dx_in, g, right_in, left_in, fin_out, fin_in, co_out, co_in, sums, sums_in, sends, recvs, local,
     ) = refs[12:]
     half = features // 2
     width = features // heads
@@ -556,6 +558,7 @@
     other_half = pl.ds(pl.multiple_of((1 - c) * half, half), half)
     core_peer = (x * 2 + 1 - c, s)
     x_peer = ((1 - x) * 2 + c, s)
+    cross_peer = ((1 - x) * 2 + 1 - c, s)
     right_peer = (b, seq_of(at(1)))
     left_peer = (b, seq_of(at(-1)))
     plan = Plan()
@@ -599,9 +602,9 @@
         pl.semaphore_signal(
             barrier, inc=1, device_id=(b, lax.rem(s + step, count)), device_id_type=MESH
         )
-    for device in (core_peer, x_peer):
+    for device in (core_peer, x_peer, cross_peer):
         pl.semaphore_signal(barrier, inc=1, device_id=device, device_id_type=MESH)
-    pl.semaphore_wait(barrier, count + 1)
+    pl.semaphore_wait(barrier, count + 2)
 
     spans, first = [], 0
     for size in sizes:
@@ -643,8 +646,8 @@
             have[3] += [("h", name), ("hy", name)]
         else:
             begin = spans[k][0] + offset
-            gathers.append((rank, name, (k,), begin, begin if k in GATHER_QUARTERS else None, size))
-            have[k] += [("h", name)] + ([("hy", name)] if k in GATHER_QUARTERS else [])
+            gathers.append((rank, name, (k,), begin, begin if k == 5 else None, size))
+            have[k] += [("h", name)]
     piece_bytes = rows_of * half * 2
 
     quarter = half // 2
@@ -652,7 +655,8 @@
     plane_away = pl.ds(pl.multiple_of((1 - x) * quarter, quarter), quarter)
 
     def gather_chunk(rank, name, parents, here, there, size):
-        split, quarters = there is not None, there is here
+        quarters = there is here
+        split = there is not None and not quarters
         load = size * piece_bytes // (2 if quarters else 1)
         blocks = pl.ds(here, size)
         away = pl.ds(there, size) if split else blocks
@@ -960,23 +964,35 @@
         pltpu.make_async_copy(grad, grad_hbm, local.at[4]),
     ]
 
+    def place_up(r, value, core, plane):
+        for micro in range(micros):
+            wide_up[micro, 2 * core + plane, pl.ds(r, units, stride=3), :] = value[micro * units : (micro + 1) * units]
+
+    def lift_away():
+        for r in range(3):
+            for core in range(2):
+                value = contract(t_left[QUARTERS[5], 0:own], w[up_base + r, core, :, plane_span], 1, 0)
+                u_out[:, (2 * r + core) * quarter : (2 * r + core + 1) * quarter] = value.astype(LOW)
+        send("ux", u_out, u_in, x_peer)
+
     def lift(r):
         def run():
-            for h in range(2):
-                value = contract(x_short[0:own], w[up_base + r, h], 1, 0)
-                for micro in range(micros):
-                    for tile in range(half // TILE):
-                        wide_up[micro, h * (half // TILE) + tile, pl.ds(r, units, stride=3), :] = value[
-                            micro * units : (micro + 1) * units, columns_at(tile)
-                        ]
-            if r == 2:
-                for micro in range(micros):
-                    for tile in tiles:
-                        columns = columns_at(tile)
-                        mixed[micro, :, columns] = tok[micro, :, columns].astype(WIDE) + wide_up[micro, tile]
-                outs[0].start()
+            for core in range(2):
+                place_up(r, contract(x_short[0:own], w[up_base + r, core, :, plane_span], 1, 0), core, x)
 
         return run
+
+    def finish_mixed():
+        arrive("ux")()
+        for r in range(3):
+            for core in range(2):
+                begin = (2 * r + core) * quarter
+                place_up(r, u_in[:, begin : begin + quarter].astype(WIDE), core, 1 - x)
+        for micro in range(micros):
+            for tile in tiles:
+                columns = columns_at(tile)
+                mixed[micro, :, columns] = tok[micro, :, columns].astype(WIDE) + wide_up[micro, tile]
+        outs[0].start()
 
     plan.add("po", pool, ["pc", *have[0]], (), [shared("en", features)], 0.6, rank=3)
     plan.add("pr", project, ["po", *have[1]], (), spread_sends("q", 3 * units), 0.6, rank=3)
@@ -994,17 +1010,33 @@
         rank=3,
     )
     for r in range(3):
-        plan.add(
-            ("li", r), lift(r), ["na", *have[5], "tok"] + ([("li", i) for i in range(r)]), (), (), 0.3, rank=8
-        )
-
-    def back_short():
+        plan.add(("li", r), lift(r), ["na", *have[5]], (), (), 0.2, rank=8)
+    quarter_lump = own * 3 * half * 2
+    plan.add("lq", lift_away, [("tw", 5, 0), *have[5]], (), [("ux", "x", quarter_lump)], 0.6, rank=8)
+    plan.add("lf", finish_mixed, ["lq", "tok"] + [("li", r) for r in range(3)], ["ux"], (), 0.4, rank=8)
+
+    def back_short_away():
         total = None
         for r in range(3):
-            for h in range(2):
-                begin = r * features + h * half
-                term = contract(d_up[0:own, begin : begin + half], w[up_base + r, h], 1, 1)
+            for core in range(2):
+                columns = slice(core * quarter, (core + 1) * quarter)
+                term = contract(t_in[QUARTERS[5] + r, 0:own, columns], w[up_base + r, core, :, plane_span], 1, 1)
                 total = term if total is None else total + term
+        dx_out[...] = total.astype(LOW)
+        send("dx", dx_out, dx_in, x_peer)
+
+    def back_short_here():
+        total = None
+        for r in range(3):
+            for core in range(2):
+                columns = pl.ds(pl.multiple_of(r * features + core * half + x * quarter, quarter), quarter)
+                term = contract(d_up[0:own, columns], w[up_base + r, core, :, plane_span], 1, 1)
+                total = term if total is None else total + term
+        short_grad[...] = total
+
+    def back_short():
+        arrive("dx")()
+        total = short_grad[...] + dx_in[...].astype(WIDE)
         short_grad[...] = total
         d_low[0:own] = total.astype(LOW)
         exchange("el", d_low)
@@ -1127,7 +1159,11 @@
                 grad[micro, :, columns] = cot[micro, :, columns].astype(WIDE) + wide_grad[micro, tile, 8 : 8 + tokens]
         outs[1].start()
 
-    plan.add("bs", back_short, ["cot", *have[5]], (), [shared("el", features)], 0.65, rank=4)
+    plan.add(
+        "bq", back_short_away, [("tz", 5, r) for r in range(3)] + have[5], (), [("dx", "x", own * features * 2)], 0.6, rank=2
+    )
+    plan.add("bh", back_short_here, ["cot", *have[5]], (), (), 0.6, rank=3)
+    plan.add("bs", back_short, ["bq", "bh"], ["dx"], [shared("el", features)], 0.1, rank=3)
     for j in range(hidden_blocks):
         last = j == hidden_blocks - 1
         plan.add(
@@ -1279,7 +1315,12 @@
                 t_out[place, :, core * quarter : (core + 1) * quarter] = quartered[k][2][
                     0:own, pl.ds(pl.multiple_of(begin, quarter), quarter)
                 ]
-            send(("ty", k, r), t_out.at[place], t_in.at[place, 0:own], x_peer)
+            if k == 5:
+                send(("ty", k, r), t_out.at[place], t_in.at[place, 0:own], x_peer)
+                return
+            lanes = [pl.ds(pl.multiple_of(core * quarter, quarter), quarter) for core in (c, 1 - c)]
+            send(("ty", k, r), t_out.at[place, :, lanes[0]], t_in.at[place, 0:own, 0:quarter], x_peer, ("ty", k, r))
+            send(("tu", k, r), t_out.at[place, :, lanes[1]], t_in.at[place, own : 2 * own, 0:quarter], cross_peer, ("ty", k, r))
 
         return run
 
@@ -1296,7 +1337,7 @@
         def run():
             left, _, right = quartered[k][:3]
             near = pl.ds(pl.multiple_of(r * features + c * half + x * quarter, quarter), quarter)
-            away = pl.ds(pl.multiple_of(c * quarter, quarter), quarter)
+            away = pl.ds(pl.multiple_of(c * quarter, quarter), quarter) if k == 5 else slice(0, quarter)
             total = contract(left[:, j * features : (j + 1) * features], right[:, near], 0, 0)
             total = total + contract(t_left[QUARTERS[k] + j], t_in[QUARTERS[k] + r, :, away], 0, 0)
             g[spans[k][0] + j + r, :, plane_span] = total.astype(LOW)
@@ -1304,16 +1345,23 @@
         return run
 
     for k, (_, lefts, _, rights, left_dep, right_dep, left_got, right_got) in quartered.items():
-        urgency = 2.6 if k == 0 else 2.5
+        urgency = 3.5 if k == 0 else 2.5
         for j in range(lefts):
             plan.add(("tx", k, j), left_away(k, j), [left_dep] + list(AFTER.get(k, ())), (), [(("tx", k, j), "x", lump)], 0.05, urgency)
             plan.add(("tw", k, j), left_core(k, j), [("tx", k, j)], [("tx", k, j)], [(("tc", k, j), "c", lump)], 0.05, urgency)
             plan.add(("got", "tc", k, j), arrive(("tc", k, j)), [("tw", k, j)], [("tc", k, j)], (), 0.02, urgency)
         for r in range(rights):
+            if k != 5:
+                parts = [("ty", k, r), ("tu", k, r)]
+                whole = t_in.at[QUARTERS[k] + r, :, 0:quarter]
+                plan.add(parts[0], right_away(k, r), [right_dep], (), [(p, "x", lump // 4) for p in parts], 0.1, 2.5)
+                take = lambda k=k, r=r, whole=whole: gather_up(("ty", k, r), whole)
+                plan.add(("got", "td", k, r), take, parts[:1], parts, (), 0.02, 2.5)
+                continue
             plan.add(("ty", k, r), right_away(k, r), [right_dep], (), [(("ty", k, r), "x", lump // 2)], 0.05, 2.5)
             plan.add(("tz", k, r), right_core(k, r), [("ty", k, r)], [("ty", k, r)], [(("td", k, r), "c", lump // 2)], 0.05, 2.5)
             plan.add(("got", "td", k, r), arrive(("td", k, r)), [("tz", k, r)], [("td", k, r)], (), 0.02, 2.5)
-        for j in range(lefts):
+        for j in range(lefts if k not in WHOLE else 0):
             for r in range(rights):
                 deps = [("got", left_got), ("got", right_got), ("got", "tc", k, j), ("got", "td", k, r)]
                 plan.add(("gr", spans[k][0] + j + r), outer_quarter(k, j, r), deps, cost=0.4, rank=5)
@@ -1323,7 +1371,7 @@
             (0, x_pool, r, d_pool, 0, ("ep", "ed1")), (1, x_norm, 0, d_qkv, r, ("en", "eq")),
             (2, x_att, 0, d_res, 0, ("ea", "er")), (5, x_short, 0, d_up, r, ("es", "eu")),
         ):
-            if k not in QUARTERS and r < sizes[k]:
+            if (k in WHOLE or k not in QUARTERS) and r < sizes[k]:
                 deps = [("got", dep) for dep in deps]
                 weight_grads.append((spans[k][0] + r, left, left_block, right, right_block, deps))
     for block, left, left_block, right, right_block, deps in weight_grads:
@@ -1374,15 +1422,18 @@
             total = total + right_in[3, blocks, :, span].astype(WIDE) + left_in[3, blocks, :, span].astype(WIDE)
             fin_out[blocks, :, span] = total.astype(LOW)
             send(("rx", name), fin_out.at[blocks, :, span], fin_in.at[blocks, :, span], x_peer)
+            if quarters:
+                send(("rd", name), fin_out.at[blocks, :, span], co_in.at[blocks, :, span], cross_peer)
             if split:
+                send(("rc", name), fin_out.at[blocks, :, span], co_in.at[blocks, :, span], core_peer)
                 red[blocks, :, out_span] = fin_out[blocks, :, span]
-                send(("rc", name), fin_out.at[blocks, :, span], co_in.at[blocks, :, span], core_peer)
 
         def finish_x():
             arrive(("rx", name))()
             if split:
                 red[away, :, out_away] = fin_in[away, :, away_span]
-                send(("rd", name), fin_in.at[away, :, away_span], co_in.at[away, :, away_span], core_peer)
+                if not quarters:
+                    send(("rd", name), fin_in.at[away, :, away_span], co_in.at[away, :, away_span], core_peer)
             else:
                 total = (fin_out[blocks].astype(WIDE) + fin_in[blocks].astype(WIDE)).astype(LOW)
                 co_out[blocks] = total
@@ -1405,9 +1456,10 @@
         own_out = [(("rc", name), "c", load)]
         plan.add(
             ("fi", name), finish, [("r", 4, name)], [("R", "s", 4, name), ("L", "s", 4, name)],
-            [(("rx", name), "x", load)] + (own_out if split else []), 0.02 * size, rank,
-        )
-        late_out = [(("rd", name), "c", load)] if split else own_out
+            [(("rx", name), "x", load)] + (own_out if split else []) + ([(("rd", name), "x", load)] if quarters else []),
+            0.02 * size, rank,
+        )
+        late_out = ([] if quarters else [(("rd", name), "c", load)]) if split else own_out
         plan.add(("fx", name), finish_x, [("fi", name)], [("rx", name)], late_out, 0.02 * size, rank)
         plan.add(
             ("fc", name), finish_core, [("fx", name)], [("rc", name)] + ([("rd", name)] if split else []), (), 0.02 * size, rank
@@ -1420,7 +1472,7 @@
             scatter_chunk(rank, name, ours + offset, theirs + offset, size, deps)
         else:
             begin = spans[k][0] + offset
-            scatter_chunk(rank, name, begin, begin if k in QUARTERS else None, size, [("gr", begin + j) for j in range(size)])
+            scatter_chunk(rank, name, begin, begin if k in QUARTERS and k not in WHOLE else None, size, [("gr", begin + j) for j in range(size)])
 
     for name, _ in plan.order():
         plan.tasks[name][0]()
@@ -1504,7 +1556,8 @@
         wide(micros, lane_units, lane_units), wide(micros, tok_rows, features), wide(micros, tok_rows, features),
         wide(micros, split, tok_rows, TILE), wide(micros, split, 8 + tok_rows, TILE), wide(micros, split, 8, TILE),
         low(2 * own, features), low(2 * own, FF),
-        low(10, 2 * own, features), low(10, own, half), low(10, 2 * own, half), low(blocks, features, half), low(4, blocks, rows, half), low(4, blocks, rows, half),
+        low(10, 2 * own, features), low(10, own, half), low(10, 2 * own, half),
+        low(own, 3 * half), low(own, 3 * half), low(own, features), low(own, features), low(blocks, features, half), low(4, blocks, rows, half), low(4, blocks, rows, half),
         pieces(), pieces(), pieces(), pieces(), wide(48, features), wide(40, features),
         pltpu.SemaphoreType.DMA((SENDS,)), pltpu.SemaphoreType.DMA((RECEIVES,)), pltpu.SemaphoreType.DMA((5,)),
     ]

time: 113 us -> 112 us (level)
  no operation moved by 1% of the time
where the time goes in v6:
time: 112 us
  Pallas kernels  111 us (99%)
    pallas_call x1, Pallas kernels, fused_body(): pl.pallas_call(lambda *refs: main_kernel(dims, refs), out_shape=(jax.Shap...  106 us
    pallas_call x1, Pallas kernels, fused_body(): pl.pallas_call(lambda *refs: adam_kernel(sizes, refs), grid=(steps,), out...  5.13 us

profile of v6, /device:TPU:0, one launch (start us, length us, event | category | flops | bytes accessed | tf_op | source)
XLA Modules:
  0.0 112.2 jit_solution(13244114469355117433)
XLA Ops:
  0.6 106.3 %block.1 = (f32[2,144,512]{2,1,0:T(8,128)}, f32[2,144,512]{2,1,0:T(8,128)}, bf16[18,64,512]{2,1,0:T(8,128)(2,1)}, f32[8,512]{1,0:T(8,128)}) custom-call(s32[6]{0:T(128)} %refs_0_.3, s32[2,4]{1,0:T(2,128)} %bitcast.33, f32[8]{0:T(128)} %refs_2_.1, f32[2,512]{1,0:T(2,128)} %refs_3_.3, f32[2,512]{1,0:T(2,128)} %refs_4_.3, bf16[2,144,512]{2,1,0:T(8,128)(2,1)} %bitcast.30, ...), custom_call_target="tpu_custom_call" | custom-call | tf_op jit(solution)/shard_map/block/pallas_call | solution.py:1566
  106.9 5.1 %adam.1 = (f32[8,64,512]{2,1,0:T(8,128)}, f32[8,64,512]{2,1,0:T(8,128)}, f32[8,64,512]{2,1,0:T(8,128)}, bf16[8,64,512]{2,1,0:T(8,128)(2,1)}, f32[4,512]{1,0:T(4,...) custom-call(s32[6]{0:T(128)} %refs_0_.3, ...), custom_call_target="tpu_custom_call" | custom-call | tf_op jit(solution)/shard_map/adam/pallas_call | solution.py:1591

commit v7 on v6

--- a/solution.py
+++ b/solution.py
@@ -524,14 +524,16 @@
 
 def main_kernel(dims, refs):
     units, features, hidden_width, heads, micros, sizes = dims
-    owners, docs, slopes, gain, bias, tok_hbm, cot_hbm, master_hbm = refs[:8]
-    mixed_hbm, grad_hbm, red, small = refs[8:12]
+    tables, (tok_hbm, cot_hbm, master_hbm, first_hbm, second_hbm) = refs[:10], refs[10:15]
+    mixed_hbm, grad_hbm, slot_grads, small, masters, firsts, seconds = refs[15:22]
+    held = refs[22:32]
+    owners, docs, slopes, gain, bias, norm_m, norm_v, slope_row, slope_m, slope_v = held
     (
-        w, masters, mine, other, core_in, both, x_in, tok, cot, tail_in, wide_tok, wide_cot, x_pool, x_norm, x_att,
+        w, red, mine, other, core_in, both, x_in, tok, cot, tail_in, wide_tok, wide_cot, x_pool, x_norm, x_att,
         x_two, x_act, x_short, d_up, d_low, d_inner, d_res, d_qkv, d_pool, pooled, hat_one, hat_two, root_one, root_two,
         resid, hidden, short_grad, res_grad, q_out, q_in, a_out, a_in, da_out, da_in, dq_out, dq_in, probs, mixed, grad,
         wide_up, wide_grad, edge_in, x_near, x_wide, t_left, t_out, t_in, u_out, u_in, dx_out, dx_in, g, right_in, left_in, fin_out, fin_in, co_out, co_in, sums, sums_in, sends, recvs, local,
-    ) = refs[12:]
+    ) = refs[32:]
     half = features // 2
     width = features // heads
     rows_of = masters.shape[1]
@@ -595,8 +597,14 @@
         pltpu.make_async_copy(tok_hbm, tok, local.at[1]),
         pltpu.make_async_copy(cot_hbm, cot, local.at[2]),
     ]
+    for table, place in zip(tables, held):
+        loads.append(pltpu.make_async_copy(table, place, local.at[len(loads) + 2]))
     for copy in loads:
         copy.start()
+    moments = [
+        pltpu.make_async_copy(first_hbm, firsts, local.at[15]),
+        pltpu.make_async_copy(second_hbm, seconds, local.at[16]),
+    ]
     barrier = pltpu.get_barrier_semaphore()
     for step in range(1, count):
         pl.semaphore_signal(
@@ -605,6 +613,8 @@
     for device in (core_peer, x_peer, cross_peer):
         pl.semaphore_signal(barrier, inc=1, device_id=device, device_id_type=MESH)
     pl.semaphore_wait(barrier, count + 2)
+    for copy in loads[3:]:
+        copy.wait()
 
     spans, first = [], 0
     for size in sizes:
@@ -1182,6 +1192,33 @@
     plan.add("bx", back_pieces, ["b1"], (), [("ed", "f", 2 * 8 * features * 4)], 0.65, rank=9)
     plan.add("fg", finish_grad, ["bx", "cot"], ["ed"], (), 0.3, rank=9)
 
+    fixes = (1.0 - beta_one**STEP, 1.0 - beta_two**STEP)
+
+    def finish_small(total):
+        for begin, values in ((0, gain), (2, bias)):
+            rows = slice(begin, begin + 2)
+            new = adam_update(values[...], total[rows], norm_m[rows], norm_v[rows], *fixes, rate_norm, 0.0)
+            for place, value in enumerate(new):
+                small[4 * place + begin : 4 * place + begin + 2] = value
+        new = adam_update(slope_row[...], total[4:5, 0:heads], slope_m[...], slope_v[...], *fixes, rate_slope, 0.0)
+        for place, value in enumerate(new):
+            small[12 + place : 13 + place, 0:heads] = value
+
+    def fill_slots():
+        lanes = lax.broadcasted_iota(jnp.int32, (1, features), 1)
+        marks = jnp.zeros((1, features), WIDE)
+        for slot in range(masters.shape[0]):
+            block, mark, base = jnp.int32(0), jnp.float32(0), 0
+            for matrix_id, size in enumerate(sizes):
+                begin = start_of(owners, matrix_id, sizes)
+                inside = (owners[matrix_id] == b) & (slot >= begin) & (slot < begin + size)
+                block = jnp.where(inside, base + slot - begin, block)
+                mark = jnp.where(inside, 1.0, mark)
+                base += size
+            slot_grads[slot] = red[block]
+            marks = jnp.where(lanes == slot, mark, marks)
+        small[15:16, :] = marks
+
     def add_pair(step, device):
         def run():
             if step > 0:
@@ -1190,7 +1227,7 @@
             if device is not None:
                 send(("s", step), sums.at[8 * step : 8 * step + 8], sums_in.at[8 * step : 8 * step + 8], device)
             else:
-                small[...] = sums[8 * step : 8 * step + 8]
+                finish_small(sums[8 * step : 8 * step + 8])
 
         return run
 
@@ -1474,58 +1511,45 @@
             begin = spans[k][0] + offset
             scatter_chunk(rank, name, begin, begin if k in QUARTERS and k not in WHOLE else None, size, [("gr", begin + j) for j in range(size)])
 
+    plan.add("mo", lambda: [copy.start() for copy in moments], ["pc"], (), (), 0.02, rank=8)
+    plan.add("sl", fill_slots, ["mo"] + [("fc", ("g", k, offset)) for k, offset, _, _ in SCATTERS], (), (), 0.2, rank=9)
     for name, _ in plan.order():
         plan.tasks[name][0]()
     assert len(boxes) <= RECEIVES
     for copy in started[-SENDS:]:
         copy.wait_send()
-    for copy in outs:
+    for copy in outs + moments:
         copy.wait()
 
 
-def adam_kernel(sizes, refs):
-    owners, red, small, gain, bias, norm_m, norm_v, slope, slope_m, slope_v, master, first, second, mixed, grad = refs[:15]
-    (
-        new_w, new_m, new_v, new_low, norm_out, norm_m_out, norm_v_out, slope_out, slope_m_out, slope_v_out, mixed_out,
-        grad_out,
-    ) = refs[15:]
+def adam_kernel(refs):
+    grads, small, master, first, second, mixed, grad = refs[:7]
+    new_w, new_m, new_v, new_low, mixed_out, grad_out = refs[7:13]
+    norm_outs, slope_outs = refs[13:16], refs[16:19]
     step = pl.program_id(0)
-    fix_first = 1.0 - beta_one**STEP
-    fix_second = 1.0 - beta_two**STEP
-    mixed_out[...] = mixed[...]
-    grad_out[...] = grad[...]
+    fixes = (1.0 - beta_one**STEP, 1.0 - beta_two**STEP)
+    rows = mixed_out.shape[0]
+    part = pl.ds(pl.multiple_of(step * rows, 8), rows)
+    mixed_out[...] = mixed[part]
+    grad_out[...] = grad[part]
 
     @pl.when(step == 0)
     def _():
-        for begin, values in ((0, gain), (2, bias)):
-            rows = slice(begin, begin + 2)
-            norm_out[rows], norm_m_out[rows], norm_v_out[rows] = adam_update(
-                values[...], small[rows], norm_m[rows], norm_v[rows], fix_first, fix_second, rate_norm, 0.0
-            )
-        heads = slope.shape[1]
-        slope_out[...], slope_m_out[...], slope_v_out[...] = adam_update(
-            slope[...], small[4:5, 0:heads], slope_m[...], slope_v[...], fix_first, fix_second, rate_slope, 0.0
-        )
-
-    me = lax.axis_index("batch")
-    for place in range(master.shape[0]):
-        slot = step * master.shape[0] + place
-        block, held, base = jnp.int32(0), jnp.int32(0), 0
-        for matrix_id, size in enumerate(sizes):
-            begin = start_of(owners, matrix_id, sizes)
-            inside = (owners[matrix_id] == me) & (slot >= begin) & (slot < begin + size)
-            block = jnp.where(inside, base + slot - begin, block)
-            held = jnp.where(inside, 1, held)
-            base += size
-        gradient = red[block].astype(WIDE)
-        values = adam_update(
-            master[place], gradient, first[place], second[place], fix_first, fix_second, rate_matrix, decay_rate
-        )
-        keep = jnp.full(gradient.shape, held, jnp.int32) > 0
-        weight = jnp.where(keep, values[0], master[place])
+        heads = slope_outs[0].shape[1]
+        for place in range(3):
+            norm_outs[place][...] = small[4 * place : 4 * place + 4]
+            slope_outs[place][...] = small[12 + place : 13 + place, 0:heads]
+
+    count = new_w.shape[0]
+    lanes = lax.broadcasted_iota(jnp.int32, (1, small.shape[1]), 1)
+    for place in range(count):
+        slot = step * count + place
+        old = (master[slot], first[slot], second[slot])
+        values = adam_update(old[0], grads[slot].astype(WIDE), old[1], old[2], *fixes, rate_matrix, decay_rate)
+        mark = jnp.sum(jnp.where(lanes == slot, small[15:16, :], 0.0), axis=1, keepdims=True)
+        keep = jnp.broadcast_to(mark, old[0].shape) > 0.5
+        weight, new_m[place], new_v[place] = (jnp.where(keep, new, was) for new, was in zip(values, old))
         new_w[place] = weight
-        new_m[place] = jnp.where(keep, values[1], first[place])
-        new_v[place] = jnp.where(keep, values[2], second[place])
         new_low[place] = weight.astype(LOW)
 
 
@@ -1537,13 +1561,16 @@
     slots, rows = master.shape[1], master.shape[2]
     lane_units = units * heads
     split = features // TILE
-    hbm, vmem, smem = (pl.BlockSpec(memory_space=m) for m in (pl.ANY, pltpu.VMEM, pltpu.SMEM))
+    hbm, vmem, anywhere = (pl.BlockSpec(memory_space=m) for m in (pltpu.HBM, pltpu.VMEM, pl.ANY))
     low = lambda *shape: pltpu.VMEM(shape, LOW)
     wide = lambda *shape: pltpu.VMEM(shape, WIDE)
     pieces = lambda: low(blocks, rows, half)
     both = lambda columns: low(2 * own, columns)
     scratch = [
-        low(blocks, 2, features, half), wide(slots, rows, features), pieces(), pieces(), pieces(), pieces(), pieces(),
+        pltpu.SMEM(owners.shape, jnp.int32), pltpu.SMEM((micros, doc_lengths.shape[2]), jnp.int32),
+        pltpu.SMEM(slopes.shape, WIDE), wide(2, features), wide(2, features), wide(4, features), wide(4, features),
+        wide(1, heads), wide(1, heads), wide(1, heads),
+        low(blocks, 2, features, half), low(blocks, rows, features), pieces(), pieces(), pieces(), pieces(), pieces(),
         low(micros, tok_rows, features), low(micros, tok_rows, features), low(micros, 16, features),
         wide(micros, split, 16 + tok_rows, TILE), wide(micros, split, tok_rows, TILE),
         both(3 * features), both(features), both(features), both(features), both(FF), both(features),
@@ -1559,53 +1586,51 @@
         low(10, 2 * own, features), low(10, own, half), low(10, 2 * own, half),
         low(own, 3 * half), low(own, 3 * half), low(own, features), low(own, features), low(blocks, features, half), low(4, blocks, rows, half), low(4, blocks, rows, half),
         pieces(), pieces(), pieces(), pieces(), wide(48, features), wide(40, features),
-        pltpu.SemaphoreType.DMA((SENDS,)), pltpu.SemaphoreType.DMA((RECEIVES,)), pltpu.SemaphoreType.DMA((5,)),
+        pltpu.SemaphoreType.DMA((SENDS,)), pltpu.SemaphoreType.DMA((RECEIVES,)), pltpu.SemaphoreType.DMA((17,)),
     ]
     token_shape = (micros, tok_rows, features)
     dims = (units, features, FF, heads, micros, sizes)
-    mixed, grad, red, small = pl.pallas_call(
+    moment_shape = jax.ShapeDtypeStruct((slots, rows, features), WIDE)
+    mixed, grad, grads, small, weights, firsts, seconds = pl.pallas_call(
         lambda *refs: main_kernel(dims, refs),
         out_shape=(
             jax.ShapeDtypeStruct(token_shape, WIDE),
             jax.ShapeDtypeStruct(token_shape, WIDE),
-            jax.ShapeDtypeStruct((blocks, rows, features), LOW),
-            jax.ShapeDtypeStruct((8, features), WIDE),
+            jax.ShapeDtypeStruct((slots, rows, features), LOW),
+            jax.ShapeDtypeStruct((16, features), WIDE),
+            moment_shape, moment_shape, moment_shape,
         ),
-        in_specs=[smem, smem, smem, vmem, vmem, hbm, hbm, hbm],
-        out_specs=(hbm, hbm, vmem, vmem),
+        in_specs=[hbm] * 15,
+        out_specs=(anywhere, anywhere) + (vmem,) * 5,
         scratch_shapes=scratch,
         compiler_params=pltpu.CompilerParams(
-            collective_id=0, has_side_effects=True, vmem_limit_bytes=60 * 2**20
+            collective_id=0, has_side_effects=True, vmem_limit_bytes=47 * 2**20
         ),
         name="block",
-    )(
-        owners, doc_lengths[:, 0], slopes, ln_gain, ln_bias, tokens[:, 0], cotangent[:, 0], master[0]
-    )
+    )(*[pltpu.with_memory_space_constraint(value, pltpu.HBM) for value in (
+        owners, doc_lengths[:, 0], slopes, ln_gain, ln_bias, norm_m, norm_v, slopes[None], slope_m[None], slope_v[None],
+        tokens[:, 0], cotangent[:, 0], master[0], first_moment[0], second_moment[0],
+    )])
     steps = 2
+    flat = (micros * tok_rows, features)
     slot = pl.BlockSpec((slots // steps, rows, features), lambda j: (j, 0, 0))
-    flat = (micros * tok_rows, features)
     some = pl.BlockSpec((flat[0] // steps, features), lambda j: (j, 0))
-    moment_shape = jax.ShapeDtypeStruct((slots, rows, features), WIDE)
     norm_shape = jax.ShapeDtypeStruct((4, features), WIDE)
     slope_shape = jax.ShapeDtypeStruct((1, heads), WIDE)
     out = pl.pallas_call(
-        lambda *refs: adam_kernel(sizes, refs),
+        lambda *refs: adam_kernel(refs),
         grid=(steps,),
         out_shape=(
             moment_shape, moment_shape, moment_shape, jax.ShapeDtypeStruct((slots, rows, features), LOW),
+            jax.ShapeDtypeStruct(flat, WIDE), jax.ShapeDtypeStruct(flat, WIDE),
             norm_shape, norm_shape, norm_shape, slope_shape, slope_shape, slope_shape,
-            jax.ShapeDtypeStruct(flat, WIDE), jax.ShapeDtypeStruct(flat, WIDE),
         ),
-        in_specs=[smem] + [vmem] * 9 + [slot] * 3 + [some] * 2,
-        out_specs=(slot, slot, slot, slot, vmem, vmem, vmem, vmem, vmem, vmem, some, some),
-        compiler_params=pltpu.CompilerParams(dimension_semantics=("arbitrary",)),
+        in_specs=[vmem] * 7,
+        out_specs=(slot, slot, slot, slot, some, some) + (vmem,) * 6,
+        compiler_params=pltpu.CompilerParams(dimension_semantics=("arbitrary",), vmem_limit_bytes=12 * 2**20),
         name="adam",
-    )(
-        owners, red, small, ln_gain, ln_bias, norm_m, norm_v, slopes[None], slope_m[None],
-        slope_v[None], master[0], first_moment[0], second_moment[0],
-        mixed.reshape(flat), grad.reshape(flat),
-    )
-    new_w, new_m, new_v, new_low, norm, norm_m, norm_v, slope, slope_m, slope_v, mixed, grad = out
+    )(grads, small, weights, firsts, seconds, mixed.reshape(flat), grad.reshape(flat))
+    new_w, new_m, new_v, new_low, mixed, grad, norm, norm_m, norm_v, slope, slope_m, slope_v = out
     return (
         mixed.reshape(tokens.shape), grad.reshape(tokens.shape), new_w[None], new_m[None], new_v[None], new_low[None], norm, norm_m, norm_v,
         slope[0], slope_m[0], slope_v[0],

time: 112 us -> 109 us (0.973)
  Pallas kernels: 111 us -> 108 us
    pallas_call x1, Pallas kernels: 5.13 us -> 2.87 us  [fused_body(): pl.pallas_call(lambda *refs: adam_kernel(refs), grid=(steps,), out_shape=...]
    pallas_call x1, Pallas kernels: 106 us -> 105 us  [fused_body(): pl.pallas_call(lambda *refs: main_kernel(dims, refs), out_shape=(jax.Shap...]
where the time goes in v7:
time: 109 us; the launch traced here: 108 us
  Pallas kernels  108 us (99%)
    pallas_call x1, Pallas kernels, fused_body(): pl.pallas_call(lambda *refs: main_kernel(dims, refs), out_shape=(jax.Shap...  105 us
    pallas_call x1, Pallas kernels, fused_body(): pl.pallas_call(lambda *refs: adam_kernel(refs), grid=(steps,), out_shape=...  2.87 us

profile of v7, /device:TPU:0, one launch (start us, length us, event | category | flops | bytes accessed | tf_op | source)
XLA Modules:
  0.0 108.4 jit_solution(12755578853138719100)
XLA Ops:
  0.6 104.7 %block.1 = (f32[2,144,512]{2,1,0:T(8,128)S(1)}, f32[2,144,512]{2,1,0:T(8,128)S(1)}, bf16[8,64,512]{2,1,0:T(8,128)(2,1)S(1)}, f32[16,512]{1,0:T(8,128)S(1)}, f32[...) custom-call(s32[6]{0:T(128)} %refs_0_.1, s32[2,4]{1,0:T(2,128)} %bitcast.32, ...), custom_call_target="tpu_custom_call" | custom-call | tf_op jit(solution)/shard_map/block/pallas_call | solution.py:1594
  105.4 2.9 %adam.1 = (f32[8,64,512]{2,1,0:T(8,128)}, f32[8,64,512]{2,1,0:T(8,128)}, f32[8,64,512]{2,1,0:T(8,128)}, bf16[8,64,512]{2,1,0:T(8,128)(2,1)}, f32[288,512]{1,0:T(...) custom-call(bf16[8,64,512]{2,1,0:T(8,128)(2,1)S(1)} %get-tuple-eleme, ...), custom_call_target="tpu_custom_call" | custom-call | tf_op jit(solution)/shard_map/adam/pallas_call | solution.py:1620

commit v8 on v7

--- a/solution.py
+++ b/solution.py
@@ -464,7 +464,7 @@
 
 
 SLACK = 2.0
-SENDS, RECEIVES = 32, 180
+SENDS, RECEIVES = 24, 180
 GATHERS = (
     (0, 0, 1, 0.0),
     (0, 1, 1, 0.07),
@@ -480,6 +480,7 @@
 QUARTERS = {5: 0, 1: 3, 0: 6}
 AFTER = {}
 WHOLE = ()
+FIRST = ("w", 0, 0)
 SCATTERS = (
     (5, 0, 3, 0.93),
     (3, 0, 2, 1.01),
@@ -529,7 +530,7 @@
     held = refs[22:32]
     owners, docs, slopes, gain, bias, norm_m, norm_v, slope_row, slope_m, slope_v = held
     (
-        w, red, mine, other, core_in, both, x_in, tok, cot, tail_in, wide_tok, wide_cot, x_pool, x_norm, x_att,
+        w, red, cross_in, mine, other, core_in, both, x_in, tok, cot, tail_in, wide_tok, wide_cot, x_pool, x_norm, x_att,
         x_two, x_act, x_short, d_up, d_low, d_inner, d_res, d_qkv, d_pool, pooled, hat_one, hat_two, root_one, root_two,
         resid, hidden, short_grad, res_grad, q_out, q_in, a_out, a_in, da_out, da_in, dq_out, dq_in, probs, mixed, grad,
         wide_up, wide_grad, edge_in, x_near, x_wide, t_left, t_out, t_in, u_out, u_in, dx_out, dx_in, g, right_in, left_in, fin_out, fin_in, co_out, co_in, sums, sums_in, sends, recvs, local,
@@ -635,6 +636,9 @@
                 slot = jnp.minimum(begin + (block - lo), masters.shape[0] - 1)
                 mine[block] = (masters[slot, :, my_half] * mask).astype(LOW)
                 other[block] = (masters[slot, :, other_half] * mask).astype(LOW)
+                if block == 0:
+                    send(("g1", FIRST), mine.at[0], x_in.at[0], x_peer, ("g1", FIRST))
+                    send(("g2", FIRST), other.at[0], cross_in, cross_peer, ("g1", FIRST))
             send(("g0", k), other.at[lo:hi], core_in.at[lo:hi], core_peer)
 
         return run
@@ -679,8 +683,12 @@
             send(("g1", name), both.at[away, :, away_span], x_in.at[away, :, away_span], x_peer)
 
         def join_x():
-            flying[("g1", name)].wait_recv()
-            w[blocks, c, rows_at(0), span] = both[blocks, :, span] + x_in[blocks, :, span]
+            if name == FIRST:
+                gather_up(("g1", FIRST), w.at[0:2, c, 0:rows_of])
+                w[0, c, rows_at(0)] = both[0] + (x_in[0] + cross_in[...])
+            else:
+                flying[("g1", name)].wait_recv()
+                w[blocks, c, rows_at(0), span] = both[blocks, :, span] + x_in[blocks, :, span]
             send(("R", 1, name), piece(0), piece(0), right_peer, (1, name))
             send(("L", 1, name), piece(0), piece(0), left_peer, (1, name))
 
@@ -714,9 +722,12 @@
 
             return run
 
-        plan.add(("cx", name), join_here, [("cs", k) for k in parents], (), [(("g1", name), "x", load)], 0.05, rank)
+        before = ("cs", 0)
+        if name != FIRST:
+            before = ("cx", name)
+            plan.add(before, join_here, [("cs", k) for k in parents], (), [(("g1", name), "x", load)], 0.05, rank)
         plan.add(
-            ("x", name), join_x, [("cx", name)], [("g1", name)],
+            ("x", name), join_x, [before], [("g1", name)] + ([("g2", name)] if name == FIRST else []),
             [(("R", 1, name), "r", load), (("L", 1, name), "l", load)], 0.05, rank,
         )
         crossing = []
@@ -756,7 +767,8 @@
     for k in (0, 1, 3, 4, 2, 5):
         lo, hi = spans[k]
         load = (hi - lo) * piece_bytes
-        plan.add(("co", k), contribute(k), ["ms"], (), [(("g0", k), "c", load)], 0.04 * (hi - lo), 0.1)
+        early = [((which, FIRST), "x", piece_bytes) for which in ("g1", "g2")] if k == 0 else []
+        plan.add(("co", k), contribute(k), ["ms"], (), early + [(("g0", k), "c", load)], 0.04 * (hi - lo), 0.1)
         plan.add(("cs", k), join_cores(k), [("co", k)], [("g0", k)], (), 0.02 * (hi - lo), 0.1)
     for chunk in gathers:
         gather_chunk(*chunk)
@@ -1570,7 +1582,7 @@
         pltpu.SMEM(owners.shape, jnp.int32), pltpu.SMEM((micros, doc_lengths.shape[2]), jnp.int32),
         pltpu.SMEM(slopes.shape, WIDE), wide(2, features), wide(2, features), wide(4, features), wide(4, features),
         wide(1, heads), wide(1, heads), wide(1, heads),
-        low(blocks, 2, features, half), low(blocks, rows, features), pieces(), pieces(), pieces(), pieces(), pieces(),
+        low(blocks, 2, features, half), low(blocks, rows, features), low(rows, half), pieces(), pieces(), pieces(), pieces(), pieces(),
         low(micros, tok_rows, features), low(micros, tok_rows, features), low(micros, 16, features),
         wide(micros, split, 16 + tok_rows, TILE), wide(micros, split, tok_rows, TILE),
         both(3 * features), both(features), both(features), both(features), both(FF), both(features),

time: 109 us -> 109 us (level)
  no operation moved by 1% of the time
where the time goes in v8:
time: 109 us; the launch traced here: 108 us
  Pallas kernels  107 us (98%)
    pallas_call x1, Pallas kernels, fused_body(): pl.pallas_call(lambda *refs: main_kernel(dims, refs), out_shape=(jax.Shap...  105 us
    pallas_call x1, Pallas kernels, fused_body(): pl.pallas_call(lambda *refs: adam_kernel(refs), grid=(steps,), out_shape=...  2.87 us

profile of v8, /device:TPU:0, one launch (start us, length us, event | category | flops | bytes accessed | tf_op | source)
XLA Modules:
  0.0 108.3 jit_solution(16624032582769920270)
XLA Ops:
  0.6 104.6 %block.1 = (f32[2,144,512]{2,1,0:T(8,128)S(1)}, f32[2,144,512]{2,1,0:T(8,128)S(1)}, bf16[8,64,512]{2,1,0:T(8,128)(2,1)S(1)}, f32[16,512]{1,0:T(8,128)S(1)}, f32[...) custom-call(s32[6]{0:T(128)} %refs_0_.1, s32[2,4]{1,0:T(2,128)} %bitcast.32, ...), custom_call_target="tpu_custom_call" | custom-call | tf_op jit(solution)/shard_map/block/pallas_call | solution.py:1606
  105.3 2.9 %adam.1 = (f32[8,64,512]{2,1,0:T(8,128)}, f32[8,64,512]{2,1,0:T(8,128)}, f32[8,64,512]{2,1,0:T(8,128)}, bf16[8,64,512]{2,1,0:T(8,128)(2,1)}, f32[288,512]{1,0:T(...) custom-call(bf16[8,64,512]{2,1,0:T(8,128)(2,1)S(1)} %get-tuple-eleme, ...), custom_call_target="tpu_custom_call" | custom-call | tf_op jit(solution)/shard_map/adam/pallas_call | solution.py:1632

commit v9 on v8

--- a/solution.py
+++ b/solution.py
@@ -464,7 +464,7 @@
 
 
 SLACK = 2.0
-SENDS, RECEIVES = 24, 180
+SENDS, RECEIVES = 24, 175
 GATHERS = (
     (0, 0, 1, 0.0),
     (0, 1, 1, 0.07),
@@ -1472,7 +1472,7 @@
             fin_out[blocks, :, span] = total.astype(LOW)
             send(("rx", name), fin_out.at[blocks, :, span], fin_in.at[blocks, :, span], x_peer)
             if quarters:
-                send(("rd", name), fin_out.at[blocks, :, span], co_in.at[blocks, :, span], cross_peer)
+                send(("rd", name), fin_out.at[blocks, :, span], co_in.at[blocks, :, span], cross_peer, ("rc", name))
             if split:
                 send(("rc", name), fin_out.at[blocks, :, span], co_in.at[blocks, :, span], core_peer)
                 red[blocks, :, out_span] = fin_out[blocks, :, span]
@@ -1490,7 +1490,10 @@
                 send(("rc", name), co_out.at[blocks], co_in.at[blocks], core_peer)
 
         def finish_core():
-            arrive(("rc", name), *([("rd", name)] if split else []))()
+            if quarters:
+                gather_up(("rc", name), co_in.at[blocks])
+            else:
+                arrive(("rc", name), *([("rd", name)] if split else []))()
             red[blocks, :, other_half] = co_in[blocks]
             if split and not quarters:
                 red[away, :, other_half] = co_in[away]

time: 109 us -> 108 us (level)
  no operation moved by 1% of the time
where the time goes in v9:
time: 108 us
  Pallas kernels  107 us (99%)
    pallas_call x1, Pallas kernels, fused_body(): pl.pallas_call(lambda *refs: main_kernel(dims, refs), out_shape=(jax.Shap...  105 us
    pallas_call x1, Pallas kernels, fused_body(): pl.pallas_call(lambda *refs: adam_kernel(refs), grid=(steps,), out_shape=...  2.87 us

profile of v9, /device:TPU:0, one launch (start us, length us, event | category | flops | bytes accessed | tf_op | source)
XLA Modules:
  0.0 108.3 jit_solution(1945934612530358157)
XLA Ops:
  0.6 104.6 %block.1 = (f32[2,144,512]{2,1,0:T(8,128)S(1)}, f32[2,144,512]{2,1,0:T(8,128)S(1)}, bf16[8,64,512]{2,1,0:T(8,128)(2,1)S(1)}, f32[16,512]{1,0:T(8,128)S(1)}, f32[...) custom-call(s32[6]{0:T(128)} %refs_0_.1, s32[2,4]{1,0:T(2,128)} %bitcast.32, ...), custom_call_target="tpu_custom_call" | custom-call | tf_op jit(solution)/shard_map/block/pallas_call | solution.py:1609
  105.2 2.9 %adam.1 = (f32[8,64,512]{2,1,0:T(8,128)}, f32[8,64,512]{2,1,0:T(8,128)}, f32[8,64,512]{2,1,0:T(8,128)}, bf16[8,64,512]{2,1,0:T(8,128)(2,1)}, f32[288,512]{1,0:T(...) custom-call(bf16[8,64,512]{2,1,0:T(8,128)(2,1)S(1)} %get-tuple-eleme, ...), custom_call_target="tpu_custom_call" | custom-call | tf_op jit(solution)/shard_map/adam/pallas_call | solution.py:1635
